TPU v7x, 128 devices: a whole 4x4x4 slice. The times are simulated.
128 devices in a mesh: gx: 16 (over z, y), gy: 8 (over x, core).
Axes of the slice: x: 4, y: 4, z: 4, core: 2. Of those that a mesh axis runs over, the one named last changes fastest.
Arguments:
- ensemble: bfloat16 [2, 3, 128, 512, 1024], P(None, None, None, 'gx', 'gy'), may hold values from -6 to 6
- layer_depth: float32 [2, 512, 1024], P(None, 'gx', 'gy'), may hold values from 0.5 to 2
- obs_dest: int32 [16, 8, 32], P('gx', 'gy'), may hold values from 0 to 7, as said below
- obs_cell: int32 [16, 8, 32, 128], P('gx', 'gy'), may hold values from 0 to 4095
- obs_value: float32 [16, 8, 32, 128], P('gx', 'gy'), may hold values from -10 to 10
- obs_sigma: float32 [16, 8, 32, 128], P('gx', 'gy'), may hold values from 2 to 20
Outputs:
- analysis: bfloat16 [2, 3, 128, 512, 1024], P(None, None, None, 'gx', 'gy')
Inputs may be any that keep to these rules, and one draw needn't show every extreme that they name: `obs_dest`: at most 10 blocks of one tile name one tile column, and in every row of tiles one column is named by exactly 10 blocks of every tile of that row. `obs_cell`: cells are numbered row by row, 128 to a row.
All inputs are finite; a program needn't handle non-finite values.
Results may differ from a plain program's by a relative error of at most 0.025.
Values may be sent and summed in bfloat16 or wider, within the bound.
No kernel may reach another device: no remote copies, remote signals or barrier semaphores. Data moves between devices by JAX's collectives and lax.ppermute only.
A program may use at most 128 MiB of HBM per device.

v0:
```python
import jax
import jax.numpy as jnp
from jax import lax
from jax.sharding import PartitionSpec as P

STEPS = 4
CAP = 10


cfl_number = 0.3
coriolis = 0.4
coupling = 0.5


def padded(x, sides, width):
    for axis, dim in sides:
        devices, length = (lax.axis_size(axis), x.shape[dim])
        up = [(i, (i + 1) % devices) for i in range(devices - 1)]
        down = [(j, i) for i, j in up]
        last = lax.slice_in_dim(x, length - width, length, axis=dim)
        initial = lax.slice_in_dim(x, 0, width, axis=dim)
        before = lax.ppermute(last, axis, up)
        after = lax.ppermute(initial, axis, down)
        x = jnp.concatenate([before, x, after], axis=dim)
    return x


def advance(state, depth_local):
    half_step = 0.5 * cfl_number
    depth_cells = depth_local[:, None]
    vel_x = state[:, 0].astype(jnp.float32)
    vel_y = state[:, 1].astype(jnp.float32)
    thick = state[:, 2].astype(jnp.float32)
    flux_x = (depth_cells * vel_x).astype(jnp.bfloat16)
    flux_y = (depth_cells * vel_y).astype(jnp.bfloat16)
    wide_x = padded(flux_x, (("gx", 2),), 1).astype(jnp.float32)
    wide_y = padded(flux_y, (("gy", 3),), 1).astype(jnp.float32)
    spread_div = wide_x[:, :, 2:] - wide_x[:, :, :-2] + (wide_y[:, :, :, 2:] - wide_y[:, :, :, :-2])
    thick_new = (thick - half_step * spread_div).astype(jnp.bfloat16)
    thick_f = thick_new.astype(jnp.float32)
    pressure = jnp.stack([thick_f[0] + thick_f[1], coupling * thick_f[0] + thick_f[1]]).astype(
        jnp.bfloat16
    )
    wide_p = padded(pressure, (("gx", 2), ("gy", 3)), 1).astype(jnp.float32)
    grad_x = wide_p[:, :, 2:, 1:-1] - wide_p[:, :, :-2, 1:-1]
    grad_y = wide_p[:, :, 1:-1, 2:] - wide_p[:, :, 1:-1, :-2]
    turn = cfl_number * coriolis
    vel_x_new = (vel_x + turn * vel_y - half_step * grad_x).astype(jnp.bfloat16)
    vel_y_new = (vel_y - turn * vel_x - half_step * grad_y).astype(jnp.bfloat16)
    return jnp.stack([vel_x_new, vel_y_new, thick_new], 1)


def make_transform(gram, proj, members):
    eye = jnp.eye(members, dtype=jnp.float32)
    lower = jnp.linalg.cholesky(gram)
    inverse = lax.linalg.triangular_solve(lower, eye, left_side=True, lower=True)
    inner = jnp.dot(
        inverse, proj, precision=lax.Precision.HIGHEST, preferred_element_type=jnp.float32
    )
    weights = jnp.dot(
        inverse.T, inner, precision=lax.Precision.HIGHEST, preferred_element_type=jnp.float32
    )
    scale = jnp.sqrt(jnp.float32(members - 1))
    return (weights[:, None] + scale * inverse.T).astype(jnp.bfloat16)


def on_device(ensemble, layer_depth, obs_dest, obs_cell, obs_value, obs_sigma):
    members = ensemble.shape[2]
    rows_tile = ensemble.shape[3]
    cols_tile = ensemble.shape[4]
    block_obs = obs_cell.shape[3]
    tiles_y = lax.axis_size("gy")
    capacity = CAP
    dest = obs_dest[0, 0]
    onehot = (dest[:, None] == jnp.arange(tiles_y, dtype=jnp.int32)[None, :]).astype(jnp.int32)
    ranks = jnp.sum(onehot * jnp.cumsum(onehot, 0), 1) - 1
    bucket = dest * capacity + ranks
    place = (bucket[None, :] == jnp.arange(tiles_y * capacity, dtype=jnp.int32)[:, None]).astype(
        jnp.float32
    )

    def placed(values):
        spread_rows = jnp.dot(
            place, values, precision=lax.Precision.HIGHEST, preferred_element_type=jnp.float32
        )
        return spread_rows.reshape(tiles_y, capacity, block_obs)

    cell_buf = placed(obs_cell[0, 0].astype(jnp.float32))
    value_buf = placed(obs_value[0, 0])
    weight_buf = placed(1.0 / obs_sigma[0, 0])
    state = ensemble
    for _ in range(STEPS):
        state = advance(state, layer_depth)
    surface_elevation = state[0, 2].astype(jnp.float32) + state[1, 2].astype(jnp.float32)
    height_flat = surface_elevation.reshape(members, rows_tile * cols_tile)
    picked = jnp.transpose(
        height_flat[
            :,
            lax.all_to_all(
                cell_buf.astype(jnp.int32), "gy", split_axis=0, concat_axis=0, tiled=True
            ),
        ],
        (1, 2, 0, 3),
    )
    returned = lax.all_to_all(picked, "gy", split_axis=0, concat_axis=0, tiled=True)
    seen = jnp.transpose(returned, (2, 0, 1, 3))
    mean_seen = jnp.mean(seen, 0)
    spread = (seen - mean_seen) * weight_buf
    innovation = (value_buf - mean_seen) * weight_buf
    gram_local = jnp.einsum("myco,nyco->mn", spread, spread, precision=lax.Precision.HIGHEST)
    proj_local = jnp.einsum("myco,yco->m", spread, innovation, precision=lax.Precision.HIGHEST)
    eye = jnp.eye(members, dtype=jnp.float32)
    gram_all, proj_all = lax.psum((gram_local, proj_local), ("gx", "gy"))
    transform = make_transform(gram_all + (members - 1) * eye, proj_all, members)
    center = jnp.mean(state.astype(jnp.float32), axis=2, keepdims=True)
    anomaly = (state.astype(jnp.float32) - center).astype(jnp.bfloat16)
    mixed = jnp.einsum("nm,lcnxy->lcmxy", transform, anomaly, preferred_element_type=jnp.float32)
    return (center + mixed).astype(jnp.bfloat16)


def solution(mesh):
    in_specs = (
        P(None, None, None, "gx", "gy"),
        P(None, "gx", "gy"),
        P("gx", "gy", None),
        P("gx", "gy", None, None),
        P("gx", "gy", None, None),
        P("gx", "gy", None, None),
    )
    out_specs = P(None, None, None, "gx", "gy")
    return jax.shard_map(
        on_device, mesh=mesh, in_specs=in_specs, out_specs=out_specs, check_vma=False
    )
```

profile of v0, /device:TPU:1, one launch (start us, length us, event | category | flops | bytes accessed | tf_op | source)
XLA Modules:
  0.0 530.5 jit_solution(4588675104599431242)
XLA Ops:
  6.5 6.1 %fusion.112 = (bf16[2,1,128,32,128]{4,3,2,1,0:T(8,128)(2,1)}, bf16[2,1,128,32,128]{4,3,2,1,0:T(8,128)(2,1)}, bf16[2,1,128,32,128]{4,3,2,1,0:T(8,128)(2,1)}) fusion(bf16[2,3,128,32,128]{4,3,2,1,0:T(8,128)(2,1)} %param.6), kind=kLoop, calls=%fused_computation.210 | loop fusion | bytes 12582912 | tf_op jit(solution)/shard_map/slice | solution.py:33
  17.0 5.2 copy.103
  38.4 5.2 copy.104
  59.7 5.2 collective-permute-start.6
  72.1 5.0 fusion.11
  88.0 5.4 %collective-permute-done.9 = bf16[2,128,1,128]{1,2,3,0:T(2,128)(2,1)S(1)} collective-permute-done((bf16[2,128,1,128]{1,2,3,0:T(2,128)(2,1)S(1)}, bf16[2,128,1,128]{1,2,3,0:T(2,128)(2,1)S(1)}, u32[]{:S(2)}, u32[]{:S(2)}) %collective-permute-start.9) | collective-permute-done | bytes 65568 | tf_op jit(solution)/shard_map/ppermute | solution.py:23
  98.7 5.5 %collective-permute-start.12 = (bf16[2,128,1,128]{1,2,3,0:T(2,128)(2,1)S(1)}, bf16[2,128,1,128]{1,2,3,0:T(2,128)(2,1)S(1)}, u32[]{:S(2)}, u32[]{:S(2)}) collective-permute-start(bf16[2,128,1,128]{1,2,3,0:T(2,128)(2,1)S(1)} %get-tuple-element.58), channel_id=1, source_target_pairs={{0,8},{8,16},{16,24},{24,32},{32,40},{40,48},{48,56},{56,64},{64,7... | collective-permute-start | bytes 196616 | tf_op jit(solution)/shard_map/ppermute | solution.py:22
  117.9 4.6 all-to-all-start
  124.8 4.9 fusion.17
  162.0 4.8 collective-permute-start.22
  174.0 4.9 fusion.23
  201.0 34.5 %gather_fusion = f32[10240,128]{1,0:T(8,128)} fusion(f32[128,4096]{0,1:T(8,128)S(1)} %bitcast.96, s32[10240]{0:T(1024)S(1)} %broadcast_clamp_fusion), kind=kCustom, calls=%fused_computation | custom fusion | bytes 10526720 | tf_op jit(solution)/shard_map/gather | solution.py:97
  235.5 5.9 %copy.86 = f32[8,10,128,128]{2,3,1,0:T(8,128)} copy(f32[8,10,128,128]{3,2,1,0:T(8,128)} %bitcast.97) | data formatting | bytes 10485760 | tf_op jit(solution)/shard_map/gather | solution.py:97
  241.5 5.1 all-to-all-start.1
  264.8 38.8 %collective-permute-done.30 = bf16[2,128,34,1]{1,0,3,2:T(2,128)(2,1)S(1)} collective-permute-done((bf16[2,128,34,1]{1,0,3,2:T(2,128)(2,1)S(1)}, bf16[2,128,34,1]{1,0,3,2:T(2,128)(2,1)S(1)}, u32[]{:S(2)}, u32[]{:S(2)}) %collective-permute-start.30) | collective-permute-done | bytes 17440 | tf_op jit(solution)/shard_map/ppermute | solution.py:22
  318.1 8.5 %fusion = bf16[2,3,128,32,128]{2,3,4,0,1:T(8,128)(2,1)} fusion(f32[2,3,32,128]{2,3,0,1:T(8,128)S(1)} %copy.84, bf16[2,1,128,32,128]{2,3,4,0,1:T(8,128)(2,1)S(1)} %bitcast.99, bf16[2,1,128,32,128]{2,3,4,0,1:T(8,128)(2,1)} %copy-done.9, bf16[2,1,128,32,128]{2,3,4,0,1:T(8,128)(2,1)} %copy-done.8), kind=kLoop, calls=%fused_computation.3 | loop fusion | flops 15728640 | bytes 12681216 | tf_op jit(solution)/shard_map/convert_element_type | solution.py:116
  330.0 9.7 %fusion.64 = f32[128,128]{1,0:T(8,128)} fusion(f32[8,10,128,128]{3,2,1,0:T(8,128)} %all-to-all-done.1, f32[8,10,128]{2,1,0:T(8,128)S(1)} %fusion.73, f32[8,10,128]{2,1,0:T(8,128)S(1)} %broadcast_multiply_fusion.1), kind=kOutput, calls=%fused_computation.130 | convolution fusion | flops 2015887360 | bytes 5390336 | tf_op jit(solution)/shard_map/myco,nyco->mn/dot_general | solution.py:110
  339.7 6.1 %fusion.69 = f32[128]{0:T(128)S(1)} fusion(f32[8,10,128,1]{2,1,0,3:T(8,128)S(1)} %fusion.68, f32[8,10,128,128]{3,2,1,0:T(8,128)} %all-to-all-done.1, f32[8,10,128]{2,1,0:T(8,128)S(1)} %fusion.73, f32[8,10,128]{2,1,0:T(8,128)S(1)} %broadcast_multiply_fusion.1), kind=kOutput, calls=%fused_computation.135 | convolution fusion | flops 18350080 | bytes 5366272 | tf_op jit(solution)/shard_map/myco,yco->m/dot_general | solution.py:111
  345.8 67.6 %psum.15 = f32[128]{0:T(128)S(1)} all-reduce(f32[128]{0:T(128)S(1)} %fusion.69), channel_id=1, replica_groups=mesh['gx'=16,'gy'=8] {'gx','gy'}, use_global_device_ids=true, to_apply=%region_7.8 | all-reduce | flops 128 | bytes 1024 | tf_op jit(solution)/shard_map/psum | solution.py:113
  413.4 66.6 %all-reduce.2.cloned.1.call-done = f32[128,128]{1,0:T(8,128)} async-done(((f32[128,128]{1,0:T(8,128)}), f32[128,128]{1,0:T(8,128)}) %all-reduce.2.cloned.1.call-update) | async-done | bytes 65552 | tf_op jit(solution)/shard_map/psum | solution.py:113
  481.8 11.7 %cholesky.17 = f32[128,128]{1,0:T(8,128)S(1)} custom-call(f32[128,128]{1,0:T(8,128)S(1)} %fusion.82), custom_call_target="Cholesky" | custom-call | tf_op jit(solution)/shard_map/jit(cholesky)/cholesky | solution.py:55
  494.8 9.8 %custom-call.6 = f32[1,128,128]{1,2,0:T(8,128)S(1)} custom-call(f32[1,128,128]{2,1,0:T(8,128)S(1)} %fusion.76), custom_call_target="InvertDiagBlocksLowerTriangular" | custom-call | tf_op jit(solution)/shard_map/triangular_solve | solution.py:56
  505.2 9.3 %fusion.1 = bf16[2,3,128,32,128]{2,4,3,1,0:T(8,128)(2,1)} fusion(bf16[2,3,128,32,128]{2,3,4,0,1:T(8,128)(2,1)} %fusion, f32[128,128]{1,0:T(8,128)S(1)} %fusion.80, f32[128]{0:T(128)S(1)} %convolution_bitcast_fusion, f32[2,3,32,128]{3,2,0,1:T(8,128)S(1)} %copy.100), kind=kOutput, calls=%fused_computation.5 | convolution fusion | flops 811671552 | bytes 12747264 | tf_op jit(solution)/shard_map/nm,lcnxy->lcmxy/dot_general | solution.py:117
  514.5 9.0 %copy.94 = bf16[2,3,128,32,128]{4,3,2,1,0:T(8,128)(2,1)} copy(bf16[2,3,128,32,128]{2,4,3,1,0:T(8,128)(2,1)} %fusion.1) | data formatting | bytes 12582912 | tf_op jit(solution)/shard_map/convert_element_type | solution.py:118
  (196 shorter events, 176.4 us)
Async XLA Ops:
  27.0 18.7 %collective-permute-start = (bf16[2,128,1,128]{1,2,3,0:T(2,128)(2,1)S(1)}, bf16[2,128,1,128]{1,2,3,0:T(2,128)(2,1)S(1)}, u32[]{:S(2)}, u32[]{:S(2)}) collective-permute-start(bf16[2,128,1,128]{1,2,3,0:T(2,128)(2,1)S(1)} %get-tuple-element.66), channel_id=1, source_target_pairs={{0,8},{8,16},{16,24},{24,32},{32,40},{40,48},{48,56},{56,64},{64,7... | collective-permute-start | bytes 196616 | tf_op jit(solution)/shard_map/ppermute | solution.py:22
  31.1 14.6 %collective-permute-start.1 = (bf16[2,128,1,128]{1,2,3,0:T(2,128)(2,1)S(1)}, bf16[2,128,1,128]{1,2,3,0:T(2,128)(2,1)S(1)}, u32[]{:S(2)}, u32[]{:S(2)}) collective-permute-start(bf16[2,128,1,128]{1,2,3,0:T(2,128)(2,1)S(1)} %get-tuple-element.67), channel_id=1, source_target_pairs={{8,0},{16,8},{24,16},{32,24},{40,32},{48,40},{56,48},{64,56},{72,6... | collective-permute-start | bytes 196616 | tf_op jit(solution)/shard_map/ppermute | solution.py:23
  32.4 11.2 %collective-permute-start.2 = (bf16[2,128,32,1]{1,2,3,0:T(8,128)(2,1)S(1)}, bf16[2,128,32,1]{1,2,3,0:T(8,128)(2,1)S(1)}, u32[]{:S(2)}, u32[]{:S(2)}) collective-permute-start(bf16[2,128,32,1]{1,2,3,0:T(8,128)(2,1)S(1)} %get-tuple-element.68), channel_id=1, source_target_pairs={{0,1},{1,2},{2,3},{3,4},{4,5},{5,6},{6,7},{8,9},{9,10},{10,11},{11... | collective-permute-start | bytes 49160 | tf_op jit(solution)/shard_map/ppermute | solution.py:22
  36.4 7.2 %collective-permute-start.3 = (bf16[2,128,32,1]{1,2,3,0:T(8,128)(2,1)S(1)}, bf16[2,128,32,1]{1,2,3,0:T(8,128)(2,1)S(1)}, u32[]{:S(2)}, u32[]{:S(2)}) collective-permute-start(bf16[2,128,32,1]{1,2,3,0:T(8,128)(2,1)S(1)} %get-tuple-element.69), channel_id=1, source_target_pairs={{1,0},{2,1},{3,2},{4,3},{5,4},{6,5},{7,6},{9,8},{10,9},{11,10},{12... | collective-permute-start | bytes 49160 | tf_op jit(solution)/shard_map/ppermute | solution.py:23
  59.7 7.2 %collective-permute-start.6 = (bf16[2,128,34,1]{1,0,3,2:T(2,128)(2,1)S(1)}, bf16[2,128,34,1]{1,0,3,2:T(2,128)(2,1)S(1)}, u32[]{:S(2)}, u32[]{:S(2)}) collective-permute-start(bf16[2,128,34,1]{1,0,3,2:T(2,128)(2,1)S(1)} %copy.66), channel_id=1, source_target_pairs={{0,1},{1,2},{2,3},{3,4},{4,5},{5,6},{6,7},{8,9},{9,10},{10,11},{11... | collective-permute-start | bytes 52232 | tf_op jit(solution)/shard_map/ppermute | solution.py:22
  77.0 9.2 %collective-permute-start.10 = (bf16[2,128,32,1]{1,2,3,0:T(8,128)(2,1)S(1)}, bf16[2,128,32,1]{1,2,3,0:T(8,128)(2,1)S(1)}, u32[]{:S(2)}, u32[]{:S(2)}) collective-permute-start(bf16[2,128,32,1]{1,2,3,0:T(8,128)(2,1)S(1)} %get-tuple-element.62), channel_id=1, source_target_pairs={{0,1},{1,2},{2,3},{3,4},{4,5},{5,6},{6,7},{8,9},{9,10},{10,11},{11... | collective-permute-start | bytes 49160 | tf_op jit(solution)/shard_map/ppermute | solution.py:22
  79.0 7.3 %collective-permute-start.11 = (bf16[2,128,32,1]{1,2,3,0:T(8,128)(2,1)S(1)}, bf16[2,128,32,1]{1,2,3,0:T(8,128)(2,1)S(1)}, u32[]{:S(2)}, u32[]{:S(2)}) collective-permute-start(bf16[2,128,32,1]{1,2,3,0:T(8,128)(2,1)S(1)} %get-tuple-element.63), channel_id=1, source_target_pairs={{1,0},{2,1},{3,2},{4,3},{5,4},{6,5},{7,6},{9,8},{10,9},{11,10},{12... | collective-permute-start | bytes 49160 | tf_op jit(solution)/shard_map/ppermute | solution.py:23
  84.8 8.6 %collective-permute-start.9 = (bf16[2,128,1,128]{1,2,3,0:T(2,128)(2,1)S(1)}, bf16[2,128,1,128]{1,2,3,0:T(2,128)(2,1)S(1)}, u32[]{:S(2)}, u32[]{:S(2)}) collective-permute-start(bf16[2,128,1,128]{1,2,3,0:T(2,128)(2,1)S(1)} %get-tuple-element.61), channel_id=1, source_target_pairs={{8,0},{16,8},{24,16},{32,24},{40,32},{48,40},{56,48},{64,56},{72,6... | collective-permute-start | bytes 196616 | tf_op jit(solution)/shard_map/ppermute | solution.py:23
  98.7 7.9 %collective-permute-start.12 = (bf16[2,128,1,128]{1,2,3,0:T(2,128)(2,1)S(1)}, bf16[2,128,1,128]{1,2,3,0:T(2,128)(2,1)S(1)}, u32[]{:S(2)}, u32[]{:S(2)}) collective-permute-start(bf16[2,128,1,128]{1,2,3,0:T(2,128)(2,1)S(1)} %get-tuple-element.58), channel_id=1, source_target_pairs={{0,8},{8,16},{16,24},{24,32},{32,40},{40,48},{48,56},{56,64},{64,7... | collective-permute-start | bytes 196616 | tf_op jit(solution)/shard_map/ppermute | solution.py:22
  110.9 11.7 %collective-permute-start.14 = (bf16[2,128,34,1]{1,0,3,2:T(2,128)(2,1)S(1)}, bf16[2,128,34,1]{1,0,3,2:T(2,128)(2,1)S(1)}, u32[]{:S(2)}, u32[]{:S(2)}) collective-permute-start(bf16[2,128,34,1]{1,0,3,2:T(2,128)(2,1)S(1)} %copy.70), channel_id=1, source_target_pairs={{0,1},{1,2},{2,3},{3,4},{4,5},{5,6},{6,7},{8,9},{9,10},{10,11},{11... | collective-permute-start | bytes 52232 | tf_op jit(solution)/shard_map/ppermute | solution.py:22
  115.1 7.5 %collective-permute-start.15 = (bf16[2,128,34,1]{1,0,3,2:T(2,128)(2,1)S(1)}, bf16[2,128,34,1]{1,0,3,2:T(2,128)(2,1)S(1)}, u32[]{:S(2)}, u32[]{:S(2)}) collective-permute-start(bf16[2,128,34,1]{1,0,3,2:T(2,128)(2,1)S(1)} %copy.71), channel_id=1, source_target_pairs={{1,0},{2,1},{3,2},{4,3},{5,4},{6,5},{7,6},{9,8},{10,9},{11,10},{12... | collective-permute-start | bytes 52232 | tf_op jit(solution)/shard_map/ppermute | solution.py:23
  117.9 37.8 %all-to-all-start = ((s32[8,10,128]{2,1,0:T(8,128)}), s32[8,10,128]{2,1,0:T(8,128)S(1)}, u32[]{:S(2)}, u32[]{:S(2)}) async-start(s32[8,10,128]{2,1,0:T(8,128)} %convolution_convert_fusion), calls=%async_computation | async-start | bytes 131072 | tf_op jit(solution)/shard_map/all_to_all | solution.py:99
  129.7 10.7 %collective-permute-start.18 = (bf16[2,128,32,1]{1,2,3,0:T(8,128)(2,1)S(1)}, bf16[2,128,32,1]{1,2,3,0:T(8,128)(2,1)S(1)}, u32[]{:S(2)}, u32[]{:S(2)}) collective-permute-start(bf16[2,128,32,1]{1,2,3,0:T(8,128)(2,1)S(1)} %get-tuple-element.56), channel_id=1, source_target_pairs={{0,1},{1,2},{2,3},{3,4},{4,5},{5,6},{6,7},{8,9},{9,10},{10,11},{11... | collective-permute-start | bytes 49160 | tf_op jit(solution)/shard_map/ppermute | solution.py:22
  133.3 7.2 %collective-permute-start.19 = (bf16[2,128,32,1]{1,2,3,0:T(8,128)(2,1)S(1)}, bf16[2,128,32,1]{1,2,3,0:T(8,128)(2,1)S(1)}, u32[]{:S(2)}, u32[]{:S(2)}) collective-permute-start(bf16[2,128,32,1]{1,2,3,0:T(8,128)(2,1)S(1)} %get-tuple-element.57), channel_id=1, source_target_pairs={{1,0},{2,1},{3,2},{4,3},{5,4},{6,5},{7,6},{9,8},{10,9},{11,10},{12... | collective-permute-start | bytes 49160 | tf_op jit(solution)/shard_map/ppermute | solution.py:23
  154.4 7.6 %collective-permute-start.21 = (bf16[2,128,1,128]{1,2,3,0:T(2,128)(2,1)S(1)}, bf16[2,128,1,128]{1,2,3,0:T(2,128)(2,1)S(1)}, u32[]{:S(2)}, u32[]{:S(2)}) collective-permute-start(bf16[2,128,1,128]{1,2,3,0:T(2,128)(2,1)S(1)} %get-tuple-element.53), channel_id=1, source_target_pairs={{8,0},{16,8},{24,16},{32,24},{40,32},{48,40},{56,48},{64,56},{72,6... | collective-permute-start | bytes 196616 | tf_op jit(solution)/shard_map/ppermute | solution.py:23
  162.0 7.0 %collective-permute-start.22 = (bf16[2,128,34,1]{1,0,3,2:T(2,128)(2,1)S(1)}, bf16[2,128,34,1]{1,0,3,2:T(2,128)(2,1)S(1)}, u32[]{:S(2)}, u32[]{:S(2)}) collective-permute-start(bf16[2,128,34,1]{1,0,3,2:T(2,128)(2,1)S(1)} %copy.74), channel_id=1, source_target_pairs={{0,1},{1,2},{2,3},{3,4},{4,5},{5,6},{6,7},{8,9},{9,10},{10,11},{11... | collective-permute-start | bytes 52232 | tf_op jit(solution)/shard_map/ppermute | solution.py:22
  178.9 9.6 %collective-permute-start.26 = (bf16[2,128,32,1]{1,2,3,0:T(8,128)(2,1)S(1)}, bf16[2,128,32,1]{1,2,3,0:T(8,128)(2,1)S(1)}, u32[]{:S(2)}, u32[]{:S(2)}) collective-permute-start(bf16[2,128,32,1]{1,2,3,0:T(8,128)(2,1)S(1)} %get-tuple-element.50), channel_id=1, source_target_pairs={{0,1},{1,2},{2,3},{3,4},{4,5},{5,6},{6,7},{8,9},{9,10},{10,11},{11... | collective-permute-start | bytes 49160 | tf_op jit(solution)/shard_map/ppermute | solution.py:22
  180.9 7.7 %collective-permute-start.27 = (bf16[2,128,32,1]{1,2,3,0:T(8,128)(2,1)S(1)}, bf16[2,128,32,1]{1,2,3,0:T(8,128)(2,1)S(1)}, u32[]{:S(2)}, u32[]{:S(2)}) collective-permute-start(bf16[2,128,32,1]{1,2,3,0:T(8,128)(2,1)S(1)} %get-tuple-element.51), channel_id=1, source_target_pairs={{1,0},{2,1},{3,2},{4,3},{5,4},{6,5},{7,6},{9,8},{10,9},{11,10},{12... | collective-permute-start | bytes 49160 | tf_op jit(solution)/shard_map/ppermute | solution.py:23
  187.2 7.4 %collective-permute-start.25 = (bf16[2,128,1,128]{1,2,3,0:T(2,128)(2,1)S(1)}, bf16[2,128,1,128]{1,2,3,0:T(2,128)(2,1)S(1)}, u32[]{:S(2)}, u32[]{:S(2)}) collective-permute-start(bf16[2,128,1,128]{1,2,3,0:T(2,128)(2,1)S(1)} %get-tuple-element.49), channel_id=1, source_target_pairs={{8,0},{16,8},{24,16},{32,24},{40,32},{48,40},{56,48},{64,56},{72,6... | collective-permute-start | bytes 196616 | tf_op jit(solution)/shard_map/ppermute | solution.py:23
  241.5 85.1 %all-to-all-start.1 = ((f32[8,10,128,128]{3,2,1,0:T(8,128)}), f32[8,10,128,128]{3,2,1,0:T(8,128)}, u32[]{:S(2)}, u32[]{:S(2)}) async-start(f32[8,10,128,128]{3,2,1,0:T(8,128)} %bitcast.100), calls=%async_computation.1 | async-start | bytes 10485760 | tf_op jit(solution)/shard_map/all_to_all | solution.py:105
  246.6 233.4 %all-reduce.2.cloned.1.call-start = ((), (), s32[]{:S(2)}) async-start(), calls=%async_computation.2 | async-start | bytes 131072 | tf_op jit(solution)/shard_map/psum | solution.py:113
  250.5 7.2 %collective-permute-start.29 = (bf16[2,128,1,128]{1,2,3,0:T(2,128)(2,1)S(1)}, bf16[2,128,1,128]{1,2,3,0:T(2,128)(2,1)S(1)}, u32[]{:S(2)}, u32[]{:S(2)}) collective-permute-start(bf16[2,128,1,128]{1,2,3,0:T(2,128)(2,1)S(1)} %get-tuple-element.47), channel_id=1, source_target_pairs={{8,0},{16,8},{24,16},{32,24},{40,32},{48,40},{56,48},{64,56},{72,6... | collective-permute-start | bytes 196616 | tf_op jit(solution)/shard_map/ppermute | solution.py:23
  257.8 45.8 %collective-permute-start.30 = (bf16[2,128,34,1]{1,0,3,2:T(2,128)(2,1)S(1)}, bf16[2,128,34,1]{1,0,3,2:T(2,128)(2,1)S(1)}, u32[]{:S(2)}, u32[]{:S(2)}) collective-permute-start(bf16[2,128,34,1]{1,0,3,2:T(2,128)(2,1)S(1)} %copy.78), channel_id=1, source_target_pairs={{0,1},{1,2},{2,3},{3,4},{4,5},{5,6},{6,7},{8,9},{9,10},{10,11},{11... | collective-permute-start | bytes 52232 | tf_op jit(solution)/shard_map/ppermute | solution.py:22
  262.2 43.7 %collective-permute-start.31 = (bf16[2,128,34,1]{1,0,3,2:T(2,128)(2,1)S(1)}, bf16[2,128,34,1]{1,0,3,2:T(2,128)(2,1)S(1)}, u32[]{:S(2)}, u32[]{:S(2)}) collective-permute-start(bf16[2,128,34,1]{1,0,3,2:T(2,128)(2,1)S(1)} %copy.79), channel_id=1, source_target_pairs={{1,0},{2,1},{3,2},{4,3},{5,4},{6,5},{7,6},{9,8},{10,9},{11,10},{12... | collective-permute-start | bytes 52232 | tf_op jit(solution)/shard_map/ppermute | solution.py:23
  (36 other events, 640.1 us)
Sparse Core Ops, SparseCore 0:
  339.8 140.1 all-reduce.1
where the time goes:
time: 540 us; the launch traced here: 531 us
  waiting for transfers between devices  152 us (28%)
  starting transfers between devices  99 us (18%)
  other arithmetic  90.8 us (17%)
  local copies, waits for them, and re-layouts  79.1 us (15%)
  blocking collectives  67.6 us (13%)
  matrix products  27 us (5%)
  between operations  14.7 us (3%)
    psum x1, blocking collectives, on_device(): gram_all, proj_all = lax.psum((gram_local, proj_local), ('gx', 'gy'))  67.6 us
    psum x1, waiting for transfers between devices, on_device(): gram_all, proj_all = lax.psum((gram_local, proj_local), ('gx', 'gy'))  66.6 us
    ppermute x16, starting transfers between devices, padded(): before = lax.ppermute(last, axis, up)  61.9 us
    ppermute x16, waiting for transfers between devices, padded(): before = lax.ppermute(last, axis, up)  46.9 us
    gather x2, local copies, waits for them, and re-layouts, on_device(): height_flat[:, lax.all_to_all(cell_buf.astype(jnp.int32), 'gy', split_axi...  40.5 us
    ppermute x16, waiting for transfers between devices, padded(): after = lax.ppermute(initial, axis, down)  38.8 us
    ppermute x16, starting transfers between devices, padded(): after = lax.ppermute(initial, axis, down)  27.4 us
    unnamed x55, local copies, waits for them, and re-layouts  21 us
  transfers between devices with their start and end apart: 35, of which 19 were waited for; matrix products, arithmetic and copies ran while one was open for 9% of the time, Pallas kernels for 0%

commit v1 on v0

v1 whole, which is shorter than its diff:
```python
import jax
import jax.numpy as jnp
from jax import lax
from jax.experimental import pallas as pl
from jax.experimental.pallas import tpu as pltpu
from jax.sharding import PartitionSpec as P

MEMBERS = 128
ROWS = 32
COLS = 128
HALO = 8
STEPS = 4
CHUNK = 32
CHUNKS = COLS // CHUNK
WIDE_ROWS = ROWS + 2 * HALO
WIDE_COLS = CHUNK + 2 * HALO
LAYERS = 2
HALF = 0.15
TURN = 0.12
COUPLING = 0.5
VMEM = 60 * 1024 * 1024

F32 = jnp.float32
BF16 = jnp.bfloat16


def params():
    return pltpu.CompilerParams(vmem_limit_bytes=VMEM)


def shift(x, axis, by):
    n = lax.axis_size(axis)
    return lax.ppermute(x, axis, [(i, (i + by) % n) for i in range(n)])


def to_lanes_kernel(e_ref, o_ref, rows):
    rows[...] = e_ref[0, 0].astype(F32).reshape(MEMBERS * ROWS, COLS)

    def body(x, carry):
        plane = rows[pl.ds(x, MEMBERS, stride=ROWS), :]
        o_ref[0, 0, x] = plane.T.astype(BF16)
        return carry

    lax.fori_loop(0, ROWS, body, 0, unroll=4)


def to_lanes(ensemble):
    return pl.pallas_call(
        to_lanes_kernel,
        grid=(LAYERS, 3),
        in_specs=[pl.BlockSpec((1, 1, MEMBERS, ROWS, COLS), lambda i, j: (i, j, 0, 0, 0))],
        out_specs=pl.BlockSpec((1, 1, ROWS, COLS, MEMBERS), lambda i, j: (i, j, 0, 0, 0)),
        out_shape=jax.ShapeDtypeStruct((LAYERS, 3, ROWS, COLS, MEMBERS), BF16),
        scratch_shapes=[pltpu.VMEM((MEMBERS * ROWS, COLS), F32)],
        compiler_params=params(),
        name="to_lanes",
    )(ensemble)


def forecast_kernel(
    chunk, et, sides, top, bottom, corner_t, corner_b, depth, col_scale, row_scale,
    out, raw, raw_side, dep, us, vs, hs, fx, fy, pr, sems,
):
    first, last = chunk == 0, chunk == CHUNKS - 1
    lo = 0 if first else chunk * CHUNK - 16
    hi = COLS if last else chunk * CHUNK + 48
    at = 16 if first else 0
    src, dst = pl.ds(lo, hi - lo), pl.ds(at, hi - lo)
    parts = [
        (et.at[:, :, :, src], raw.at[:, :, HALO:HALO + ROWS, dst]),
        (top.at[:, :, :, src], raw.at[:, :, 0:HALO, dst]),
        (bottom.at[:, :, :, src], raw.at[:, :, HALO + ROWS:WIDE_ROWS, dst]),
        (depth.at[:, :, pl.ds(chunk * CHUNK, WIDE_COLS)], dep),
    ]
    if first or last:
        parts += [
            (sides, raw_side.at[:, :, HALO:HALO + ROWS]),
            (corner_t, raw_side.at[:, :, 0:HALO]),
            (corner_b, raw_side.at[:, :, HALO + ROWS:WIDE_ROWS]),
        ]
    copies = [pltpu.make_async_copy(a, b, sems.at[k]) for k, (a, b) in enumerate(parts)]
    for c in copies:
        c.start()
    for c in copies:
        c.wait()

    def load(l, c, r):
        x = raw[l, c, r].astype(F32)
        if first:
            return jnp.concatenate([raw_side[l, c, r].astype(F32)[0:8], x[16:56]], axis=0)
        if last:
            return jnp.concatenate([x[8:48], raw_side[l, c, r].astype(F32)[8:16]], axis=0)
        return x[8:56]

    mid = pl.ds(8, WIDE_COLS)
    left, right = pl.ds(7, WIDE_COLS), pl.ds(9, WIDE_COLS)

    def unpack(r, carry):
        for l in range(LAYERS):
            d = dep[l, r]
            u, v = load(l, 0, r), load(l, 1, r)
            us[l, r] = u
            vs[l, r] = v
            hs[l, r] = load(l, 2, r)
            fx[l, r] = d * u
            fy[l, r, mid] = d * v
        return carry

    lax.fori_loop(0, WIDE_ROWS, unpack, 0)
    cs = col_scale[pl.ds(chunk * CHUNK, WIDE_COLS), :]
    inner = slice(HALO, HALO + CHUNK)

    for step in range(1, STEPS + 1):
        final = step == STEPS

        def thickness(r, carry):
            new = []
            for l in range(LAYERS):
                div = (fx[l, r + 1] - fx[l, r - 1]) + (fy[l, r, right] - fy[l, r, left])
                h = hs[l, r] - div
                hs[l, r] = h
                new.append(h)
            scale = cs * row_scale[0, r]
            pr[0, r, mid] = (new[0] + new[1]) * scale
            pr[1, r, mid] = (COUPLING * new[0] + new[1]) * scale
            return carry

        lax.fori_loop(2 * step - 1, WIDE_ROWS - (2 * step - 1), thickness, 0)

        def velocity(r, carry):
            for l in range(LAYERS):
                u, v = us[l, r], vs[l, r]
                u_new = (u + TURN * v) - (pr[l, r + 1, mid] - pr[l, r - 1, mid])
                v_new = (v - TURN * u) - (pr[l, r, right] - pr[l, r, left])
                if final:
                    out[l, 0, r - HALO] = u_new[inner].astype(BF16)
                    out[l, 1, r - HALO] = v_new[inner].astype(BF16)
                    out[l, 2, r - HALO] = hs[l, r, inner].astype(BF16)
                else:
                    d = dep[l, r]
                    us[l, r] = u_new
                    vs[l, r] = v_new
                    fx[l, r] = d * u_new
                    fy[l, r, mid] = d * v_new
            return carry

        lax.fori_loop(2 * step, WIDE_ROWS - 2 * step, velocity, 0)


def forecast(chunk, et, sides, top, bottom, corner_t, corner_b, depth, col_scale, row_scale):
    plane = (LAYERS, WIDE_ROWS, WIDE_COLS, MEMBERS)
    padded = (LAYERS, WIDE_ROWS, WIDE_COLS + 16, MEMBERS)
    anywhere = pl.BlockSpec(memory_space=pl.ANY)

    def kernel(*refs):
        forecast_kernel(chunk, *refs)

    return pl.pallas_call(
        kernel,
        in_specs=[anywhere] * 7
        + [pl.BlockSpec(memory_space=pltpu.VMEM), pl.BlockSpec(memory_space=pltpu.SMEM)],
        out_specs=pl.BlockSpec(memory_space=pltpu.VMEM),
        out_shape=jax.ShapeDtypeStruct((LAYERS, 3, ROWS, CHUNK, MEMBERS), BF16),
        scratch_shapes=[
            pltpu.VMEM((LAYERS, 3, WIDE_ROWS, 64, MEMBERS), BF16),
            pltpu.VMEM((LAYERS, 3, WIDE_ROWS, 16, MEMBERS), BF16),
            pltpu.VMEM(plane, F32),
            pltpu.VMEM(plane, F32),
            pltpu.VMEM(plane, F32),
            pltpu.VMEM(plane, F32),
            pltpu.VMEM(plane, F32),
            pltpu.VMEM(padded, F32),
            pltpu.VMEM(padded, F32),
            pltpu.SemaphoreType.DMA((7,)),
        ],
        compiler_params=params(),
        name="forecast_%d" % chunk,
    )(et, sides, top, bottom, corner_t, corner_b, depth, col_scale, row_scale)


def gram_kernel(s0, s1, s2, s3, weight, pull, out, high, low):
    def body(x, acc):
        for j, s in enumerate((s0, s1, s2, s3)):
            cols = slice(j * CHUNK, (j + 1) * CHUNK)
            ssh = s[0, 0, x].astype(F32) + s[1, 0, x].astype(F32)
            mean = jnp.sum(ssh, axis=1, keepdims=True) * (1.0 / MEMBERS)
            z = ssh - mean
            w = weight[x, cols]
            y = z * jnp.sqrt(w)
            y_high = y.astype(BF16)
            at = pl.ds(pl.multiple_of(x * COLS + j * CHUNK, CHUNK), CHUNK)
            high[at, :] = y_high
            low[at, :] = (y - y_high.astype(F32)).astype(BF16)
            acc = acc + z * (pull[x, cols] - mean * w)
        return acc

    acc = lax.fori_loop(0, ROWS, body, jnp.zeros((CHUNK, MEMBERS), F32))
    contract = (((0,), (0,)), ((), ()))
    main = lax.dot_general(high[...], high[...], contract, preferred_element_type=F32)
    cross = lax.dot_general(high[...], low[...], contract, preferred_element_type=F32)
    out[0:MEMBERS, :] = main + (cross + cross.T)
    out[MEMBERS:MEMBERS + 8, :] = jnp.broadcast_to(
        jnp.sum(acc, axis=0, keepdims=True), (8, MEMBERS)
    )


def gram_of(states, weight, pull):
    heights = pl.BlockSpec((LAYERS, 1, ROWS, CHUNK, MEMBERS), lambda i: (0, 2, 0, 0, 0))
    cells = pl.BlockSpec((ROWS, COLS, MEMBERS), lambda i: (0, 0, 0))
    return pl.pallas_call(
        gram_kernel,
        grid=(1,),
        in_specs=[heights] * CHUNKS + [cells, cells],
        out_specs=pl.BlockSpec((MEMBERS + 8, MEMBERS), lambda i: (0, 0)),
        out_shape=jax.ShapeDtypeStruct((MEMBERS + 8, MEMBERS), F32),
        scratch_shapes=[
            pltpu.VMEM((ROWS * COLS, MEMBERS), BF16),
            pltpu.VMEM((ROWS * COLS, MEMBERS), BF16),
        ],
        compiler_params=params(),
        name="gram",
    )(*states, weight, pull)


def analysis_kernel(s0, s1, s2, s3, transform_t, out, rows):
    share = jnp.full((MEMBERS, MEMBERS), 1.0 / MEMBERS, BF16)
    share_row = jnp.full((8, MEMBERS), 1.0 / MEMBERS, BF16)
    over_last = (((1,), (1,)), ((), ()))
    tt = transform_t[...]

    def body(x, carry):
        s = jnp.concatenate([r[0, 0, x] for r in (s0, s1, s2, s3)], axis=0)
        center = jnp.dot(s, share, preferred_element_type=F32)
        anomaly = (s.astype(F32) - center).astype(BF16)
        center_row = lax.dot_general(share_row, s, over_last, preferred_element_type=F32)
        mixed = lax.dot_general(tt, anomaly, over_last, preferred_element_type=F32)
        rows[pl.ds(x, MEMBERS, stride=ROWS), :] = mixed + center_row[0:1]
        return carry

    lax.fori_loop(0, ROWS, body, 0, unroll=2)
    out[0, 0] = rows[...].reshape(MEMBERS, ROWS, COLS).astype(BF16)


def analyse(states, transform_t):
    part = pl.BlockSpec((1, 1, ROWS, CHUNK, MEMBERS), lambda i, j: (i, j, 0, 0, 0))
    return pl.pallas_call(
        analysis_kernel,
        grid=(LAYERS, 3),
        in_specs=[part] * CHUNKS + [pl.BlockSpec((MEMBERS, MEMBERS), lambda i, j: (0, 0))],
        out_specs=pl.BlockSpec((1, 1, MEMBERS, ROWS, COLS), lambda i, j: (i, j, 0, 0, 0)),
        out_shape=jax.ShapeDtypeStruct((LAYERS, 3, MEMBERS, ROWS, COLS), BF16),
        scratch_shapes=[pltpu.VMEM((MEMBERS * ROWS, COLS), F32)],
        compiler_params=params(),
        name="analysis",
    )(*states, transform_t)


def split3(x):
    a = lax.reduce_precision(x, 8, 7)
    b = lax.reduce_precision(x - a, 8, 7)
    c = lax.reduce_precision(x - a - b, 8, 7)
    return [p.astype(BF16) for p in (a, b, c)]


def observed_cells(dest, cell, value, sigma):
    tiles = lax.axis_size("gy")
    inverse = 1.0 / sigma
    weight = inverse * inverse
    pieces = jnp.stack(split3(weight) + split3(value * weight), 0).reshape(6, -1)
    row = (dest[:, None] * ROWS + cell // COLS).reshape(-1)
    col = (cell % COLS).reshape(-1)
    row_hot = (row[None, :] == jnp.arange(tiles * ROWS, dtype=jnp.int32)[:, None]).astype(BF16)
    col_hot = col[:, None] == jnp.arange(COLS, dtype=jnp.int32)[None, :]
    spread = jnp.where(col_hot[None], pieces[:, :, None], jnp.zeros((), BF16))
    field = jnp.einsum("rk,pkc->prc", row_hot, spread, preferred_element_type=F32)
    field = jnp.stack([field[2] + field[1] + field[0], field[5] + field[4] + field[3]], 0)
    field = field.reshape(2, tiles, ROWS, COLS).transpose(1, 0, 2, 3)
    me = lax.axis_index("gy")
    bit = tiles // 2
    while bit:
        pair = field.reshape((2, bit) + field.shape[1:])
        mine = (me // bit) % 2
        keep = lax.dynamic_index_in_dim(pair, mine, 0, keepdims=False)
        send = lax.dynamic_index_in_dim(pair, 1 - mine, 0, keepdims=False)
        field = keep + lax.ppermute(send, "gy", [(i, i ^ bit) for i in range(tiles)])
        bit //= 2
    return field[0, 0], field[0, 1]


def sum_everywhere(x):
    def other(axis, k):
        return lax.ppermute(x, axis, [(i, i ^ k) for i in range(lax.axis_size(axis))])

    x = x + other("gy", 1)
    for axis, unit in (("gy", 2), ("gx", 1), ("gx", 4)):
        x = (x + other(axis, unit)) + (other(axis, 2 * unit) + other(axis, 3 * unit))
    return x


def make_transform(gram, proj):
    eye = jnp.eye(MEMBERS, dtype=F32)
    lower = jnp.linalg.cholesky(gram)
    inverse = lax.linalg.triangular_solve(lower, eye, left_side=True, lower=True)
    inner = jnp.dot(inverse, proj, precision=lax.Precision.HIGHEST, preferred_element_type=F32)
    weights = jnp.dot(inverse.T, inner, precision=lax.Precision.HIGHEST, preferred_element_type=F32)
    return (weights[None, :] + jnp.sqrt(F32(MEMBERS - 1)) * inverse).astype(BF16)


def on_device(ensemble, layer_depth, obs_dest, obs_cell, obs_value, obs_sigma):
    et = to_lanes(ensemble)
    from_left = shift(et[:, :, :, COLS - HALO:], "gy", 1)
    from_right = shift(et[:, :, :, :HALO], "gy", -1)
    top = shift(et[:, :, ROWS - HALO:], "gx", 1)
    bottom = shift(et[:, :, :HALO], "gx", -1)
    sides = jnp.concatenate([from_left, from_right], axis=3)
    corner_t = shift(sides[:, :, ROWS - HALO:], "gx", 1)
    corner_b = shift(sides[:, :, :HALO], "gx", -1)

    row0 = lax.axis_index("gx") * ROWS - HALO + jnp.arange(WIDE_ROWS, dtype=jnp.int32)
    col0 = lax.axis_index("gy") * COLS - HALO + jnp.arange(COLS + 2 * HALO, dtype=jnp.int32)
    row_in = (row0 >= 0) & (row0 < lax.axis_size("gx") * ROWS)
    col_in = (col0 >= 0) & (col0 < lax.axis_size("gy") * COLS)
    d = layer_depth
    d = jnp.concatenate(
        [shift(d[:, :, COLS - HALO:], "gy", 1), d, shift(d[:, :, :HALO], "gy", -1)], axis=2
    )
    d = jnp.concatenate(
        [shift(d[:, ROWS - HALO:], "gx", 1), d, shift(d[:, :HALO], "gx", -1)], axis=1
    )
    d = jnp.where(row_in[:, None] & col_in[None, :], HALF * d, 0.0)
    depth = jnp.broadcast_to(d[..., None], d.shape + (MEMBERS,))
    col_scale = jnp.broadcast_to(
        jnp.where(col_in, F32(HALF), F32(0.0))[:, None], (COLS + 2 * HALO, MEMBERS)
    )
    row_scale = row_in.astype(F32)[None, :]

    weight, pull = observed_cells(obs_dest[0, 0], obs_cell[0, 0], obs_value[0, 0], obs_sigma[0, 0])
    weight = jnp.broadcast_to(weight[..., None], (ROWS, COLS, MEMBERS))
    pull = jnp.broadcast_to(pull[..., None], (ROWS, COLS, MEMBERS))

    states = [
        forecast(j, et, sides, top, bottom, corner_t, corner_b, depth, col_scale, row_scale)
        for j in range(CHUNKS)
    ]
    total = sum_everywhere(gram_of(states, weight, pull))
    gram = total[:MEMBERS] + (MEMBERS - 1) * jnp.eye(MEMBERS, dtype=F32)
    return analyse(states, make_transform(gram, total[MEMBERS]))


def solution(mesh):
    in_specs = (
        P(None, None, None, "gx", "gy"),
        P(None, "gx", "gy"),
        P("gx", "gy", None),
        P("gx", "gy", None, None),
        P("gx", "gy", None, None),
        P("gx", "gy", None, None),
    )
    out_specs = P(None, None, None, "gx", "gy")
    return jax.shard_map(
        on_device, mesh=mesh, in_specs=in_specs, out_specs=out_specs, check_vma=False
    )
```

time: 540 us -> 243 us (0.45)
  the two profiles are of different devices: /device:TPU:1 before, /device:TPU:0 now
where the time goes in v1:
time: 243 us
  Pallas kernels  118 us (49%)
  waiting for transfers between devices  39.7 us (16%)
  starting transfers between devices  33.7 us (14%)
  other arithmetic  29.1 us (12%)
  local copies, waits for them, and re-layouts  18.2 us (7%)
  matrix products  3.58 us (1%)
    pallas_call x4, Pallas kernels, forecast(): pl.pallas_call(kernel, in_specs=[anywhere] * 7 + [pl.BlockSpec(memory_spa...  53.2 us
    pallas_call x1, Pallas kernels, analyse(): pl.pallas_call(analysis_kernel, grid=(LAYERS, 3), in_specs=[part] * CHUNK...  43.8 us
    ppermute x10, waiting for transfers between devices, shift(): return lax.ppermute(x, axis, [(i, (i + by) % n) for i in range(n)])  23.2 us
    ppermute x10, starting transfers between devices, shift(): return lax.ppermute(x, axis, [(i, (i + by) % n) for i in range(n)])  19.5 us
    pallas_call x1, Pallas kernels, to_lanes(): pl.pallas_call(to_lanes_kernel, grid=(LAYERS, 3), in_specs=[pl.BlockSpec(...  13.2 us
    another operation x3, other arithmetic, make_transform(): lower = jnp.linalg.cholesky(gram)  12.4 us
    ppermute x10, waiting for transfers between devices, other(): lax.ppermute(x, axis, [(i, i ^ k) for i in range(lax.axis_size(axis))])  12.2 us
    ppermute x10, starting transfers between devices, other(): lax.ppermute(x, axis, [(i, i ^ k) for i in range(lax.axis_size(axis))])  11.6 us
  transfers between devices with their start and end apart: 23, of which 13 were waited for; matrix products, arithmetic and copies ran while one was open for 6% of the time, Pallas kernels for 0%

profile of v1, /device:TPU:0, one launch (start us, length us, event | category | flops | bytes accessed | tf_op | source)
XLA Modules:
  0.0 242.6 jit_solution(8295913230208471710)
XLA Ops:
  0.0 13.2 %to_lanes.1.refs_0_ = bf16[2,3,32,128,128]{4,3,2,1,0:T(8,128)(2,1)} custom-call(bf16[2,3,128,32,128]{4,3,2,1,0:T(8,128)(2,1)} %e_ref.1), custom_call_target="tpu_custom_call" | custom-call | tf_op jit(solution)/shard_map/to_lanes/pallas_call | solution.py:48
  15.4 4.0 %fusion.29 = (bf16[2,3,8,128,128]{4,3,2,1,0:T(8,128)(2,1)}, bf16[2,3,8,128,128]{4,3,2,1,0:T(8,128)(2,1)}) fusion(bf16[2,3,32,128,128]{4,3,2,1,0:T(8,128)(2,1)} %to_lanes.1.refs_0_), kind=kLoop, calls=%fused_computation.83 | loop fusion | bytes 6291456 | tf_op jit(solution)/shard_map/slice | solution.py:314
  21.0 4.9 %collective-permute-start.3 = (bf16[2,3,8,128,128]{4,3,2,1,0:T(8,128)(2,1)}, bf16[2,3,8,128,128]{4,3,2,1,0:T(8,128)(2,1)S(1)}, u32[]{:S(2)}, u32[]{:S(2)}) collective-permute-start(bf16[2,3,8,128,128]{4,3,2,1,0:T(8,128)(2,1)} %get-tuple-element.5), channel_id=1, source_target_pairs={{0,120},{8,0},{16,8},{24,16},{32,24},{40,32},{48,40},{56,48},{64,5... | collective-permute-start | bytes 4718600 | tf_op jit(solution)/shard_map/ppermute | solution.py:33
  26.6 2.6 %collective-permute-start.7 = (f32[2,32,8]{2,1,0:T(8,128)}, f32[2,32,8]{2,1,0:T(8,128)}, u32[]{:S(2)}, u32[]{:S(2)}) collective-permute-start(f32[2,32,8]{2,1,0:T(8,128)} %get-tuple-element.23), channel_id=1, source_target_pairs={{0,7},{1,0},{2,1},{3,2},{4,3},{5,4},{6,5},{7,6},{8,15},{9,8},{10,9... | collective-permute-start | bytes 6152 | tf_op jit(solution)/shard_map/ppermute | solution.py:33
  30.6 3.0 %fusion.8 = f32[6,256,128]{1,2,0:T(8,128)S(1)} fusion(s32[4096]{0:T(1024)S(1)} %get-tuple-element.28, pred[4096,128]{0,1:T(8,128)(4,1)} %iota_compare_fusion.1, bf16[6,4096]{1,0:T(8,128)(2,1)S(1)} %bitcast.90), kind=kOutput, calls=%fused_computation.9 | convolution fusion | flops 1614807040 | bytes 1376256 | tf_op jit(solution)/shard_map/rk,pkc->prc/dot_general | solution.py:275
  38.0 4.0 %collective-permute-done.10 = f32[4,2,32,128]{3,2,1,0:T(8,128)S(1)} collective-permute-done((f32[4,2,32,128]{3,2,1,0:T(8,128)S(1)}, f32[4,2,32,128]{3,2,1,0:T(8,128)S(1)}, u32[]{:S(2)}, u32[]{:S(2)}) %collective-permute-start.10) | collective-permute-done | bytes 131104 | tf_op jit(solution)/shard_map/ppermute | solution.py:285
  42.8 4.0 %collective-permute-done.6 = f32[2,32,8]{2,1,0:T(8,128)S(1)} collective-permute-done((f32[2,32,8]{2,1,0:T(8,128)}, f32[2,32,8]{2,1,0:T(8,128)S(1)}, u32[]{:S(2)}, u32[]{:S(2)}) %collective-permute-start.6) | collective-permute-done | bytes 2080 | tf_op jit(solution)/shard_map/ppermute | solution.py:33
  49.8 10.9 %collective-permute-done.9 = f32[2,8,144]{2,1,0:T(8,128)S(1)} collective-permute-done((f32[2,8,144]{2,1,0:T(8,128)S(1)}, f32[2,8,144]{2,1,0:T(8,128)S(1)}, u32[]{:S(2)}, u32[]{:S(2)}) %collective-permute-start.9) | collective-permute-done | bytes 9248 | tf_op jit(solution)/shard_map/ppermute | solution.py:33
  65.3 3.3 %collective-permute-done.1 = bf16[2,3,32,8,128]{4,3,2,1,0:T(8,128)(2,1)S(1)} collective-permute-done((bf16[2,3,32,8,128]{4,3,2,1,0:T(8,128)(2,1)}, bf16[2,3,32,8,128]{4,3,2,1,0:T(8,128)(2,1)S(1)}, u32[]{:S(2)}, u32[]{:S(2)}) %collective-permute-start.1) | collective-permute-done | bytes 393248 | tf_op jit(solution)/shard_map/ppermute | solution.py:33
  68.8 5.9 %collective-permute-start.5 = (bf16[2,3,8,16,128]{4,3,2,1,0:T(8,128)(2,1)S(1)}, bf16[2,3,8,16,128]{4,3,2,1,0:T(8,128)(2,1)S(1)}, u32[]{:S(2)}, u32[]{:S(2)}) collective-permute-start(bf16[2,3,8,16,128]{4,3,2,1,0:T(8,128)(2,1)S(1)} %get-tuple-element.11), channel_id=1, source_target_pairs={{0,120},{8,0},{16,8},{24,16},{32,24},{40,32},{48,40},{56,48},{64,5... | collective-permute-start | bytes 589832 | tf_op jit(solution)/shard_map/ppermute | solution.py:33
  74.7 4.9 %collective-permute-done.4.refs_4_ = bf16[2,3,8,16,128]{4,3,2,1,0:T(8,128)(2,1)S(1)} collective-permute-done((bf16[2,3,8,16,128]{4,3,2,1,0:T(8,128)(2,1)S(1)}, bf16[2,3,8,16,128]{4,3,2,1,0:T(8,128)(2,1)S(1)}, u32[]{:S(2)}, u32[]{:S(2)}) %collective-permute-start.4) | collective-permute-done | bytes 196640 | tf_op jit(solution)/shard_map/ppermute | solution.py:33
  79.6 4.5 %broadcast_in_dim.75.refs_6_ = f32[2,48,144,128]{3,2,1,0:T(8,128)} broadcast(f32[2,48,144]{2,1,0:T(8,128)S(1)} %fusion.14), dimensions={0,1,2} | broadcast | bytes 7133184 | tf_op jit(solution)/shard_map/broadcast_in_dim | solution.py:331
  84.9 13.3 %forecast_0.1.s0 = bf16[2,3,32,32,128]{4,3,2,1,0:T(8,128)(2,1)} custom-call(bf16[2,3,32,128,128]{4,3,2,1,0:T(8,128)(2,1)} %to_lanes.1.refs_0_, bf16[2,3,32,16,128]{4,3,2,1,0:T(8,128)(2,1)} %copy-done.2, bf16[2,3,8,128,128]{4,3,2,1,0:T(8,128)(2,1)} %copy-done, bf16[2,3,8,128,128]{4,3,2,1,0:T(8,128)(2,1)} %copy-done.1, bf16[2,3,8,16,128]{4,3,2,1,0:T(8,128)(2,1)} %copy-done.3, ...), custom_call_target="tpu_custom_call" | custom-call | tf_op jit(solution)/shard_map/forecast_0/pallas_call | solution.py:158
  98.2 13.3 %forecast_1.1.s1 = bf16[2,3,32,32,128]{4,3,2,1,0:T(8,128)(2,1)} custom-call(bf16[2,3,32,128,128]{4,3,2,1,0:T(8,128)(2,1)} %to_lanes.1.refs_0_, bf16[2,3,32,16,128]{4,3,2,1,0:T(8,128)(2,1)} %copy-done.2, bf16[2,3,8,128,128]{4,3,2,1,0:T(8,128)(2,1)} %copy-done, bf16[2,3,8,128,128]{4,3,2,1,0:T(8,128)(2,1)} %copy-done.1, bf16[2,3,8,16,128]{4,3,2,1,0:T(8,128)(2,1)} %copy-done.3, ...), custom_call_target="tpu_custom_call" | custom-call | tf_op jit(solution)/shard_map/forecast_1/pallas_call | solution.py:158
  111.5 13.4 %forecast_2.1.s2 = bf16[2,3,32,32,128]{4,3,2,1,0:T(8,128)(2,1)} custom-call(bf16[2,3,32,128,128]{4,3,2,1,0:T(8,128)(2,1)} %to_lanes.1.refs_0_, bf16[2,3,32,16,128]{4,3,2,1,0:T(8,128)(2,1)} %copy-done.2, bf16[2,3,8,128,128]{4,3,2,1,0:T(8,128)(2,1)} %copy-done, bf16[2,3,8,128,128]{4,3,2,1,0:T(8,128)(2,1)} %copy-done.1, bf16[2,3,8,16,128]{4,3,2,1,0:T(8,128)(2,1)} %copy-done.3, ...), custom_call_target="tpu_custom_call" | custom-call | tf_op jit(solution)/shard_map/forecast_2/pallas_call | solution.py:158
  124.8 13.3 %forecast_3.1.s3 = bf16[2,3,32,32,128]{4,3,2,1,0:T(8,128)(2,1)} custom-call(bf16[2,3,32,128,128]{4,3,2,1,0:T(8,128)(2,1)} %to_lanes.1.refs_0_, bf16[2,3,32,16,128]{4,3,2,1,0:T(8,128)(2,1)} %copy-done.2, bf16[2,3,8,128,128]{4,3,2,1,0:T(8,128)(2,1)} %copy-done, bf16[2,3,8,128,128]{4,3,2,1,0:T(8,128)(2,1)} %copy-done.1, bf16[2,3,8,16,128]{4,3,2,1,0:T(8,128)(2,1)} %copy-done.3, ...), custom_call_target="tpu_custom_call" | custom-call | tf_op jit(solution)/shard_map/forecast_3/pallas_call | solution.py:158
  142.0 7.7 %gram.1 = f32[136,128]{1,0:T(8,128)} custom-call(bf16[2,3,32,32,128]{4,3,2,1,0:T(8,128)(2,1)} %forecast_0.1.s0, bf16[2,3,32,32,128]{4,3,2,1,0:T(8,128)(2,1)} %forecast_1.1.s1, bf16[2,3,32,32,128]{4,3,2,1,0:T(8,128)(2,1)} %forecast_2.1.s2, bf16[2,3,32,32,128]{4,3,2,1,0:T(8,128)(2,1)} %forecast_3.1.s3, f32[32,128,128]{2,1,0:T(8,128)} %broadcast_in_dim.84.weight, ...), custom_call_target="tpu_custom_call" | custom-call | tf_op jit(solution)/shard_map/gram/pallas_call | solution.py:210
  155.6 2.4 collective-permute-done.15
  160.4 2.6 %collective-permute-start.17 = (f32[136,128]{1,0:T(8,128)S(1)}, f32[136,128]{1,0:T(8,128)S(1)}, u32[]{:S(2)}, u32[]{:S(2)}) collective-permute-start(f32[136,128]{1,0:T(8,128)S(1)} %add_add_fusion.2), channel_id=1, source_target_pairs={{0,8},{8,0},{16,24},{24,16},{32,40},{40,32},{48,56},{56,48},{64,72... | collective-permute-start | bytes 208904 | tf_op jit(solution)/shard_map/ppermute | solution.py:292
  163.0 2.8 %collective-permute-done.18 = f32[136,128]{1,0:T(8,128)S(1)} collective-permute-done((f32[136,128]{1,0:T(8,128)S(1)}, f32[136,128]{1,0:T(8,128)S(1)}, u32[]{:S(2)}, u32[]{:S(2)}) %collective-permute-start.18) | collective-permute-done | bytes 69664 | tf_op jit(solution)/shard_map/ppermute | solution.py:292
  166.1 2.8 %collective-permute-start.21 = (f32[136,128]{1,0:T(8,128)S(1)}, f32[136,128]{1,0:T(8,128)S(1)}, u32[]{:S(2)}, u32[]{:S(2)}) collective-permute-start(f32[136,128]{1,0:T(8,128)S(1)} %add_add_fusion.1), channel_id=1, source_target_pairs={{0,64},{8,72},{16,80},{24,88},{32,96},{40,104},{48,112},{56,120},{... | collective-permute-start | bytes 208904 | tf_op jit(solution)/shard_map/ppermute | solution.py:292
  174.6 11.7 %cholesky.17 = f32[128,128]{1,0:T(8,128)S(1)} custom-call(f32[128,128]{1,0:T(8,128)S(1)} %fusion.19), custom_call_target="Cholesky" | custom-call | tf_op jit(solution)/shard_map/jit(cholesky)/cholesky | solution.py:302
  187.7 9.8 %custom-call.6 = f32[1,128,128]{1,2,0:T(8,128)S(1)} custom-call(f32[1,128,128]{2,1,0:T(8,128)S(1)} %fusion.15), custom_call_target="InvertDiagBlocksLowerTriangular" | custom-call | tf_op jit(solution)/shard_map/triangular_solve | solution.py:303
  198.7 43.8 %analysis.1 = bf16[2,3,128,32,128]{4,3,2,1,0:T(8,128)(2,1)} custom-call(bf16[2,3,32,32,128]{4,3,2,1,0:T(8,128)(2,1)} %forecast_0.1.s0, bf16[2,3,32,32,128]{4,3,2,1,0:T(8,128)(2,1)} %forecast_1.1.s1, bf16[2,3,32,32,128]{4,3,2,1,0:T(8,128)(2,1)} %forecast_2.1.s2, bf16[2,3,32,32,128]{4,3,2,1,0:T(8,128)(2,1)} %forecast_3.1.s3, ...), custom_call_target="tpu_custom_call" | custom-call | tf_op jit(solution)/shard_map/analysis/pallas_call | solution.py:246
  (101 shorter events, 40.2 us)
Async XLA Ops:
  15.3 15.1 %copy-start.8 = (f32[1,1,32,128]{3,2,1,0:T(8,128)S(1)}, f32[1,1,32,128]{3,2,1,0:T(8,128)}, u32[]{:S(2)}) copy-start(f32[1,1,32,128]{3,2,1,0:T(8,128)} %param.10) | copy-start | bytes 49156
  15.3 48.9 %collective-permute-start = (bf16[2,3,32,8,128]{4,3,2,1,0:T(8,128)(2,1)}, bf16[2,3,32,8,128]{4,3,2,1,0:T(8,128)(2,1)}, u32[]{:S(2)}, u32[]{:S(2)}) collective-permute-start(bf16[2,3,32,8,128]{4,3,2,1,0:T(8,128)(2,1)} %get-tuple-element.8), channel_id=1, source_target_pairs={{0,1},{1,2},{2,3},{3,4},{4,5},{5,6},{6,7},{7,0},{8,9},{9,10},{10,1... | collective-permute-start | bytes 1179656 | tf_op jit(solution)/shard_map/ppermute | solution.py:33
  19.3 60.2 %collective-permute-start.2 = (bf16[2,3,8,128,128]{4,3,2,1,0:T(8,128)(2,1)}, bf16[2,3,8,128,128]{4,3,2,1,0:T(8,128)(2,1)S(1)}, u32[]{:S(2)}, u32[]{:S(2)}) collective-permute-start(bf16[2,3,8,128,128]{4,3,2,1,0:T(8,128)(2,1)} %get-tuple-element.6), channel_id=1, source_target_pairs={{0,8},{8,16},{16,24},{24,32},{32,40},{40,48},{48,56},{56,64},{64,7... | collective-permute-start | bytes 4718600 | tf_op jit(solution)/shard_map/ppermute | solution.py:33
  21.0 58.6 %collective-permute-start.3 = (bf16[2,3,8,128,128]{4,3,2,1,0:T(8,128)(2,1)}, bf16[2,3,8,128,128]{4,3,2,1,0:T(8,128)(2,1)S(1)}, u32[]{:S(2)}, u32[]{:S(2)}) collective-permute-start(bf16[2,3,8,128,128]{4,3,2,1,0:T(8,128)(2,1)} %get-tuple-element.5), channel_id=1, source_target_pairs={{0,120},{8,0},{16,8},{24,16},{32,24},{40,32},{48,40},{56,48},{64,5... | collective-permute-start | bytes 4718600 | tf_op jit(solution)/shard_map/ppermute | solution.py:33
  26.6 15.5 %collective-permute-start.7 = (f32[2,32,8]{2,1,0:T(8,128)}, f32[2,32,8]{2,1,0:T(8,128)}, u32[]{:S(2)}, u32[]{:S(2)}) collective-permute-start(f32[2,32,8]{2,1,0:T(8,128)} %get-tuple-element.23), channel_id=1, source_target_pairs={{0,7},{1,0},{2,1},{3,2},{4,3},{5,4},{6,5},{7,6},{8,15},{9,8},{10,9... | collective-permute-start | bytes 6152 | tf_op jit(solution)/shard_map/ppermute | solution.py:33
  35.5 6.6 %collective-permute-start.10 = (f32[4,2,32,128]{3,2,1,0:T(8,128)S(1)}, f32[4,2,32,128]{3,2,1,0:T(8,128)S(1)}, u32[]{:S(2)}, u32[]{:S(2)}) collective-permute-start(f32[4,2,32,128]{3,2,1,0:T(8,128)S(1)} %bitcast.89), channel_id=1, source_target_pairs={{0,4},{1,5},{2,6},{3,7},{4,0},{5,1},{6,2},{7,3},{8,12},{9,13},{10,... | collective-permute-start | bytes 393224 | tf_op jit(solution)/shard_map/ppermute | solution.py:285
  42.1 4.8 %collective-permute-start.6 = (f32[2,32,8]{2,1,0:T(8,128)}, f32[2,32,8]{2,1,0:T(8,128)S(1)}, u32[]{:S(2)}, u32[]{:S(2)}) collective-permute-start(f32[2,32,8]{2,1,0:T(8,128)} %get-tuple-element.22), channel_id=1, source_target_pairs={{0,1},{1,2},{2,3},{3,4},{4,5},{5,6},{6,7},{7,0},{8,9},{9,10},{10,1... | collective-permute-start | bytes 6152 | tf_op jit(solution)/shard_map/ppermute | solution.py:33
  42.1 7.3 %collective-permute-start.11 = (f32[2,2,32,128]{3,2,1,0:T(8,128)S(1)}, f32[2,2,32,128]{3,2,1,0:T(8,128)S(1)}, u32[]{:S(2)}, u32[]{:S(2)}) collective-permute-start(f32[2,2,32,128]{3,2,1,0:T(8,128)S(1)} %dynamic-slice_bitcast_fusion), channel_id=1, source_target_pairs={{0,2},{1,3},{2,0},{3,1},{4,6},{5,7},{6,4},{7,5},{8,10},{9,11},{10,... | collective-permute-start | bytes 196616 | tf_op jit(solution)/shard_map/ppermute | solution.py:285
  47.6 13.1 %collective-permute-start.9 = (f32[2,8,144]{2,1,0:T(8,128)S(1)}, f32[2,8,144]{2,1,0:T(8,128)S(1)}, u32[]{:S(2)}, u32[]{:S(2)}) collective-permute-start(f32[2,8,144]{2,1,0:T(8,128)S(1)} %get-tuple-element.16), channel_id=1, source_target_pairs={{0,120},{8,0},{16,8},{24,16},{32,24},{40,32},{48,40},{56,48},{64,5... | collective-permute-start | bytes 27656 | tf_op jit(solution)/shard_map/ppermute | solution.py:33
  49.5 13.5 %collective-permute-start.8 = (f32[2,8,144]{2,1,0:T(8,128)S(1)}, f32[2,8,144]{2,1,0:T(8,128)S(1)}, u32[]{:S(2)}, u32[]{:S(2)}) collective-permute-start(f32[2,8,144]{2,1,0:T(8,128)S(1)} %get-tuple-element.15), channel_id=1, source_target_pairs={{0,8},{8,16},{16,24},{24,32},{32,40},{40,48},{48,56},{56,64},{64,7... | collective-permute-start | bytes 27656 | tf_op jit(solution)/shard_map/ppermute | solution.py:33
  60.7 7.9 %collective-permute-start.1 = (bf16[2,3,32,8,128]{4,3,2,1,0:T(8,128)(2,1)}, bf16[2,3,32,8,128]{4,3,2,1,0:T(8,128)(2,1)S(1)}, u32[]{:S(2)}, u32[]{:S(2)}) collective-permute-start(bf16[2,3,32,8,128]{4,3,2,1,0:T(8,128)(2,1)} %get-tuple-element.7), channel_id=1, source_target_pairs={{0,7},{1,0},{2,1},{3,2},{4,3},{5,4},{6,5},{7,6},{8,15},{9,8},{10,9... | collective-permute-start | bytes 1179656 | tf_op jit(solution)/shard_map/ppermute | solution.py:33
  63.0 1.2 collective-permute-start.12
  68.7 10.8 %collective-permute-start.4 = (bf16[2,3,8,16,128]{4,3,2,1,0:T(8,128)(2,1)S(1)}, bf16[2,3,8,16,128]{4,3,2,1,0:T(8,128)(2,1)S(1)}, u32[]{:S(2)}, u32[]{:S(2)}) collective-permute-start(bf16[2,3,8,16,128]{4,3,2,1,0:T(8,128)(2,1)S(1)} %get-tuple-element.12), channel_id=1, source_target_pairs={{0,8},{8,16},{16,24},{24,32},{32,40},{40,48},{48,56},{56,64},{64,7... | collective-permute-start | bytes 589832 | tf_op jit(solution)/shard_map/ppermute | solution.py:33
  68.8 10.8 %collective-permute-start.5 = (bf16[2,3,8,16,128]{4,3,2,1,0:T(8,128)(2,1)S(1)}, bf16[2,3,8,16,128]{4,3,2,1,0:T(8,128)(2,1)S(1)}, u32[]{:S(2)}, u32[]{:S(2)}) collective-permute-start(bf16[2,3,8,16,128]{4,3,2,1,0:T(8,128)(2,1)S(1)} %get-tuple-element.11), channel_id=1, source_target_pairs={{0,120},{8,0},{16,8},{24,16},{32,24},{40,32},{48,40},{56,48},{64,5... | collective-permute-start | bytes 589832 | tf_op jit(solution)/shard_map/ppermute | solution.py:33
  149.7 1.5 collective-permute-start.13
  152.0 5.9 %collective-permute-start.15 = (f32[136,128]{1,0:T(8,128)S(1)}, f32[136,128]{1,0:T(8,128)S(1)}, u32[]{:S(2)}, u32[]{:S(2)}) collective-permute-start(f32[136,128]{1,0:T(8,128)S(1)} %add.206), channel_id=1, source_target_pairs={{0,4},{1,5},{2,6},{3,7},{4,0},{5,1},{6,2},{7,3},{8,12},{9,13},{10,... | collective-permute-start | bytes 208904 | tf_op jit(solution)/shard_map/ppermute | solution.py:292
  153.6 5.8 %collective-permute-start.16 = (f32[136,128]{1,0:T(8,128)S(1)}, f32[136,128]{1,0:T(8,128)S(1)}, u32[]{:S(2)}, u32[]{:S(2)}) collective-permute-start(f32[136,128]{1,0:T(8,128)S(1)} %add.206), channel_id=1, source_target_pairs={{0,6},{1,7},{2,4},{3,5},{4,2},{5,3},{6,0},{7,1},{8,14},{9,15},{10,... | collective-permute-start | bytes 208904 | tf_op jit(solution)/shard_map/ppermute | solution.py:292
  154.8 4.7 %collective-permute-start.14 = (f32[136,128]{1,0:T(8,128)S(1)}, f32[136,128]{1,0:T(8,128)S(1)}, u32[]{:S(2)}, u32[]{:S(2)}) collective-permute-start(f32[136,128]{1,0:T(8,128)S(1)} %add.206), channel_id=1, source_target_pairs={{0,2},{1,3},{2,0},{3,1},{4,6},{5,7},{6,4},{7,5},{8,10},{9,11},{10,... | collective-permute-start | bytes 208904 | tf_op jit(solution)/shard_map/ppermute | solution.py:292
  159.4 6.3 %collective-permute-start.18 = (f32[136,128]{1,0:T(8,128)S(1)}, f32[136,128]{1,0:T(8,128)S(1)}, u32[]{:S(2)}, u32[]{:S(2)}) collective-permute-start(f32[136,128]{1,0:T(8,128)S(1)} %add_add_fusion.2), channel_id=1, source_target_pairs={{0,16},{8,24},{16,0},{24,8},{32,48},{40,56},{48,32},{56,40},{64,80... | collective-permute-start | bytes 208904 | tf_op jit(solution)/shard_map/ppermute | solution.py:292
  159.7 6.3 %collective-permute-start.19 = (f32[136,128]{1,0:T(8,128)S(1)}, f32[136,128]{1,0:T(8,128)S(1)}, u32[]{:S(2)}, u32[]{:S(2)}) collective-permute-start(f32[136,128]{1,0:T(8,128)S(1)} %add_add_fusion.2), channel_id=1, source_target_pairs={{0,24},{8,16},{16,8},{24,0},{32,56},{40,48},{48,40},{56,32},{64,88... | collective-permute-start | bytes 208904 | tf_op jit(solution)/shard_map/ppermute | solution.py:292
  160.4 5.6 %collective-permute-start.17 = (f32[136,128]{1,0:T(8,128)S(1)}, f32[136,128]{1,0:T(8,128)S(1)}, u32[]{:S(2)}, u32[]{:S(2)}) collective-permute-start(f32[136,128]{1,0:T(8,128)S(1)} %add_add_fusion.2), channel_id=1, source_target_pairs={{0,8},{8,0},{16,24},{24,16},{32,40},{40,32},{48,56},{56,48},{64,72... | collective-permute-start | bytes 208904 | tf_op jit(solution)/shard_map/ppermute | solution.py:292
  166.1 6.5 %collective-permute-start.21 = (f32[136,128]{1,0:T(8,128)S(1)}, f32[136,128]{1,0:T(8,128)S(1)}, u32[]{:S(2)}, u32[]{:S(2)}) collective-permute-start(f32[136,128]{1,0:T(8,128)S(1)} %add_add_fusion.1), channel_id=1, source_target_pairs={{0,64},{8,72},{16,80},{24,88},{32,96},{40,104},{48,112},{56,120},{... | collective-permute-start | bytes 208904 | tf_op jit(solution)/shard_map/ppermute | solution.py:292
  168.9 5.5 %collective-permute-start.22 = (f32[136,128]{1,0:T(8,128)S(1)}, f32[136,128]{1,0:T(8,128)S(1)}, u32[]{:S(2)}, u32[]{:S(2)}) collective-permute-start(f32[136,128]{1,0:T(8,128)S(1)} %add_add_fusion.1), channel_id=1, source_target_pairs={{0,96},{8,104},{16,112},{24,120},{32,64},{40,72},{48,80},{56,88},{... | collective-permute-start | bytes 208904 | tf_op jit(solution)/shard_map/ppermute | solution.py:292
  169.9 4.5 %collective-permute-start.20 = (f32[136,128]{1,0:T(8,128)S(1)}, f32[136,128]{1,0:T(8,128)S(1)}, u32[]{:S(2)}, u32[]{:S(2)}) collective-permute-start(f32[136,128]{1,0:T(8,128)S(1)} %add_add_fusion.1), channel_id=1, source_target_pairs={{0,32},{8,40},{16,48},{24,56},{32,0},{40,8},{48,16},{56,24},{64,96... | collective-permute-start | bytes 208904 | tf_op jit(solution)/shard_map/ppermute | solution.py:292
  (9 other events, 82.6 us)

commit v2 on v1

v2 whole, which is shorter than its diff:
```python
import jax
import jax.numpy as jnp
from jax import lax
from jax.experimental import pallas as pl
from jax.experimental.pallas import tpu as pltpu
from jax.sharding import PartitionSpec as P

MEMBERS = 128
ROWS = 32
COLS = 128
HALO = 8
STEPS = 4
WIDE_ROWS = ROWS + 2 * HALO
WIDE_COLS = COLS + 2 * HALO
SEGMENTS = 16
POSITIONS = WIDE_COLS // SEGMENTS
LINE = 40
LAYERS = 2
HALF = 0.15
TURN = 0.12
COUPLING = 0.5
VMEM = 60 * 1024 * 1024

F32 = jnp.float32
BF16 = jnp.bfloat16


def params():
    return pltpu.CompilerParams(vmem_limit_bytes=VMEM)


def shift(x, axis, by):
    n = lax.axis_size(axis)
    return lax.ppermute(x, axis, [(i, (i + by) % n) for i in range(n)])


def to_lanes(block):
    layers, parts, members, rows, cols = block.shape
    pitch = rows + 1

    def kernel(e_ref, o_ref, planes):
        def spread(m, carry):
            for k in range(4):
                planes[pl.ds((4 * m + k) * pitch, rows), :] = e_ref[0, 0, 4 * m + k].astype(F32)
            return carry

        lax.fori_loop(0, members // 4, spread, 0, unroll=2)

        def turn(x, carry):
            o_ref[0, 0, x] = planes[pl.ds(x, members, stride=pitch), :].astype(BF16).T
            return carry

        lax.fori_loop(0, rows, turn, 0, unroll=4)

    return pl.pallas_call(
        kernel,
        grid=(layers, parts),
        in_specs=[pl.BlockSpec((1, 1, members, rows, cols), lambda i, j: (i, j, 0, 0, 0))],
        out_specs=pl.BlockSpec((1, 1, rows, cols, members), lambda i, j: (i, j, 0, 0, 0)),
        out_shape=jax.ShapeDtypeStruct((layers, parts, rows, cols, members), BF16),
        scratch_shapes=[pltpu.VMEM((members * pitch, cols), F32)],
        compiler_params=params(),
        name="to_lanes_%d" % rows,
    )(block)


def forecast_kernel(
    et, sides, top, bottom, corner_t, corner_b, depth, row_in, masks,
    out, raw, raw_side, st, fx, fy, pr, line, sems,
):
    low, high = pl.ds(0, HALO), pl.ds(HALO + ROWS, HALO)
    copies = []
    for l in range(LAYERS):
        for c in range(3):
            parts = [
                (et.at[l, c], raw.at[l, c, pl.ds(HALO, ROWS)]),
                (top.at[l, c], raw.at[l, c, low]),
                (bottom.at[l, c], raw.at[l, c, high]),
                (sides.at[l, c], raw_side.at[l, c, pl.ds(HALO, ROWS)]),
                (corner_t.at[l, c], raw_side.at[l, c, low]),
                (corner_b.at[l, c], raw_side.at[l, c, high]),
            ]
            copies.append(
                [
                    pltpu.make_async_copy(a, b, sems.at[(3 * l + c) * 6 + k])
                    for k, (a, b) in enumerate(parts)
                ]
            )
    for group in copies:
        for c in group:
            c.start()

    def rolled(x, by):
        return pltpu.roll(x.astype(F32), by % SEGMENTS, 0).astype(BF16)

    def put_flux(l, r, flux):
        fy[l, r, 1:POSITIONS + 1] = flux
        fy[l, r, 0] = rolled(flux[POSITIONS - 1], 1)
        fy[l, r, POSITIONS + 1] = rolled(flux[0], -1)

    def put_pressure(l, r, value):
        pr[l, r, 1:POSITIONS + 1] = value
        pr[l, r, 0] = rolled(value[POSITIONS - 1], 1)
        pr[l, r, POSITIONS + 1] = rolled(value[0], -1)

    for l in range(LAYERS):
        for c in range(3):
            for d in copies[3 * l + c]:
                d.wait()

            def unpack(r, carry):
                scale = HALF if c == 2 else 1.0
                side = raw_side[l, c, r].astype(F32) * scale
                base = lax.rem(r, 4) * (4 * LINE)
                line[pl.ds(base, 8), :] = side[0:8]
                line[pl.ds(base + 8, COLS), :] = raw[l, c, r].astype(F32) * scale
                line[pl.ds(base + 8 + COLS, 8), :] = side[8:16]
                value = jnp.stack(
                    [
                        line[pl.ds(base + p, SEGMENTS, stride=POSITIONS), :].astype(BF16)
                        for p in range(POSITIONS)
                    ],
                    axis=0,
                )
                st[l, c, r] = value
                if c == 0:
                    fx[l, r] = depth[l, r] * value
                elif c == 1:
                    put_flux(l, r, depth[l, r] * value)
                return carry

            lax.fori_loop(0, WIDE_ROWS, unpack, 0, unroll=2)

    for step in range(1, STEPS + 1):

        def thickness(r, carry):
            new = []
            for l in range(LAYERS):
                div = (fx[l, r + 1] - fx[l, r - 1]) + (
                    fy[l, r, 2:POSITIONS + 2] - fy[l, r, 0:POSITIONS]
                )
                h = st[l, 2, r] - div
                st[l, 2, r] = h
                new.append(h)
            mask = masks[row_in[0, r]]
            put_pressure(0, r, (new[0] + new[1]) * mask)
            put_pressure(1, r, (BF16(COUPLING) * new[0] + new[1]) * mask)
            return carry

        lax.fori_loop(2 * step - 1, WIDE_ROWS - (2 * step - 1), thickness, 0)

        def velocity(r, carry):
            for l in range(LAYERS):
                u, v = st[l, 0, r], st[l, 1, r]
                u_new = (u + BF16(TURN) * v) - (
                    pr[l, r + 1, 1:POSITIONS + 1] - pr[l, r - 1, 1:POSITIONS + 1]
                )
                v_new = (v - BF16(TURN) * u) - (
                    pr[l, r, 2:POSITIONS + 2] - pr[l, r, 0:POSITIONS]
                )
                st[l, 0, r] = u_new
                st[l, 1, r] = v_new
                if step < STEPS:
                    d = depth[l, r]
                    fx[l, r] = d * u_new
                    put_flux(l, r, d * v_new)
            return carry

        lax.fori_loop(2 * step, WIDE_ROWS - 2 * step, velocity, 0)

    for l in range(LAYERS):
        for c in range(3):

            def pack(r, carry):
                base = lax.rem(r, 4) * (4 * LINE)
                for p in range(POSITIONS):
                    line[pl.ds(base + p, SEGMENTS, stride=POSITIONS), :] = st[
                        l, c, r + HALO, p
                    ].astype(F32)
                value = line[pl.ds(base + 8, COLS), :]
                if c == 2:
                    value = value * (1.0 / HALF)
                out[l, c, r] = value.astype(BF16)
                return carry

            lax.fori_loop(0, ROWS, pack, 0, unroll=2)


def forecast(et, sides, top, bottom, corner_t, corner_b, depth, row_in, masks):
    plane = (LAYERS, WIDE_ROWS, POSITIONS, SEGMENTS, MEMBERS)
    padded = (LAYERS, WIDE_ROWS, POSITIONS + 2, SEGMENTS, MEMBERS)
    anywhere = pl.BlockSpec(memory_space=pl.ANY)
    vmem = pl.BlockSpec(memory_space=pltpu.VMEM)
    return pl.pallas_call(
        forecast_kernel,
        in_specs=[anywhere] * 6 + [vmem, pl.BlockSpec(memory_space=pltpu.SMEM), vmem],
        out_specs=vmem,
        out_shape=jax.ShapeDtypeStruct((LAYERS, 3, ROWS, COLS, MEMBERS), BF16),
        scratch_shapes=[
            pltpu.VMEM((LAYERS, 3, WIDE_ROWS, COLS, MEMBERS), BF16),
            pltpu.VMEM((LAYERS, 3, WIDE_ROWS, 16, MEMBERS), BF16),
            pltpu.VMEM((LAYERS, 3) + plane[1:], BF16),
            pltpu.VMEM(plane, BF16),
            pltpu.VMEM(padded, BF16),
            pltpu.VMEM(padded, BF16),
            pltpu.VMEM((16 * LINE, MEMBERS), F32),
            pltpu.SemaphoreType.DMA((36,)),
        ],
        compiler_params=params(),
        name="forecast",
    )(et, sides, top, bottom, corner_t, corner_b, depth, row_in, masks)


def gram_kernel(heights, weight, pull, out, high, low):
    def body(x, acc):
        ssh = heights[0, 0, x].astype(F32) + heights[1, 0, x].astype(F32)
        mean = jnp.sum(ssh, axis=1, keepdims=True) * (1.0 / MEMBERS)
        z = ssh - mean
        w = weight[x]
        y = z * jnp.sqrt(w)
        y_high = y.astype(BF16)
        at = pl.ds(pl.multiple_of(x * COLS, COLS), COLS)
        high[at, :] = y_high
        low[at, :] = (y - y_high.astype(F32)).astype(BF16)
        pulled = z * (pull[x] - mean * w)
        return acc + jnp.sum(pulled.reshape(COLS // 8, 8, MEMBERS), axis=0)

    acc = lax.fori_loop(0, ROWS, body, jnp.zeros((8, MEMBERS), F32))
    contract = (((0,), (0,)), ((), ()))
    main = lax.dot_general(high[...], high[...], contract, preferred_element_type=F32)
    cross = lax.dot_general(high[...], low[...], contract, preferred_element_type=F32)
    out[0:MEMBERS, :] = main + (cross + cross.T)
    out[MEMBERS:MEMBERS + 8, :] = jnp.broadcast_to(
        jnp.sum(acc, axis=0, keepdims=True), (8, MEMBERS)
    )


def gram_of(state, weight, pull):
    cells = pl.BlockSpec((ROWS, COLS, MEMBERS), lambda i: (0, 0, 0))
    return pl.pallas_call(
        gram_kernel,
        grid=(1,),
        in_specs=[
            pl.BlockSpec((LAYERS, 1, ROWS, COLS, MEMBERS), lambda i: (0, 2, 0, 0, 0)),
            cells,
            cells,
        ],
        out_specs=pl.BlockSpec((MEMBERS + 8, MEMBERS), lambda i: (0, 0)),
        out_shape=jax.ShapeDtypeStruct((MEMBERS + 8, MEMBERS), F32),
        scratch_shapes=[
            pltpu.VMEM((ROWS * COLS, MEMBERS), BF16),
            pltpu.VMEM((ROWS * COLS, MEMBERS), BF16),
        ],
        compiler_params=params(),
        name="gram",
    )(state, weight, pull)


def analysis_kernel(state, mix, out, planes):
    pitch = ROWS + 1
    over_last = (((1,), (1,)), ((), ()))
    both = mix[...]

    def body(x, carry):
        s = state[0, 0, pl.ds(2 * x, 2)].reshape(2 * COLS, MEMBERS)
        mixed = lax.dot_general(
            both, jnp.concatenate([s, s], axis=1), over_last, preferred_element_type=F32
        )
        planes[pl.ds(2 * x, MEMBERS, stride=pitch), :] = mixed[:, :COLS]
        planes[pl.ds(2 * x + 1, MEMBERS, stride=pitch), :] = mixed[:, COLS:]
        return carry

    lax.fori_loop(0, ROWS // 2, body, 0, unroll=2)

    def gather(m, carry):
        for k in range(4):
            out[0, 0, 4 * m + k] = planes[pl.ds((4 * m + k) * pitch, ROWS), :].astype(BF16)
        return carry

    lax.fori_loop(0, MEMBERS // 4, gather, 0, unroll=2)


def analyse(state, mix):
    return pl.pallas_call(
        analysis_kernel,
        grid=(LAYERS, 3),
        in_specs=[
            pl.BlockSpec((1, 1, ROWS, COLS, MEMBERS), lambda i, j: (i, j, 0, 0, 0)),
            pl.BlockSpec((MEMBERS, 2 * MEMBERS), lambda i, j: (0, 0)),
        ],
        out_specs=pl.BlockSpec((1, 1, MEMBERS, ROWS, COLS), lambda i, j: (i, j, 0, 0, 0)),
        out_shape=jax.ShapeDtypeStruct((LAYERS, 3, MEMBERS, ROWS, COLS), BF16),
        scratch_shapes=[pltpu.VMEM((MEMBERS * (ROWS + 1), COLS), F32)],
        compiler_params=params(),
        name="analysis",
    )(state, mix)


def split3(x):
    a = lax.reduce_precision(x, 8, 7)
    b = lax.reduce_precision(x - a, 8, 7)
    c = lax.reduce_precision(x - a - b, 8, 7)
    return [p.astype(BF16) for p in (a, b, c)]


def observed_cells(dest, cell, value, sigma):
    tiles = lax.axis_size("gy")
    inverse = 1.0 / sigma
    weight = inverse * inverse
    pieces = jnp.stack(split3(weight) + split3(value * weight), 0).reshape(6, -1)
    row = (dest[:, None] * ROWS + cell // COLS).reshape(-1)
    col = (cell % COLS).reshape(-1)
    row_hot = (row[None, :] == jnp.arange(tiles * ROWS, dtype=jnp.int32)[:, None]).astype(BF16)
    col_hot = col[:, None] == jnp.arange(COLS, dtype=jnp.int32)[None, :]
    spread = jnp.where(col_hot[None], pieces[:, :, None], jnp.zeros((), BF16))
    field = jnp.einsum("rk,pkc->prc", row_hot, spread, preferred_element_type=F32)
    field = jnp.stack([field[2] + field[1] + field[0], field[5] + field[4] + field[3]], 0)
    field = field.reshape(2, tiles, ROWS, COLS).transpose(1, 0, 2, 3)
    me = lax.axis_index("gy")
    bit = tiles // 2
    while bit:
        pair = field.reshape((2, bit) + field.shape[1:])
        mine = (me // bit) % 2
        keep = lax.dynamic_index_in_dim(pair, mine, 0, keepdims=False)
        send = lax.dynamic_index_in_dim(pair, 1 - mine, 0, keepdims=False)
        field = keep + lax.ppermute(send, "gy", [(i, i ^ bit) for i in range(tiles)])
        bit //= 2
    return field[0, 0], field[0, 1]


def sum_everywhere(x):
    def other(axis, k):
        return lax.ppermute(x, axis, [(i, i ^ k) for i in range(lax.axis_size(axis))])

    x = x + other("gy", 1)
    for axis, unit in (("gy", 2), ("gx", 1), ("gx", 4)):
        x = (x + other(axis, unit)) + (other(axis, 2 * unit) + other(axis, 3 * unit))
    return x


def make_transform(gram, proj):
    eye = jnp.eye(MEMBERS, dtype=F32)
    lower = jnp.linalg.cholesky(gram)
    inverse = lax.linalg.triangular_solve(lower, eye, left_side=True, lower=True)
    inner = jnp.dot(inverse, proj, precision=lax.Precision.HIGHEST, preferred_element_type=F32)
    weights = jnp.dot(inverse.T, inner, precision=lax.Precision.HIGHEST, preferred_element_type=F32)
    transform_t = weights[None, :] + jnp.sqrt(F32(MEMBERS - 1)) * inverse
    spare = (1.0 - jnp.sum(transform_t, axis=1, keepdims=True)) * (1.0 / MEMBERS)
    mix = transform_t + spare
    high = lax.reduce_precision(mix, 8, 7)
    return jnp.concatenate([high.astype(BF16), (mix - high).astype(BF16)], axis=1)


def on_device(ensemble, layer_depth, obs_dest, obs_cell, obs_value, obs_sigma):
    top = to_lanes(shift(ensemble[:, :, :, ROWS - HALO:], "gx", 1))
    bottom = to_lanes(shift(ensemble[:, :, :, :HALO], "gx", -1))
    et = to_lanes(ensemble)
    from_left = shift(et[:, :, :, COLS - HALO:], "gy", 1)
    from_right = shift(et[:, :, :, :HALO], "gy", -1)
    sides = jnp.concatenate([from_left, from_right], axis=3)
    corner_t = shift(sides[:, :, ROWS - HALO:], "gx", 1)
    corner_b = shift(sides[:, :, :HALO], "gx", -1)

    row0 = lax.axis_index("gx") * ROWS - HALO + jnp.arange(WIDE_ROWS, dtype=jnp.int32)
    col0 = lax.axis_index("gy") * COLS - HALO + jnp.arange(COLS + 2 * HALO, dtype=jnp.int32)
    row_in = (row0 >= 0) & (row0 < lax.axis_size("gx") * ROWS)
    col_in = (col0 >= 0) & (col0 < lax.axis_size("gy") * COLS)
    d = layer_depth
    d = jnp.concatenate(
        [shift(d[:, :, COLS - HALO:], "gy", 1), d, shift(d[:, :, :HALO], "gy", -1)], axis=2
    )
    d = jnp.concatenate(
        [shift(d[:, ROWS - HALO:], "gx", 1), d, shift(d[:, :HALO], "gx", -1)], axis=1
    )
    d = jnp.where(row_in[:, None] & col_in[None, :], (HALF * HALF) * d, 0.0).astype(BF16)
    d = d.reshape(LAYERS, WIDE_ROWS, SEGMENTS, POSITIONS).transpose(0, 1, 3, 2)
    depth = jnp.broadcast_to(d[..., None], d.shape + (MEMBERS,))
    mask = col_in.reshape(SEGMENTS, POSITIONS).T.astype(BF16)
    mask = jnp.stack([jnp.zeros_like(mask), mask], axis=0)
    masks = jnp.broadcast_to(mask[..., None], mask.shape + (MEMBERS,))
    row_in = row_in.astype(jnp.int32)[None, :]

    weight, pull = observed_cells(obs_dest[0, 0], obs_cell[0, 0], obs_value[0, 0], obs_sigma[0, 0])
    weight = jnp.broadcast_to(weight[..., None], (ROWS, COLS, MEMBERS))
    pull = jnp.broadcast_to(pull[..., None], (ROWS, COLS, MEMBERS))

    state = forecast(et, sides, top, bottom, corner_t, corner_b, depth, row_in, masks)
    total = sum_everywhere(gram_of(state, weight, pull))
    gram = total[:MEMBERS] + (MEMBERS - 1) * jnp.eye(MEMBERS, dtype=F32)
    return analyse(state, make_transform(gram, total[MEMBERS]))


def solution(mesh):
    in_specs = (
        P(None, None, None, "gx", "gy"),
        P(None, "gx", "gy"),
        P("gx", "gy", None),
        P("gx", "gy", None, None),
        P("gx", "gy", None, None),
        P("gx", "gy", None, None),
    )
    out_specs = P(None, None, None, "gx", "gy")
    return jax.shard_map(
        on_device, mesh=mesh, in_specs=in_specs, out_specs=out_specs, check_vma=False
    )
```

time: 243 us -> 190 us (0.78)
  Pallas kernels: 118 us -> 76 us
  waiting for transfers between devices: 39.7 us -> 16.9 us
  local copies, waits for them, and re-layouts: 18.2 us -> 27.8 us
  other arithmetic: 29.1 us -> 32.7 us
    pallas_call x7 -> x6, Pallas kernels: 118 us -> 76 us  [the longest x1 34.5 us: forecast(): pl.pallas_call(forecast_kernel, in_specs=[anywhere] * 6 + [vmem, pl.Block...]
    ppermute x10, waiting for transfers between devices: 23.2 us -> 5.6 us  [shift(): return lax.ppermute(x, axis, [(i, (i + by) % n) for i in range(n)])]
    ppermute x3, waiting for transfers between devices: 4.35 us -> 0.01 us  [observed_cells(): lax.ppermute(send, 'gy', [(i, i ^ bit) for i in range(tiles)])]
    unnamed x22 -> x32, local copies, waits for them, and re-layouts: 1.12 us -> 4.74 us
  transfers between devices with their start and end apart: 23 -> 23, of which waited for: 13 -> 10; matrix products, arithmetic and copies ran while one was open for 6% -> 12% of each run, Pallas kernels for 0% -> 10%
where the time goes in v2:
time: 190 us; the launch traced here: 189 us
  Pallas kernels  76 us (40%)
  other arithmetic  32.7 us (17%)
  starting transfers between devices  31.7 us (17%)
  local copies, waits for them, and re-layouts  27.8 us (15%)
  waiting for transfers between devices  16.9 us (9%)
  matrix products  3.56 us (2%)
    pallas_call x1, Pallas kernels, forecast(): pl.pallas_call(forecast_kernel, in_specs=[anywhere] * 6 + [vmem, pl.Block...  34.5 us
    pallas_call x3, Pallas kernels, to_lanes(): pl.pallas_call(kernel, grid=(layers, parts), in_specs=[pl.BlockSpec((1, 1...  19.6 us
    ppermute x10, starting transfers between devices, shift(): return lax.ppermute(x, axis, [(i, (i + by) % n) for i in range(n)])  18.8 us
    pallas_call x1, Pallas kernels, analyse(): pl.pallas_call(analysis_kernel, grid=(LAYERS, 3), in_specs=[pl.BlockSpec(...  14.2 us
    another operation x3, other arithmetic, make_transform(): lower = jnp.linalg.cholesky(gram)  12.4 us
    ppermute x10, waiting for transfers between devices, other(): lax.ppermute(x, axis, [(i, i ^ k) for i in range(lax.axis_size(axis))])  11.3 us
    ppermute x10, starting transfers between devices, other(): lax.ppermute(x, axis, [(i, i ^ k) for i in range(lax.axis_size(axis))])  10.7 us
    another operation x2, other arithmetic, make_transform(): lax.linalg.triangular_solve(lower, eye, left_side=True, lower=True)  10.5 us
  transfers between devices with their start and end apart: 23, of which 10 were waited for; matrix products, arithmetic and copies ran while one was open for 12% of the time, Pallas kernels for 10%

profile of v2, /device:TPU:0, one launch (start us, length us, event | category | flops | bytes accessed | tf_op | source)
XLA Modules:
  0.0 188.9 jit_solution(11619586717517852465)
XLA Ops:
  0.0 3.8 %fusion.39 = (bf16[2,3,128,8,128]{4,3,2,1,0:T(8,128)(2,1)}, bf16[2,3,128,8,128]{4,3,2,1,0:T(8,128)(2,1)}) fusion(bf16[2,3,128,32,128]{4,3,2,1,0:T(8,128)(2,1)} %e_ref.1), kind=kLoop, calls=%fused_computation.96 | loop fusion | bytes 6291456 | tf_op jit(solution)/shard_map/slice | solution.py:356
  5.5 4.9 %collective-permute-start.3 = (bf16[2,3,128,8,128]{4,3,2,1,0:T(8,128)(2,1)}, bf16[2,3,128,8,128]{4,3,2,1,0:T(8,128)(2,1)S(1)}, u32[]{:S(2)}, u32[]{:S(2)}) collective-permute-start(bf16[2,3,128,8,128]{4,3,2,1,0:T(8,128)(2,1)} %get-tuple-element.5), channel_id=1, source_target_pairs={{0,120},{8,0},{16,8},{24,16},{32,24},{40,32},{48,40},{56,48},{64,5... | collective-permute-start | bytes 4718600 | tf_op jit(solution)/shard_map/ppermute | solution.py:34
  11.1 1.9 %collective-permute-start.7 = (f32[2,32,8]{2,1,0:T(8,128)}, f32[2,32,8]{2,1,0:T(8,128)}, u32[]{:S(2)}, u32[]{:S(2)}) collective-permute-start(f32[2,32,8]{2,1,0:T(8,128)} %get-tuple-element.25), channel_id=1, source_target_pairs={{0,7},{1,0},{2,1},{3,2},{4,3},{5,4},{6,5},{7,6},{8,15},{9,8},{10,9... | collective-permute-start | bytes 6152 | tf_op jit(solution)/shard_map/ppermute | solution.py:34
  14.4 3.0 %fusion.8 = f32[6,256,128]{1,2,0:T(8,128)S(1)} fusion(s32[4096]{0:T(1024)S(1)} %get-tuple-element.30, pred[4096,128]{0,1:T(8,128)(4,1)} %iota_compare_fusion.1, bf16[6,4096]{1,0:T(8,128)(2,1)S(1)} %bitcast.97), kind=kOutput, calls=%fused_computation.9 | convolution fusion | flops 1614807040 | bytes 1376256 | tf_op jit(solution)/shard_map/rk,pkc->prc/dot_general | solution.py:316
  21.5 9.2 %to_lanes_32.1.et = bf16[2,3,32,128,128]{4,3,2,1,0:T(8,128)(2,1)} custom-call(bf16[2,3,128,32,128]{4,3,2,1,0:T(8,128)(2,1)} %e_ref.1), custom_call_target="tpu_custom_call" | custom-call | tf_op jit(solution)/shard_map/to_lanes_32/pallas_call | solution.py:55
  30.8 2.1 %fusion.40 = (bf16[2,3,32,8,128]{4,3,2,1,0:T(8,128)(2,1)}, bf16[2,3,32,8,128]{4,3,2,1,0:T(8,128)(2,1)}) fusion(bf16[2,3,32,128,128]{4,3,2,1,0:T(8,128)(2,1)} %to_lanes_32.1.et), kind=kLoop, calls=%fused_computation.97 | loop fusion | bytes 1572864 | tf_op jit(solution)/shard_map/slice | solution.py:359
  35.0 2.1 %collective-permute-start.9 = (f32[2,8,144]{2,1,0:T(8,128)S(1)}, f32[2,8,144]{2,1,0:T(8,128)S(1)}, u32[]{:S(2)}, u32[]{:S(2)}) collective-permute-start(f32[2,8,144]{2,1,0:T(8,128)S(1)} %get-tuple-element.18), channel_id=1, source_target_pairs={{0,120},{8,0},{16,8},{24,16},{32,24},{40,32},{48,40},{56,48},{64,5... | collective-permute-start | bytes 27656 | tf_op jit(solution)/shard_map/ppermute | solution.py:34
  40.4 4.2 %collective-permute-done.9 = f32[2,8,144]{2,1,0:T(8,128)S(1)} collective-permute-done((f32[2,8,144]{2,1,0:T(8,128)S(1)}, f32[2,8,144]{2,1,0:T(8,128)S(1)}, u32[]{:S(2)}, u32[]{:S(2)}) %collective-permute-start.9) | collective-permute-done | bytes 9248 | tf_op jit(solution)/shard_map/ppermute | solution.py:34
  45.3 2.4 %collective-permute-start.1 = (bf16[2,3,32,8,128]{4,3,2,1,0:T(8,128)(2,1)}, bf16[2,3,32,8,128]{4,3,2,1,0:T(8,128)(2,1)}, u32[]{:S(2)}, u32[]{:S(2)}) collective-permute-start(bf16[2,3,32,8,128]{4,3,2,1,0:T(8,128)(2,1)} %get-tuple-element.7), channel_id=1, source_target_pairs={{0,7},{1,0},{2,1},{3,2},{4,3},{5,4},{6,5},{7,6},{8,15},{9,8},{10,9... | collective-permute-start | bytes 1179656 | tf_op jit(solution)/shard_map/ppermute | solution.py:34
  56.4 5.8 %collective-permute-start.5 = (bf16[2,3,8,16,128]{4,3,2,1,0:T(8,128)(2,1)}, bf16[2,3,8,16,128]{4,3,2,1,0:T(8,128)(2,1)}, u32[]{:S(2)}, u32[]{:S(2)}) collective-permute-start(bf16[2,3,8,16,128]{4,3,2,1,0:T(8,128)(2,1)} %get-tuple-element.11), channel_id=1, source_target_pairs={{0,120},{8,0},{16,8},{24,16},{32,24},{40,32},{48,40},{56,48},{64,5... | collective-permute-start | bytes 589832 | tf_op jit(solution)/shard_map/ppermute | solution.py:34
  63.9 5.2 %to_lanes_8.2.top = bf16[2,3,8,128,128]{4,3,2,1,0:T(8,128)(2,1)} custom-call(bf16[2,3,128,8,128]{4,3,2,1,0:T(8,128)(2,1)} %copy-done.2), custom_call_target="tpu_custom_call" | custom-call | tf_op jit(solution)/shard_map/to_lanes_8/pallas_call | solution.py:55
  70.4 5.2 %to_lanes_8.3.bottom = bf16[2,3,8,128,128]{4,3,2,1,0:T(8,128)(2,1)} custom-call(bf16[2,3,128,8,128]{4,3,2,1,0:T(8,128)(2,1)} %copy-done.1), custom_call_target="tpu_custom_call" | custom-call | tf_op jit(solution)/shard_map/to_lanes_8/pallas_call | solution.py:55
  75.6 4.7 %broadcast_in_dim.68.depth = bf16[2,48,9,16,128]{4,3,2,1,0:T(8,128)(2,1)} broadcast(bf16[2,48,9,16]{3,2,1,0:T(8,128)(2,1)} %copy.15), dimensions={0,1,2,3} | broadcast | bytes 3566592 | tf_op jit(solution)/shard_map/broadcast_in_dim | solution.py:377
  81.1 34.5 %forecast.1.heights.state = bf16[2,3,32,128,128]{4,3,2,1,0:T(8,128)(2,1)} custom-call(bf16[2,3,32,128,128]{4,3,2,1,0:T(8,128)(2,1)} %to_lanes_32.1.et, bf16[2,3,32,16,128]{4,3,2,1,0:T(8,128)(2,1)} %copy-done, bf16[2,3,8,128,128]{4,3,2,1,0:T(8,128)(2,1)} %to_lanes_8.2.top, bf16[2,3,8,128,128]{4,3,2,1,0:T(8,128)(2,1)} %to_lanes_8.3.bottom, ...), custom_call_target="tpu_custom_call" | custom-call | tf_op jit(solution)/shard_map/forecast/pallas_call | solution.py:194
  115.6 1.9 %broadcast_in_dim.75.weight = f32[32,128,128]{2,1,0:T(8,128)} broadcast(f32[32,128]{1,0:T(8,128)S(1)} %copy-done.9), dimensions={0,1} | broadcast | bytes 2113536 | tf_op jit(solution)/shard_map/broadcast_in_dim | solution.py:384
  117.5 2.0 %broadcast_in_dim.77.pull = f32[32,128,128]{2,1,0:T(8,128)} broadcast(f32[32,128]{1,0:T(8,128)S(1)} %copy-done.8), dimensions={0,1} | broadcast | bytes 2113536 | tf_op jit(solution)/shard_map/broadcast_in_dim | solution.py:385
  119.5 7.6 %gram.1 = f32[136,128]{1,0:T(8,128)} custom-call(bf16[2,3,32,128,128]{4,3,2,1,0:T(8,128)(2,1)} %forecast.1.heights.state, f32[32,128,128]{2,1,0:T(8,128)} %broadcast_in_dim.75.weight, f32[32,128,128]{2,1,0:T(8,128)} %broadcast_in_dim.77.pull), custom_call_target="tpu_custom_call" | custom-call | tf_op jit(solution)/shard_map/gram/pallas_call | solution.py:240
  133.1 2.4 %collective-permute-done.15 = f32[136,128]{1,0:T(8,128)S(1)} collective-permute-done((f32[136,128]{1,0:T(8,128)S(1)}, f32[136,128]{1,0:T(8,128)S(1)}, u32[]{:S(2)}, u32[]{:S(2)}) %collective-permute-start.15) | collective-permute-done | bytes 69664 | tf_op jit(solution)/shard_map/ppermute | solution.py:333
  137.1 3.4 %collective-permute-start.17 = (f32[136,128]{1,0:T(8,128)S(1)}, f32[136,128]{1,0:T(8,128)S(1)}, u32[]{:S(2)}, u32[]{:S(2)}) collective-permute-start(f32[136,128]{1,0:T(8,128)S(1)} %add_add_fusion.2), channel_id=1, source_target_pairs={{0,8},{8,0},{16,24},{24,16},{32,40},{40,32},{48,56},{56,48},{64,72... | collective-permute-start | bytes 208904 | tf_op jit(solution)/shard_map/ppermute | solution.py:333
  140.5 2.4 %collective-permute-done.18 = f32[136,128]{1,0:T(8,128)S(1)} collective-permute-done((f32[136,128]{1,0:T(8,128)S(1)}, f32[136,128]{1,0:T(8,128)S(1)}, u32[]{:S(2)}, u32[]{:S(2)}) %collective-permute-start.18) | collective-permute-done | bytes 69664 | tf_op jit(solution)/shard_map/ppermute | solution.py:333
  147.0 2.3 %collective-permute-done.21 = f32[136,128]{1,0:T(8,128)S(1)} collective-permute-done((f32[136,128]{1,0:T(8,128)S(1)}, f32[136,128]{1,0:T(8,128)S(1)}, u32[]{:S(2)}, u32[]{:S(2)}) %collective-permute-start.21) | collective-permute-done | bytes 69664 | tf_op jit(solution)/shard_map/ppermute | solution.py:333
  150.2 11.7 %cholesky.17 = f32[128,128]{1,0:T(8,128)S(1)} custom-call(f32[128,128]{1,0:T(8,128)S(1)} %fusion.22), custom_call_target="Cholesky" | custom-call | tf_op jit(solution)/shard_map/jit(cholesky)/cholesky | solution.py:343
  163.3 9.8 %custom-call.6 = f32[1,128,128]{1,2,0:T(8,128)S(1)} custom-call(f32[1,128,128]{2,1,0:T(8,128)S(1)} %fusion.17), custom_call_target="InvertDiagBlocksLowerTriangular" | custom-call | tf_op jit(solution)/shard_map/triangular_solve | solution.py:344
  174.7 14.2 %analysis.1 = bf16[2,3,128,32,128]{4,3,2,1,0:T(8,128)(2,1)} custom-call(bf16[2,3,32,128,128]{4,3,2,1,0:T(8,128)(2,1)} %forecast.1.heights.state, bf16[128,256]{1,0:T(8,128)(2,1)} %pad_maximum_fusion.2.mix), custom_call_target="tpu_custom_call" | custom-call | tf_op jit(solution)/shard_map/analysis/pallas_call | solution.py:284
  (120 shorter events, 41.7 us)
Async XLA Ops:
  3.8 59.0 %collective-permute-start.2 = (bf16[2,3,128,8,128]{4,3,2,1,0:T(8,128)(2,1)}, bf16[2,3,128,8,128]{4,3,2,1,0:T(8,128)(2,1)S(1)}, u32[]{:S(2)}, u32[]{:S(2)}) collective-permute-start(bf16[2,3,128,8,128]{4,3,2,1,0:T(8,128)(2,1)} %get-tuple-element.6), channel_id=1, source_target_pairs={{0,8},{8,16},{16,24},{24,32},{32,40},{40,48},{48,56},{56,64},{64,7... | collective-permute-start | bytes 4718600 | tf_op jit(solution)/shard_map/ppermute | solution.py:34
  5.5 63.7 %collective-permute-start.3 = (bf16[2,3,128,8,128]{4,3,2,1,0:T(8,128)(2,1)}, bf16[2,3,128,8,128]{4,3,2,1,0:T(8,128)(2,1)S(1)}, u32[]{:S(2)}, u32[]{:S(2)}) collective-permute-start(bf16[2,3,128,8,128]{4,3,2,1,0:T(8,128)(2,1)} %get-tuple-element.5), channel_id=1, source_target_pairs={{0,120},{8,0},{16,8},{24,16},{32,24},{40,32},{48,40},{56,48},{64,5... | collective-permute-start | bytes 4718600 | tf_op jit(solution)/shard_map/ppermute | solution.py:34
  11.1 23.1 %collective-permute-start.7 = (f32[2,32,8]{2,1,0:T(8,128)}, f32[2,32,8]{2,1,0:T(8,128)}, u32[]{:S(2)}, u32[]{:S(2)}) collective-permute-start(f32[2,32,8]{2,1,0:T(8,128)} %get-tuple-element.25), channel_id=1, source_target_pairs={{0,7},{1,0},{2,1},{3,2},{4,3},{5,4},{6,5},{7,6},{8,15},{9,8},{10,9... | collective-permute-start | bytes 6152 | tf_op jit(solution)/shard_map/ppermute | solution.py:34
  13.0 21.2 %collective-permute-start.6 = (f32[2,32,8]{2,1,0:T(8,128)}, f32[2,32,8]{2,1,0:T(8,128)}, u32[]{:S(2)}, u32[]{:S(2)}) collective-permute-start(f32[2,32,8]{2,1,0:T(8,128)} %get-tuple-element.24), channel_id=1, source_target_pairs={{0,1},{1,2},{2,3},{3,4},{4,5},{5,6},{6,7},{7,0},{8,9},{9,10},{10,1... | collective-permute-start | bytes 6152 | tf_op jit(solution)/shard_map/ppermute | solution.py:34
  19.9 17.2 %collective-permute-start.10 = (f32[4,2,32,128]{3,2,1,0:T(8,128)}, f32[4,2,32,128]{3,2,1,0:T(8,128)S(1)}, u32[]{:S(2)}, u32[]{:S(2)}) collective-permute-start(f32[4,2,32,128]{3,2,1,0:T(8,128)} %bitcast.88), channel_id=1, source_target_pairs={{0,4},{1,5},{2,6},{3,7},{4,0},{5,1},{6,2},{7,3},{8,12},{9,13},{10,... | collective-permute-start | bytes 393224 | tf_op jit(solution)/shard_map/ppermute | solution.py:326
  35.0 9.5 %collective-permute-start.9 = (f32[2,8,144]{2,1,0:T(8,128)S(1)}, f32[2,8,144]{2,1,0:T(8,128)S(1)}, u32[]{:S(2)}, u32[]{:S(2)}) collective-permute-start(f32[2,8,144]{2,1,0:T(8,128)S(1)} %get-tuple-element.18), channel_id=1, source_target_pairs={{0,120},{8,0},{16,8},{24,16},{32,24},{40,32},{48,40},{56,48},{64,5... | collective-permute-start | bytes 27656 | tf_op jit(solution)/shard_map/ppermute | solution.py:34
  37.1 8.2 %collective-permute-start.8 = (f32[2,8,144]{2,1,0:T(8,128)S(1)}, f32[2,8,144]{2,1,0:T(8,128)S(1)}, u32[]{:S(2)}, u32[]{:S(2)}) collective-permute-start(f32[2,8,144]{2,1,0:T(8,128)S(1)} %get-tuple-element.17), channel_id=1, source_target_pairs={{0,8},{8,16},{16,24},{24,32},{32,40},{40,48},{48,56},{56,64},{64,7... | collective-permute-start | bytes 27656 | tf_op jit(solution)/shard_map/ppermute | solution.py:34
  38.4 9.4 %collective-permute-start.11 = (f32[2,2,32,128]{3,2,1,0:T(8,128)}, f32[2,2,32,128]{3,2,1,0:T(8,128)S(1)}, u32[]{:S(2)}, u32[]{:S(2)}) collective-permute-start(f32[2,2,32,128]{3,2,1,0:T(8,128)} %dynamic-slice_bitcast_fusion), channel_id=1, source_target_pairs={{0,2},{1,3},{2,0},{3,1},{4,6},{5,7},{6,4},{7,5},{8,10},{9,11},{10,... | collective-permute-start | bytes 196616 | tf_op jit(solution)/shard_map/ppermute | solution.py:326
  44.6 8.7 %collective-permute-start = (bf16[2,3,32,8,128]{4,3,2,1,0:T(8,128)(2,1)}, bf16[2,3,32,8,128]{4,3,2,1,0:T(8,128)(2,1)}, u32[]{:S(2)}, u32[]{:S(2)}) collective-permute-start(bf16[2,3,32,8,128]{4,3,2,1,0:T(8,128)(2,1)} %get-tuple-element.8), channel_id=1, source_target_pairs={{0,1},{1,2},{2,3},{3,4},{4,5},{5,6},{6,7},{7,0},{8,9},{9,10},{10,1... | collective-permute-start | bytes 1179656 | tf_op jit(solution)/shard_map/ppermute | solution.py:34
  45.3 9.1 %collective-permute-start.1 = (bf16[2,3,32,8,128]{4,3,2,1,0:T(8,128)(2,1)}, bf16[2,3,32,8,128]{4,3,2,1,0:T(8,128)(2,1)}, u32[]{:S(2)}, u32[]{:S(2)}) collective-permute-start(bf16[2,3,32,8,128]{4,3,2,1,0:T(8,128)(2,1)} %get-tuple-element.7), channel_id=1, source_target_pairs={{0,7},{1,0},{2,1},{3,2},{4,3},{5,4},{6,5},{7,6},{8,15},{9,8},{10,9... | collective-permute-start | bytes 1179656 | tf_op jit(solution)/shard_map/ppermute | solution.py:34
  49.4 2.4 %collective-permute-start.12 = (f32[1,2,32,128]{3,2,1,0:T(8,128)}, f32[1,2,32,128]{3,2,1,0:T(8,128)S(1)}, u32[]{:S(2)}, u32[]{:S(2)}) collective-permute-start(f32[1,2,32,128]{3,2,1,0:T(8,128)} %constant_dynamic-slice_fusion), channel_id=1, source_target_pairs={{0,1},{1,0},{2,3},{3,2},{4,5},{5,4},{6,7},{7,6},{8,9},{9,8},{10,11... | collective-permute-start | bytes 98312 | tf_op jit(solution)/shard_map/ppermute | solution.py:326
  56.3 19.2 %collective-permute-start.4 = (bf16[2,3,8,16,128]{4,3,2,1,0:T(8,128)(2,1)}, bf16[2,3,8,16,128]{4,3,2,1,0:T(8,128)(2,1)S(1)}, u32[]{:S(2)}, u32[]{:S(2)}) collective-permute-start(bf16[2,3,8,16,128]{4,3,2,1,0:T(8,128)(2,1)} %get-tuple-element.12), channel_id=1, source_target_pairs={{0,8},{8,16},{16,24},{24,32},{32,40},{40,48},{48,56},{56,64},{64,7... | collective-permute-start | bytes 589832 | tf_op jit(solution)/shard_map/ppermute | solution.py:34
  56.4 19.2 %collective-permute-start.5 = (bf16[2,3,8,16,128]{4,3,2,1,0:T(8,128)(2,1)}, bf16[2,3,8,16,128]{4,3,2,1,0:T(8,128)(2,1)}, u32[]{:S(2)}, u32[]{:S(2)}) collective-permute-start(bf16[2,3,8,16,128]{4,3,2,1,0:T(8,128)(2,1)} %get-tuple-element.11), channel_id=1, source_target_pairs={{0,120},{8,0},{16,8},{24,16},{32,24},{40,32},{48,40},{56,48},{64,5... | collective-permute-start | bytes 589832 | tf_op jit(solution)/shard_map/ppermute | solution.py:34
  81.1 36.4 %copy-start.8 = (f32[32,128]{1,0:T(8,128)S(1)}, f32[32,128]{1,0:T(8,128)}, u32[]{:S(2)}) copy-start(f32[32,128]{1,0:T(8,128)} %get-tuple-element.19) | copy-start | bytes 49156
  127.1 1.5 collective-permute-start.13
  129.5 5.9 %collective-permute-start.15 = (f32[136,128]{1,0:T(8,128)S(1)}, f32[136,128]{1,0:T(8,128)S(1)}, u32[]{:S(2)}, u32[]{:S(2)}) collective-permute-start(f32[136,128]{1,0:T(8,128)S(1)} %add.232), channel_id=1, source_target_pairs={{0,4},{1,5},{2,6},{3,7},{4,0},{5,1},{6,2},{7,3},{8,12},{9,13},{10,... | collective-permute-start | bytes 208904 | tf_op jit(solution)/shard_map/ppermute | solution.py:333
  131.4 5.5 %collective-permute-start.16 = (f32[136,128]{1,0:T(8,128)S(1)}, f32[136,128]{1,0:T(8,128)S(1)}, u32[]{:S(2)}, u32[]{:S(2)}) collective-permute-start(f32[136,128]{1,0:T(8,128)S(1)} %add.232), channel_id=1, source_target_pairs={{0,6},{1,7},{2,4},{3,5},{4,2},{5,3},{6,0},{7,1},{8,14},{9,15},{10,... | collective-permute-start | bytes 208904 | tf_op jit(solution)/shard_map/ppermute | solution.py:333
  132.6 4.3 %collective-permute-start.14 = (f32[136,128]{1,0:T(8,128)S(1)}, f32[136,128]{1,0:T(8,128)S(1)}, u32[]{:S(2)}, u32[]{:S(2)}) collective-permute-start(f32[136,128]{1,0:T(8,128)S(1)} %add.232), channel_id=1, source_target_pairs={{0,2},{1,3},{2,0},{3,1},{4,6},{5,7},{6,4},{7,5},{8,10},{9,11},{10,... | collective-permute-start | bytes 208904 | tf_op jit(solution)/shard_map/ppermute | solution.py:333
  136.9 6.0 %collective-permute-start.18 = (f32[136,128]{1,0:T(8,128)S(1)}, f32[136,128]{1,0:T(8,128)S(1)}, u32[]{:S(2)}, u32[]{:S(2)}) collective-permute-start(f32[136,128]{1,0:T(8,128)S(1)} %add_add_fusion.2), channel_id=1, source_target_pairs={{0,16},{8,24},{16,0},{24,8},{32,48},{40,56},{48,32},{56,40},{64,80... | collective-permute-start | bytes 208904 | tf_op jit(solution)/shard_map/ppermute | solution.py:333
  137.0 6.3 %collective-permute-start.19 = (f32[136,128]{1,0:T(8,128)S(1)}, f32[136,128]{1,0:T(8,128)S(1)}, u32[]{:S(2)}, u32[]{:S(2)}) collective-permute-start(f32[136,128]{1,0:T(8,128)S(1)} %add_add_fusion.2), channel_id=1, source_target_pairs={{0,24},{8,16},{16,8},{24,0},{32,56},{40,48},{48,40},{56,32},{64,88... | collective-permute-start | bytes 208904 | tf_op jit(solution)/shard_map/ppermute | solution.py:333
  137.1 6.3 %collective-permute-start.17 = (f32[136,128]{1,0:T(8,128)S(1)}, f32[136,128]{1,0:T(8,128)S(1)}, u32[]{:S(2)}, u32[]{:S(2)}) collective-permute-start(f32[136,128]{1,0:T(8,128)S(1)} %add_add_fusion.2), channel_id=1, source_target_pairs={{0,8},{8,0},{16,24},{24,16},{32,40},{40,32},{48,56},{56,48},{64,72... | collective-permute-start | bytes 208904 | tf_op jit(solution)/shard_map/ppermute | solution.py:333
  143.4 5.9 %collective-permute-start.21 = (f32[136,128]{1,0:T(8,128)S(1)}, f32[136,128]{1,0:T(8,128)S(1)}, u32[]{:S(2)}, u32[]{:S(2)}) collective-permute-start(f32[136,128]{1,0:T(8,128)S(1)} %add_add_fusion.1), channel_id=1, source_target_pairs={{0,64},{8,72},{16,80},{24,88},{32,96},{40,104},{48,112},{56,120},{... | collective-permute-start | bytes 208904 | tf_op jit(solution)/shard_map/ppermute | solution.py:333
  144.3 5.7 %collective-permute-start.22 = (f32[136,128]{1,0:T(8,128)S(1)}, f32[136,128]{1,0:T(8,128)S(1)}, u32[]{:S(2)}, u32[]{:S(2)}) collective-permute-start(f32[136,128]{1,0:T(8,128)S(1)} %add_add_fusion.1), channel_id=1, source_target_pairs={{0,96},{8,104},{16,112},{24,120},{32,64},{40,72},{48,80},{56,88},{... | collective-permute-start | bytes 208904 | tf_op jit(solution)/shard_map/ppermute | solution.py:333
  145.3 4.7 %collective-permute-start.20 = (f32[136,128]{1,0:T(8,128)S(1)}, f32[136,128]{1,0:T(8,128)S(1)}, u32[]{:S(2)}, u32[]{:S(2)}) collective-permute-start(f32[136,128]{1,0:T(8,128)S(1)} %add_add_fusion.1), channel_id=1, source_target_pairs={{0,32},{8,40},{16,48},{24,56},{32,0},{40,8},{48,16},{56,24},{64,96... | collective-permute-start | bytes 208904 | tf_op jit(solution)/shard_map/ppermute | solution.py:333
  (14 other events, 153.8 us)

commit v3 on v2

v3 whole, which is shorter than its diff:
```python
import jax
import jax.numpy as jnp
from jax import lax
from jax.experimental import pallas as pl
from jax.experimental.pallas import tpu as pltpu
from jax.sharding import PartitionSpec as P

MEMBERS = 128
ROWS = 32
COLS = 128
HALO = 8
STEPS = 4
WIDE_ROWS = ROWS + 2 * HALO
WIDE_COLS = COLS + 2 * HALO
SEGMENTS = 16
POSITIONS = WIDE_COLS // SEGMENTS
LINE = 40
PANEL = 8
LAYERS = 2
HALF = 0.15
TURN = 0.12
COUPLING = 0.5
VMEM = 60 * 1024 * 1024

F32 = jnp.float32
BF16 = jnp.bfloat16


COST = pl.CostEstimate(flops=1, bytes_accessed=1, transcendentals=0)


def params():
    return pltpu.CompilerParams(vmem_limit_bytes=VMEM)


def shift(x, axis, by):
    n = lax.axis_size(axis)
    return lax.ppermute(x, axis, [(i, (i + by) % n) for i in range(n)])


def turn_rows(e_ref, planes, rows, put):
    pitch = ROWS + 1
    tiles = sorted({x // 8 * 8 for x in rows})

    def spread(m, carry):
        for k in range(4):
            plane = e_ref[0, 0, 4 * m + k].astype(F32)
            for lo in tiles:
                planes[pl.ds((4 * m + k) * pitch + lo, 8), :] = plane[lo:lo + 8]
        return carry

    lax.fori_loop(0, MEMBERS // 4, spread, 0, unroll=2)
    for x in rows:
        put(x, planes[pl.ds(x, MEMBERS, stride=pitch), :].astype(BF16).T)


E_BLOCK = pl.BlockSpec((1, 1, MEMBERS, ROWS, COLS), lambda i, j: (i, j, 0, 0, 0))
FAR = 3 * HALO - 2


def edge_rows(ensemble):
    def kernel(e_ref, north, south, planes):
        part = pl.program_id(1)
        base = pl.program_id(0) * FAR + part * (HALO - 1) + (part > 0)

        def put(x, value):
            if x < HALO - 1:
                north[base + x] = value
            elif x > ROWS - HALO:
                south[base + (x - (ROWS - HALO)) - (part > 0)] = value
            else:

                @pl.when(part == 0)
                def _():
                    if x < HALO:
                        north[base + x] = value
                    else:
                        south[base] = value

        rows = list(range(HALO)) + list(range(ROWS - HALO, ROWS))
        turn_rows(e_ref, planes, rows, put)

    whole = pl.BlockSpec((LAYERS * FAR, COLS, MEMBERS), lambda i, j: (0, 0, 0))
    shape = jax.ShapeDtypeStruct((LAYERS * FAR, COLS, MEMBERS), BF16)
    return pl.pallas_call(
        kernel,
        grid=(LAYERS, 3),
        in_specs=[E_BLOCK],
        out_specs=[whole, whole],
        out_shape=[shape, shape],
        scratch_shapes=[pltpu.VMEM((MEMBERS * (ROWS + 1), COLS), F32)],
        compiler_params=params(),
        cost_estimate=COST,
        name="edge_rows",
    )(ensemble)


def all_rows(ensemble, after):
    def kernel(e_ref, after_ref, own, left, right, planes):
        held = {}

        def put(x, value):
            own[0, 0, x] = value
            if x % 2:
                other = held.pop(x - 1)
                left[0, 0, x // 2] = jnp.concatenate([other[:HALO], value[:HALO]], axis=0)
                right[0, 0, x // 2] = jnp.concatenate(
                    [other[COLS - HALO:], value[COLS - HALO:]], axis=0
                )
            else:
                held[x] = value

        turn_rows(e_ref, planes, list(range(ROWS)), put)

    def whole(block):
        return jax.ShapeDtypeStruct((LAYERS, 3) + block[2:], BF16)

    def spec(block):
        return pl.BlockSpec(block, lambda i, j: (i, j, 0, 0, 0))

    tile = (1, 1, ROWS, COLS, MEMBERS)
    side = (1, 1, ROWS // 2, 16, MEMBERS)
    return pl.pallas_call(
        kernel,
        grid=(LAYERS, 3),
        in_specs=[E_BLOCK, pl.BlockSpec(memory_space=pl.ANY)],
        out_specs=[spec(tile), spec(side), spec(side)],
        out_shape=[whole(tile), whole(side), whole(side)],
        scratch_shapes=[pltpu.VMEM((MEMBERS * (ROWS + 1), COLS), F32)],
        compiler_params=params(),
        cost_estimate=COST,
        name="all_rows",
    )(ensemble, after)


def forecast_kernel(
    own, top, bottom, left, right, corner_t, corner_b, depth_in, row_in, masks,
    out, raw, raw_side, depth, st, fx, fy, pr, line, sems,
):
    depth_copy = pltpu.make_async_copy(depth_in, depth, sems.at[54])
    depth_copy.start()
    order = [(l, c) for l in range(LAYERS) for c in range(3)]
    copies = {}
    for l, c in order:
        count = HALO - (c > 0)
        at = pl.ds(l * FAR + c * (HALO - 1) + (c > 0), count)
        rows = [
            (own.at[l, c], raw.at[l, c, pl.ds(HALO, ROWS)]),
            (top.at[at], raw.at[l, c, pl.ds(HALO - count, count)]),
            (bottom.at[at], raw.at[l, c, pl.ds(HALO + ROWS, count)]),
        ]
        for k, piece in enumerate((left, right)):
            rows.append((piece.at[l, c], raw_side.at[k, l, c, pl.ds(4, 16)]))
            rows.append((corner_t.at[k, l, c], raw_side.at[k, l, c, pl.ds(0, 4)]))
            rows.append((corner_b.at[k, l, c], raw_side.at[k, l, c, pl.ds(20, 4)]))
        copies[l, c] = [
            pltpu.make_async_copy(x, y, sems.at[(3 * l + c) * 9 + k])
            for k, (x, y) in enumerate(rows)
        ]
    for key in order:
        for c in copies[key]:
            c.start()
    depth_copy.wait()

    def rolled(x, by):
        return pltpu.roll(x.astype(F32), by % SEGMENTS, 0).astype(BF16)

    def put_flux(l, r, flux):
        fy[l, r, 1:POSITIONS + 1] = flux
        fy[l, r, 0] = rolled(flux[POSITIONS - 1], 1)
        fy[l, r, POSITIONS + 1] = rolled(flux[0], -1)

    def put_pressure(l, r, value):
        pr[l, r, 1:POSITIONS + 1] = value
        pr[l, r, 0] = rolled(value[POSITIONS - 1], 1)
        pr[l, r, POSITIONS + 1] = rolled(value[0], -1)

    for l, c in order:
        for d in copies[l, c]:
            d.wait()

        def unpack(pair, carry):
            scale = HALF if c == 2 else 1.0
            sides = [raw_side[k, l, c, pair].astype(F32) * scale for k in range(2)]
            for odd in range(2):
                r = 2 * pair + odd
                base = lax.rem(pair, 2) * (8 * LINE) + odd * (4 * LINE)
                half = slice(8 * odd, 8 * odd + 8)
                line[pl.ds(base, 8), :] = sides[0][half]
                line[pl.ds(base + 8, COLS), :] = raw[l, c, r].astype(F32) * scale
                line[pl.ds(base + 8 + COLS, 8), :] = sides[1][half]
                value = jnp.stack(
                    [
                        line[pl.ds(base + p, SEGMENTS, stride=POSITIONS), :].astype(BF16)
                        for p in range(POSITIONS)
                    ],
                    axis=0,
                )
                st[l, c, r] = value
                if c == 0:
                    fx[l, r] = depth[l, r] * value
                elif c == 1:
                    put_flux(l, r, depth[l, r] * value)
            return carry

        lax.fori_loop(0, WIDE_ROWS // 2, unpack, 0)

    mid = slice(1, POSITIONS + 1)

    def sweep(body, rows_from, rows_to, first):
        for start in (rows_from, rows_from + 1):
            lax.fori_loop(
                0,
                (rows_to - rows_from) // 2,
                lambda i, above, start=start: body(start + 2 * i, above),
                first(start),
                unroll=2,
            )

    for step in range(1, STEPS + 1):

        def thickness(r, above):
            new, below = [], []
            for l in range(LAYERS):
                nxt = fx[l, r + 1]
                g = fy[l, r]
                h = st[l, 2, r] - ((nxt - above[l]) + (g[2:] - g[:POSITIONS]))
                st[l, 2, r] = h
                new.append(h)
                below.append(nxt)
            mask = masks[row_in[0, r]]
            put_pressure(0, r, (new[0] + new[1]) * mask)
            put_pressure(1, r, (BF16(COUPLING) * new[0] + new[1]) * mask)
            return tuple(below)

        sweep(
            thickness, 2 * step - 1, WIDE_ROWS - (2 * step - 1),
            lambda r: tuple(fx[l, r - 1] for l in range(LAYERS)),
        )

        def velocity(r, above):
            below = []
            for l in range(LAYERS):
                u, v = st[l, 0, r], st[l, 1, r]
                nxt = pr[l, r + 1, mid]
                g = pr[l, r]
                u_new = (u + BF16(TURN) * v) - (nxt - above[l])
                v_new = (v - BF16(TURN) * u) - (g[2:] - g[:POSITIONS])
                st[l, 0, r] = u_new
                st[l, 1, r] = v_new
                if step < STEPS:
                    d = depth[l, r]
                    fx[l, r] = d * u_new
                    put_flux(l, r, d * v_new)
                below.append(nxt)
            return tuple(below)

        sweep(
            velocity, 2 * step, WIDE_ROWS - 2 * step,
            lambda r: tuple(pr[l, r - 1, mid] for l in range(LAYERS)),
        )

    done = []
    for l in range(LAYERS):
        for c in range(3):

            def pack(r, carry):
                base = lax.rem(r, 4) * (4 * LINE)
                for p in range(POSITIONS):
                    line[pl.ds(base + p, SEGMENTS, stride=POSITIONS), :] = st[
                        l, c, r + HALO, p
                    ].astype(F32)
                value = line[pl.ds(base + 8, COLS), :]
                if c == 2:
                    value = value * (1.0 / HALF)
                raw[l, c, r] = value.astype(BF16)
                return carry

            lax.fori_loop(0, ROWS, pack, 0, unroll=2)
            done.append(
                pltpu.make_async_copy(
                    raw.at[l, c, pl.ds(0, ROWS)], out.at[l, c], sems.at[55 + 3 * l + c]
                )
            )
            done[-1].start()
    for d in done:
        d.wait()


def forecast(*operands):
    plane = (LAYERS, WIDE_ROWS, POSITIONS, SEGMENTS, MEMBERS)
    padded = (LAYERS, WIDE_ROWS, POSITIONS + 2, SEGMENTS, MEMBERS)
    anywhere = pl.BlockSpec(memory_space=pl.ANY)
    vmem = pl.BlockSpec(memory_space=pltpu.VMEM)
    return pl.pallas_call(
        forecast_kernel,
        in_specs=[anywhere] * 8 + [pl.BlockSpec(memory_space=pltpu.SMEM), vmem],
        out_specs=anywhere,
        out_shape=jax.ShapeDtypeStruct((LAYERS, 3, ROWS, COLS, MEMBERS), BF16),
        scratch_shapes=[
            pltpu.VMEM((LAYERS, 3, WIDE_ROWS, COLS, MEMBERS), BF16),
            pltpu.VMEM((2, LAYERS, 3, WIDE_ROWS // 2, 16, MEMBERS), BF16),
            pltpu.VMEM(plane, BF16),
            pltpu.VMEM((LAYERS, 3) + plane[1:], BF16),
            pltpu.VMEM(plane, BF16),
            pltpu.VMEM(padded, BF16),
            pltpu.VMEM(padded, BF16),
            pltpu.VMEM((16 * LINE, MEMBERS), F32),
            pltpu.SemaphoreType.DMA((61,)),
        ],
        compiler_params=params(),
        cost_estimate=COST,
        name="forecast",
    )(*operands)


def gram_kernel(heights, weight, pull, out, left, right, acc):
    n = MEMBERS
    over_last = (((1,), (1,)), ((), ()))
    eye = lax.broadcasted_iota(jnp.int32, (n, n), 0) == lax.broadcasted_iota(jnp.int32, (n, n), 1)
    away = (eye.astype(F32) - 1.0 / n).astype(BF16)
    away = jnp.concatenate([away, away], axis=1)
    share = jnp.full((8, 2 * n), 1.0 / n, BF16)
    acc[...] = jnp.zeros_like(acc)

    def body(x, carry):
        both = jnp.concatenate([heights[0, 0, x], heights[1, 0, x]], axis=1)
        z = lax.dot_general(both, away, over_last, preferred_element_type=F32)
        zt = lax.dot_general(away, both, over_last, preferred_element_type=F32)
        mean = lax.dot_general(share, both, over_last, preferred_element_type=F32)[0:1]
        w = weight[pl.ds(x, 1), :]
        y = zt * w
        at = pl.ds(pl.multiple_of(x * COLS, COLS), COLS)
        y_high = y.astype(BF16)
        z_high = z.astype(BF16)
        left[0, x] = y_high
        left[1, x] = (y - y_high.astype(F32)).astype(BF16)
        right[x, :, 0:n] = z_high
        right[x, :, n:2 * n] = (z - z_high.astype(F32)).astype(BF16)
        acc[...] += zt * (pull[pl.ds(x, 1), :] - mean * w)
        return carry

    lax.fori_loop(0, ROWS, body, 0, unroll=2)

    def multiply(x, total):
        a = jnp.concatenate([left[0, 2 * x], left[0, 2 * x + 1]], axis=1)
        b = jnp.concatenate([left[1, 2 * x], left[1, 2 * x + 1]], axis=1)
        z = right[pl.ds(2 * x, 2)].reshape(2 * COLS, 2 * n)
        main = jnp.dot(a, z, preferred_element_type=F32)
        low = jnp.dot(b, z[:, 0:n], preferred_element_type=F32)
        return total + (main[:, 0:n] + (main[:, n:2 * n] + low))

    out[0:n, :] = lax.fori_loop(0, ROWS // 2, multiply, jnp.zeros((n, n), F32), unroll=2)
    out[n:n + 8, :] = jnp.broadcast_to(jnp.sum(acc[...].T, axis=0, keepdims=True), (8, n))


def gram_of(state, weight, pull):
    cells = pl.BlockSpec((ROWS, COLS), lambda i: (0, 0))
    return pl.pallas_call(
        gram_kernel,
        grid=(1,),
        in_specs=[
            pl.BlockSpec((LAYERS, 1, ROWS, COLS, MEMBERS), lambda i: (0, 2, 0, 0, 0)),
            cells,
            cells,
        ],
        out_specs=pl.BlockSpec((MEMBERS + 8, MEMBERS), lambda i: (0, 0)),
        out_shape=jax.ShapeDtypeStruct((MEMBERS + 8, MEMBERS), F32),
        scratch_shapes=[
            pltpu.VMEM((2, ROWS, MEMBERS, COLS), BF16),
            pltpu.VMEM((ROWS, COLS, 2 * MEMBERS), BF16),
            pltpu.VMEM((MEMBERS, COLS), F32),
        ],
        compiler_params=params(),
        cost_estimate=COST,
        name="gram",
    )(state, weight, pull)


def analysis_kernel(state, mix, out, planes):
    pitch = ROWS + 1
    over_last = (((1,), (1,)), ((), ()))
    both = mix[...]

    def body(x, carry):
        s = state[0, 0, pl.ds(2 * x, 2)].reshape(2 * COLS, MEMBERS)
        mixed = lax.dot_general(
            both, jnp.concatenate([s, s], axis=1), over_last, preferred_element_type=F32
        )
        planes[pl.ds(2 * x, MEMBERS, stride=pitch), :] = mixed[:, :COLS]
        planes[pl.ds(2 * x + 1, MEMBERS, stride=pitch), :] = mixed[:, COLS:]
        return carry

    lax.fori_loop(0, ROWS // 2, body, 0, unroll=2)

    def gather(m, carry):
        for k in range(4):
            out[0, 0, 4 * m + k] = planes[pl.ds((4 * m + k) * pitch, ROWS), :].astype(BF16)
        return carry

    lax.fori_loop(0, MEMBERS // 4, gather, 0, unroll=2)


def analyse(state, mix):
    return pl.pallas_call(
        analysis_kernel,
        grid=(LAYERS, 3),
        in_specs=[
            pl.BlockSpec((1, 1, ROWS, COLS, MEMBERS), lambda i, j: (i, j, 0, 0, 0)),
            pl.BlockSpec((MEMBERS, 2 * MEMBERS), lambda i, j: (0, 0)),
        ],
        out_specs=pl.BlockSpec((1, 1, MEMBERS, ROWS, COLS), lambda i, j: (i, j, 0, 0, 0)),
        out_shape=jax.ShapeDtypeStruct((LAYERS, 3, MEMBERS, ROWS, COLS), BF16),
        scratch_shapes=[pltpu.VMEM((MEMBERS * (ROWS + 1), COLS), F32)],
        compiler_params=params(),
        cost_estimate=COST,
        name="analysis",
    )(state, mix)


def split3(x):
    a = lax.reduce_precision(x, 8, 7)
    b = lax.reduce_precision(x - a, 8, 7)
    c = lax.reduce_precision(x - a - b, 8, 7)
    return [p.astype(BF16) for p in (a, b, c)]


def observed_cells(dest, cell, value, sigma):
    tiles = lax.axis_size("gy")
    inverse = 1.0 / sigma
    weight = inverse * inverse
    pieces = jnp.stack(split3(weight) + split3(value * weight), 0).reshape(6, -1)
    row = ((dest ^ lax.axis_index("gy"))[:, None] * ROWS + cell // COLS).reshape(-1)
    col = (cell % COLS).reshape(-1)
    row_hot = (row[None, :] == jnp.arange(tiles * ROWS, dtype=jnp.int32)[:, None]).astype(BF16)
    col_hot = col[:, None] == jnp.arange(COLS, dtype=jnp.int32)[None, :]
    spread = jnp.where(col_hot[None], pieces[:, :, None], jnp.zeros((), BF16))
    field = jnp.einsum("rk,pkc->prc", row_hot, spread, preferred_element_type=F32)
    field = jnp.stack([field[2] + field[1] + field[0], field[5] + field[4] + field[3]], 0)
    field = field.reshape(2, tiles, ROWS, COLS).transpose(1, 0, 2, 3)
    bit = tiles // 2
    while bit:
        swap = [(i, i ^ bit) for i in range(tiles)]
        field = field[:bit] + lax.ppermute(field[bit:], "gy", swap)
        bit //= 2
    return field[0, 0], field[0, 1]


def sum_everywhere(x):
    def other(axis, k):
        return lax.ppermute(x, axis, [(i, i ^ k) for i in range(lax.axis_size(axis))])

    x = x + other("gy", 1)
    for axis, unit in (("gy", 2), ("gx", 1), ("gx", 4)):
        x = (x + other(axis, unit)) + (other(axis, 2 * unit) + other(axis, 3 * unit))
    return x


def transform_kernel(total, mix, work, inverse):
    n = MEMBERS
    full = lax.Precision.HIGHEST
    rows_i = lax.broadcasted_iota(jnp.int32, (n, n), 0)
    cols_i = lax.broadcasted_iota(jnp.int32, (n, n), 1)
    eye = (rows_i == cols_i).astype(F32)
    work[:, 0:n] = total[0:n, :] + F32(n - 1) * eye
    work[:, n:2 * n] = eye
    sub = lax.broadcasted_iota(jnp.int32, (PANEL, n), 0)
    for first in range(0, n, PANEL):
        rows = slice(first, first + PANEL)
        up, inv = work[rows, 0:n], work[rows, n:2 * n]
        cols = [jnp.broadcast_to(up[:, first + k:first + k + 1], (PANEL, n)) for k in range(PANEL)]
        scale = jnp.zeros((PANEL, n), F32)
        for k in range(PANEL):
            pivot = cols[k][k:k + 1]
            scale = jnp.where(sub == k, pivot, scale)
            if k + 1 < PANEL:
                times = jnp.where(sub > k, cols[k], 0.0) * (1.0 / pivot)
                for q in range(k + 1, PANEL):
                    cols[q] = cols[q] - times * cols[q][k:k + 1]
                up = up - times * up[k:k + 1]
                inv = inv - times * inv[k:k + 1]
        scale = lax.rsqrt(scale)
        up, inv = up * scale, inv * scale
        inverse[rows, :] = inv
        after = first + PANEL
        if after < n:
            update = lax.dot_general(
                up, jnp.concatenate([up, inv], axis=1), (((0,), (0,)), ((), ())),
                precision=full, preferred_element_type=F32,
            )
            work[after:, :] = work[after:, :] - update[after:, :]
    low = inverse[...]
    proj = total[n:n + 8, :]
    inner = lax.dot_general(proj, low, (((1,), (1,)), ((), ())), precision=full, preferred_element_type=F32)
    weights = jnp.dot(inner, low, precision=full, preferred_element_type=F32)
    transform_t = weights[0:1] + F32((n - 1) ** 0.5) * low
    spare = (1.0 - jnp.sum(transform_t, axis=1, keepdims=True)) * (1.0 / n)
    value = transform_t + spare
    high = value.astype(BF16)
    mix[:, 0:n] = high
    mix[:, n:2 * n] = (value - high.astype(F32)).astype(BF16)


def make_mix(total):
    vmem = pl.BlockSpec(memory_space=pltpu.VMEM)
    return pl.pallas_call(
        transform_kernel,
        in_specs=[vmem],
        out_specs=vmem,
        out_shape=jax.ShapeDtypeStruct((MEMBERS, 2 * MEMBERS), BF16),
        scratch_shapes=[
            pltpu.VMEM((MEMBERS, 2 * MEMBERS), F32),
            pltpu.VMEM((MEMBERS, MEMBERS), F32),
        ],
        compiler_params=params(),
        cost_estimate=COST,
        name="transform",
    )(total)


def on_device(ensemble, layer_depth, obs_dest, obs_cell, obs_value, obs_sigma):
    row0 = lax.axis_index("gx") * ROWS - HALO + jnp.arange(WIDE_ROWS, dtype=jnp.int32)
    col0 = lax.axis_index("gy") * COLS - HALO + jnp.arange(COLS + 2 * HALO, dtype=jnp.int32)
    row_in = (row0 >= 0) & (row0 < lax.axis_size("gx") * ROWS)
    col_in = (col0 >= 0) & (col0 < lax.axis_size("gy") * COLS)
    d = layer_depth
    d = jnp.concatenate(
        [shift(d[:, :, COLS - HALO:], "gy", 1), d, shift(d[:, :, :HALO], "gy", -1)], axis=2
    )
    d = jnp.concatenate(
        [shift(d[:, ROWS - HALO:], "gx", 1), d, shift(d[:, :HALO], "gx", -1)], axis=1
    )
    d, north, south = lax.optimization_barrier((d,) + tuple(edge_rows(ensemble)))
    top = shift(south, "gx", 1)
    bottom = shift(north, "gx", -1)
    own, left_out, right_out = all_rows(ensemble, north)
    left = shift(right_out, "gy", 1)
    right = shift(left_out, "gy", -1)
    d = jnp.where(row_in[:, None] & col_in[None, :], (HALF * HALF) * d, 0.0).astype(BF16)
    d = d.reshape(LAYERS, WIDE_ROWS, SEGMENTS, POSITIONS).transpose(0, 1, 3, 2)
    depth = jnp.broadcast_to(d[..., None], d.shape + (MEMBERS,))
    mask = col_in.reshape(SEGMENTS, POSITIONS).T.astype(BF16)
    mask = jnp.stack([jnp.zeros_like(mask), mask], axis=0)
    masks = jnp.broadcast_to(mask[..., None], mask.shape + (MEMBERS,))
    row_in = row_in.astype(jnp.int32)[None, :]
    sides = jnp.stack([left, right], axis=0)
    sides, depth, masks = lax.optimization_barrier((sides, depth, masks))
    corner_t = shift(sides[:, :, :, 12:], "gx", 1)
    corner_b = shift(sides[:, :, :, :4], "gx", -1)

    weight, pull = observed_cells(obs_dest[0, 0], obs_cell[0, 0], obs_value[0, 0], obs_sigma[0, 0])
    state = forecast(
        own, top, bottom, left, right, corner_t, corner_b, depth, row_in, masks
    )
    total = sum_everywhere(gram_of(state, weight, pull))
    return analyse(state, make_mix(total))


def solution(mesh):
    in_specs = (
        P(None, None, None, "gx", "gy"),
        P(None, "gx", "gy"),
        P("gx", "gy", None),
        P("gx", "gy", None, None),
        P("gx", "gy", None, None),
        P("gx", "gy", None, None),
    )
    out_specs = P(None, None, None, "gx", "gy")
    return jax.shard_map(
        on_device, mesh=mesh, in_specs=in_specs, out_specs=out_specs, check_vma=False
    )
```

time: 190 us -> 158 us (0.83)
  other arithmetic: 32.7 us -> 5.9 us
  local copies, waits for them, and re-layouts: 27.8 us -> 7.89 us
  waiting for transfers between devices: 16.9 us -> 24.8 us
  starting transfers between devices: 31.7 us -> 36.8 us
  Pallas kernels: 76 us -> 79.4 us
    another operation x6 -> x1, other arithmetic: 23.8 us -> 0.07 us  [on_device(): sides = jnp.stack([left, right], axis=0)]
    slice x4, local copies, waits for them, and re-layouts: 6.72 us -> 0.05 us  [the longest x1 0.03 us: on_device(): corner_b = shift(sides[:, :, :, :4], 'gx', -1)]
    ppermute x10, waiting for transfers between devices: 5.6 us -> 12 us  [shift(): return lax.ppermute(x, axis, [(i, (i + by) % n) for i in range(n)])]
    broadcast_in_dim x3 -> x0, local copies, waits for them, and re-layouts: 4.55 us -> none  [the longest x2 2.62 us: on_device(): pull = jnp.broadcast_to(pull[..., None], (ROWS, COLS, MEMBERS))]
    ppermute x10, starting transfers between devices: 18.8 us -> 22.7 us  [shift(): return lax.ppermute(x, axis, [(i, (i + by) % n) for i in range(n)])]
    unnamed x32 -> x12, local copies, waits for them, and re-layouts: 4.74 us -> 1.28 us
    pallas_call x4, Pallas kernels: 54.1 us -> 56.7 us  [the longest x1 30.8 us: forecast(): pl.pallas_call(forecast_kernel, in_specs=[anywhere] * 8 + [pl.BlockSpec(m...]
    concatenate x4 -> x0, local copies, waits for them, and re-layouts: 2.13 us -> none  [the longest x1 1.09 us: on_device(): sides = jnp.concatenate([from_left, from_right], axis=3)]
  transfers between devices with their start and end apart: 23 -> 23, of which waited for: 10 -> 12; matrix products, arithmetic and copies ran while one was open for 12% -> 8% of each run, Pallas kernels for 10% -> 10%
where the time goes in v3:
time: 158 us; the launch traced here: 157 us
  Pallas kernels  79.4 us (50%)
  starting transfers between devices  36.8 us (23%)
  waiting for transfers between devices  24.8 us (16%)
  local copies, waits for them, and re-layouts  7.89 us (5%)
  other arithmetic  5.9 us (4%)
  matrix products  1.91 us (1%)
    pallas_call x1, Pallas kernels, forecast(): pl.pallas_call(forecast_kernel, in_specs=[anywhere] * 8 + [pl.BlockSpec(m...  30.8 us
    ppermute x10, starting transfers between devices, shift(): return lax.ppermute(x, axis, [(i, (i + by) % n) for i in range(n)])  22.7 us
    pallas_call x1, Pallas kernels, analyse(): pl.pallas_call(analysis_kernel, grid=(LAYERS, 3), in_specs=[pl.BlockSpec(...  14.2 us
    ppermute x10, waiting for transfers between devices, other(): lax.ppermute(x, axis, [(i, i ^ k) for i in range(lax.axis_size(axis))])  12.1 us
    ppermute x10, waiting for transfers between devices, shift(): return lax.ppermute(x, axis, [(i, (i + by) % n) for i in range(n)])  12 us
    ppermute x10, starting transfers between devices, other(): lax.ppermute(x, axis, [(i, i ^ k) for i in range(lax.axis_size(axis))])  11.9 us
    pallas_call x1, Pallas kernels, make_mix(): pl.pallas_call(transform_kernel, in_specs=[vmem], out_specs=vmem, out_sha...  10.5 us
    pallas_call x1, Pallas kernels, gram_of(): pl.pallas_call(gram_kernel, grid=(1,), in_specs=[pl.BlockSpec((LAYERS, 1,...  8.46 us
  transfers between devices with their start and end apart: 23, of which 12 were waited for; matrix products, arithmetic and copies ran while one was open for 8% of the time, Pallas kernels for 10%

profile of v3, /device:TPU:0, one launch (start us, length us, event | category | flops | bytes accessed | tf_op | source)
XLA Modules:
  0.0 157.0 jit_solution(7882096141344235437)
XLA Ops:
  0.9 2.3 %collective-permute-start.1 = (f32[2,32,8]{2,1,0:T(8,128)S(1)}, f32[2,32,8]{2,1,0:T(8,128)S(1)}, u32[]{:S(2)}, u32[]{:S(2)}) collective-permute-start(f32[2,32,8]{2,1,0:T(8,128)S(1)} %get-tuple-element.39), channel_id=1, source_target_pairs={{0,7},{1,0},{2,1},{3,2},{4,3},{5,4},{6,5},{7,6},{8,15},{9,8},{10,9... | collective-permute-start | bytes 6152 | tf_op jit(solution)/shard_map/ppermute | solution.py:38
  6.6 1.9 %fusion.8 = f32[6,256,128]{1,2,0:T(8,128)S(1)} fusion(s32[4096]{0:T(1024)S(1)} %get-tuple-element.44, pred[4096,128]{0,1:T(8,128)(4,1)S(1)} %iota_compare_fusion.1, bf16[6,4096]{1,0:T(8,128)(2,1)S(1)} %bitcast.58), kind=kOutput, calls=%fused_computation.9 | convolution fusion | flops 1614807040 | bytes 1376256 | tf_op jit(solution)/shard_map/rk,pkc->prc/dot_general | solution.py:438
  8.8 1.4 collective-permute-start.10
  10.5 6.6 %collective-permute-start.3 = (f32[2,8,144]{2,1,0:T(8,128)S(1)}, f32[2,8,144]{2,1,0:T(8,128)S(1)}, u32[]{:S(2)}, u32[]{:S(2)}) collective-permute-start(f32[2,8,144]{2,1,0:T(8,128)S(1)} %get-tuple-element.32), channel_id=1, source_target_pairs={{0,120},{8,0},{16,8},{24,16},{32,24},{40,32},{48,40},{56,48},{64,5... | collective-permute-start | bytes 27656 | tf_op jit(solution)/shard_map/ppermute | solution.py:38
  17.0 7.1 %edge_rows.1 = (bf16[44,128,128]{2,1,0:T(8,128)(2,1)}, bf16[44,128,128]{2,1,0:T(8,128)(2,1)}) custom-call(bf16[2,3,128,32,128]{4,3,2,1,0:T(8,128)(2,1)} %e_ref.3), custom_call_target="tpu_custom_call" | custom-call | flops 1 | bytes 1 | tf_op jit(solution)/shard_map/edge_rows/pallas_call | solution.py:85
  24.3 5.4 %collective-permute-start.5 = (bf16[44,128,128]{2,1,0:T(8,128)(2,1)}, bf16[44,128,128]{2,1,0:T(8,128)(2,1)}, u32[]{:S(2)}, u32[]{:S(2)}) collective-permute-start(bf16[44,128,128]{2,1,0:T(8,128)(2,1)} %get-tuple-element.18.after_ref), channel_id=1, source_target_pairs={{0,120},{8,0},{16,8},{24,16},{32,24},{40,32},{48,40},{56,48},{64,5... | collective-permute-start | bytes 4325384 | tf_op jit(solution)/shard_map/ppermute | solution.py:38
  31.0 8.3 %all_rows.1 = (bf16[2,3,32,128,128]{4,3,2,1,0:T(8,128)(2,1)}, bf16[2,3,16,16,128]{4,3,2,1,0:T(8,128)(2,1)}, bf16[2,3,16,16,128]{4,3,2,1,0:T(8,128)(2,1)}) custom-call(bf16[2,3,128,32,128]{4,3,2,1,0:T(8,128)(2,1)} %e_ref.3, bf16[44,128,128]{2,1,0:T(8,128)(2,1)} %get-tuple-element.18.after_ref), custom_call_target="tpu_custom_call" | custom-call | flops 1 | bytes 1 | tf_op jit(solution)/shard_map/all_rows/pallas_call | solution.py:123
  40.2 2.1 %collective-permute-start.7 = (bf16[2,3,16,16,128]{4,3,2,1,0:T(8,128)(2,1)}, bf16[2,3,16,16,128]{4,3,2,1,0:T(8,128)(2,1)S(1)}, u32[]{:S(2)}, u32[]{:S(2)}) collective-permute-start(bf16[2,3,16,16,128]{4,3,2,1,0:T(8,128)(2,1)} %get-tuple-element.22), channel_id=1, source_target_pairs={{0,7},{1,0},{2,1},{3,2},{4,3},{5,4},{6,5},{7,6},{8,15},{9,8},{10,9... | collective-permute-start | bytes 1179656 | tf_op jit(solution)/shard_map/ppermute | solution.py:38
  43.6 4.3 %collective-permute-done.6.left = bf16[2,3,16,16,128]{4,3,2,1,0:T(8,128)(2,1)S(1)} collective-permute-done((bf16[2,3,16,16,128]{4,3,2,1,0:T(8,128)(2,1)}, bf16[2,3,16,16,128]{4,3,2,1,0:T(8,128)(2,1)S(1)}, u32[]{:S(2)}, u32[]{:S(2)}) %collective-permute-start.6) | collective-permute-done | bytes 393248 | tf_op jit(solution)/shard_map/ppermute | solution.py:38
  48.0 3.5 %broadcast_in_dim.51.depth_in = bf16[2,48,9,16,128]{4,3,2,1,0:T(8,128)(2,1)} broadcast(bf16[2,48,9,16]{3,2,1,0:T(8,128)(2,1)S(1)} %copy.11), dimensions={0,1,2,3} | broadcast | bytes 3566592 | tf_op jit(solution)/shard_map/broadcast_in_dim | solution.py:541
  52.4 5.3 %collective-permute-start.9 = (bf16[2,2,3,4,16,128]{5,4,3,2,1,0:T(8,128)(2,1)S(1)}, bf16[2,2,3,4,16,128]{5,4,3,2,1,0:T(8,128)(2,1)S(1)}, u32[]{:S(2)}, u32[]{:S(2)}) collective-permute-start(bf16[2,2,3,4,16,128]{5,4,3,2,1,0:T(8,128)(2,1)S(1)} %get-tuple-element.29), channel_id=1, source_target_pairs={{0,120},{8,0},{16,8},{24,16},{32,24},{40,32},{48,40},{56,48},{64,5... | collective-permute-start | bytes 589832 | tf_op jit(solution)/shard_map/ppermute | solution.py:38
  58.3 7.7 %collective-permute-done.8.corner_t = bf16[2,2,3,4,16,128]{5,4,3,2,1,0:T(8,128)(2,1)S(1)} collective-permute-done((bf16[2,2,3,4,16,128]{5,4,3,2,1,0:T(8,128)(2,1)S(1)}, bf16[2,2,3,4,16,128]{5,4,3,2,1,0:T(8,128)(2,1)S(1)}, u32[]{:S(2)}, u32[]{:S(2)}) %collective-permute-start.8) | collective-permute-done | bytes 196640 | tf_op jit(solution)/shard_map/ppermute | solution.py:38
  67.3 30.8 %forecast.1.heights.state = bf16[2,3,32,128,128]{4,3,2,1,0:T(8,128)(2,1)} custom-call(bf16[2,3,32,128,128]{4,3,2,1,0:T(8,128)(2,1)} %get-tuple-element.19.own, bf16[44,128,128]{2,1,0:T(8,128)(2,1)} %copy-done.2, bf16[44,128,128]{2,1,0:T(8,128)(2,1)} %collective-permute-done.5.bottom, bf16[2,3,16,16,128]{4,3,2,1,0:T(8,128)(2,1)} %copy-done, ...), custom_call_target="tpu_custom_call" | custom-call | flops 1 | bytes 1 | tf_op jit(solution)/shard_map/forecast/pallas_call | solution.py:295
  98.2 8.5 %gram.1 = f32[136,128]{1,0:T(8,128)} custom-call(bf16[2,3,32,128,128]{4,3,2,1,0:T(8,128)(2,1)} %forecast.1.heights.state, f32[32,128]{1,0:T(8,128)} %get-tuple-element.34.weight, f32[32,128]{1,0:T(8,128)} %get-tuple-element.33.pull), custom_call_target="tpu_custom_call" | custom-call | flops 1 | bytes 1 | tf_op jit(solution)/shard_map/gram/pallas_call | solution.py:359
  106.6 1.5 collective-permute-done.13
  109.6 2.7 %collective-permute-start.16 = (f32[136,128]{1,0:T(8,128)S(1)}, f32[136,128]{1,0:T(8,128)S(1)}, u32[]{:S(2)}, u32[]{:S(2)}) collective-permute-start(f32[136,128]{1,0:T(8,128)S(1)} %add.154), channel_id=1, source_target_pairs={{0,6},{1,7},{2,4},{3,5},{4,2},{5,3},{6,0},{7,1},{8,14},{9,15},{10,... | collective-permute-start | bytes 208904 | tf_op jit(solution)/shard_map/ppermute | solution.py:451
  112.6 2.8 %collective-permute-done.15 = f32[136,128]{1,0:T(8,128)S(1)} collective-permute-done((f32[136,128]{1,0:T(8,128)S(1)}, f32[136,128]{1,0:T(8,128)S(1)}, u32[]{:S(2)}, u32[]{:S(2)}) %collective-permute-start.15) | collective-permute-done | bytes 69664 | tf_op jit(solution)/shard_map/ppermute | solution.py:451
  116.8 3.4 %collective-permute-start.17 = (f32[136,128]{1,0:T(8,128)S(1)}, f32[136,128]{1,0:T(8,128)S(1)}, u32[]{:S(2)}, u32[]{:S(2)}) collective-permute-start(f32[136,128]{1,0:T(8,128)S(1)} %add_add_fusion.2), channel_id=1, source_target_pairs={{0,8},{8,0},{16,24},{24,16},{32,40},{40,32},{48,56},{56,48},{64,72... | collective-permute-start | bytes 208904 | tf_op jit(solution)/shard_map/ppermute | solution.py:451
  120.2 2.8 %collective-permute-done.18 = f32[136,128]{1,0:T(8,128)S(1)} collective-permute-done((f32[136,128]{1,0:T(8,128)S(1)}, f32[136,128]{1,0:T(8,128)S(1)}, u32[]{:S(2)}, u32[]{:S(2)}) %collective-permute-start.18) | collective-permute-done | bytes 69664 | tf_op jit(solution)/shard_map/ppermute | solution.py:451
  123.3 2.0 %collective-permute-start.21 = (f32[136,128]{1,0:T(8,128)S(1)}, f32[136,128]{1,0:T(8,128)S(1)}, u32[]{:S(2)}, u32[]{:S(2)}) collective-permute-start(f32[136,128]{1,0:T(8,128)S(1)} %add_add_fusion.1), channel_id=1, source_target_pairs={{0,64},{8,72},{16,80},{24,88},{32,96},{40,104},{48,112},{56,120},{... | collective-permute-start | bytes 208904 | tf_op jit(solution)/shard_map/ppermute | solution.py:451
  125.2 2.1 %collective-permute-start.22 = (f32[136,128]{1,0:T(8,128)S(1)}, f32[136,128]{1,0:T(8,128)S(1)}, u32[]{:S(2)}, u32[]{:S(2)}) collective-permute-start(f32[136,128]{1,0:T(8,128)S(1)} %add_add_fusion.1), channel_id=1, source_target_pairs={{0,96},{8,104},{16,112},{24,120},{32,64},{40,72},{48,80},{56,88},{... | collective-permute-start | bytes 208904 | tf_op jit(solution)/shard_map/ppermute | solution.py:451
  128.1 1.7 %collective-permute-done.21 = f32[136,128]{1,0:T(8,128)S(1)} collective-permute-done((f32[136,128]{1,0:T(8,128)S(1)}, f32[136,128]{1,0:T(8,128)S(1)}, u32[]{:S(2)}, u32[]{:S(2)}) %collective-permute-start.21) | collective-permute-done | bytes 69664 | tf_op jit(solution)/shard_map/ppermute | solution.py:451
  132.3 10.5 %transform.1.mix = bf16[128,256]{1,0:T(8,128)(2,1)} custom-call(f32[136,128]{1,0:T(8,128)} %add_add_fusion.total), custom_call_target="tpu_custom_call" | custom-call | flops 1 | bytes 1 | tf_op jit(solution)/shard_map/transform/pallas_call | solution.py:506
  142.8 14.2 %analysis.1 = bf16[2,3,128,32,128]{4,3,2,1,0:T(8,128)(2,1)} custom-call(bf16[2,3,32,128,128]{4,3,2,1,0:T(8,128)(2,1)} %forecast.1.heights.state, bf16[128,256]{1,0:T(8,128)(2,1)} %transform.1.mix), custom_call_target="tpu_custom_call" | custom-call | flops 1 | bytes 1 | tf_op jit(solution)/shard_map/analysis/pallas_call | solution.py:405
  (78 shorter events, 17.9 us)
Async XLA Ops:
  0.9 9.4 %collective-permute-start.1 = (f32[2,32,8]{2,1,0:T(8,128)S(1)}, f32[2,32,8]{2,1,0:T(8,128)S(1)}, u32[]{:S(2)}, u32[]{:S(2)}) collective-permute-start(f32[2,32,8]{2,1,0:T(8,128)S(1)} %get-tuple-element.39), channel_id=1, source_target_pairs={{0,7},{1,0},{2,1},{3,2},{4,3},{5,4},{6,5},{7,6},{8,15},{9,8},{10,9... | collective-permute-start | bytes 6152 | tf_op jit(solution)/shard_map/ppermute | solution.py:38
  3.2 7.2 %collective-permute-start = (f32[2,32,8]{2,1,0:T(8,128)S(1)}, f32[2,32,8]{2,1,0:T(8,128)S(1)}, u32[]{:S(2)}, u32[]{:S(2)}) collective-permute-start(f32[2,32,8]{2,1,0:T(8,128)S(1)} %get-tuple-element.38), channel_id=1, source_target_pairs={{0,1},{1,2},{2,3},{3,4},{4,5},{5,6},{6,7},{7,0},{8,9},{9,10},{10,1... | collective-permute-start | bytes 6152 | tf_op jit(solution)/shard_map/ppermute | solution.py:38
  8.8 20.8 %collective-permute-start.10 = (f32[4,2,32,128]{3,2,1,0:T(8,128)S(1)}, f32[4,2,32,128]{3,2,1,0:T(8,128)S(1)}, u32[]{:S(2)}, u32[]{:S(2)}) collective-permute-start(f32[4,2,32,128]{3,2,1,0:T(8,128)S(1)} %slice.87), channel_id=1, source_target_pairs={{0,4},{1,5},{2,6},{3,7},{4,0},{5,1},{6,2},{7,3},{8,12},{9,13},{10,... | collective-permute-start | bytes 393224 | tf_op jit(solution)/shard_map/ppermute | solution.py:444
  10.5 13.6 %collective-permute-start.3 = (f32[2,8,144]{2,1,0:T(8,128)S(1)}, f32[2,8,144]{2,1,0:T(8,128)S(1)}, u32[]{:S(2)}, u32[]{:S(2)}) collective-permute-start(f32[2,8,144]{2,1,0:T(8,128)S(1)} %get-tuple-element.32), channel_id=1, source_target_pairs={{0,120},{8,0},{16,8},{24,16},{32,24},{40,32},{48,40},{56,48},{64,5... | collective-permute-start | bytes 27656 | tf_op jit(solution)/shard_map/ppermute | solution.py:38
  17.0 7.1 %collective-permute-start.2 = (f32[2,8,144]{2,1,0:T(8,128)S(1)}, f32[2,8,144]{2,1,0:T(8,128)S(1)}, u32[]{:S(2)}, u32[]{:S(2)}) collective-permute-start(f32[2,8,144]{2,1,0:T(8,128)S(1)} %get-tuple-element.31), channel_id=1, source_target_pairs={{0,8},{8,16},{16,24},{24,32},{32,40},{40,48},{48,56},{56,64},{64,7... | collective-permute-start | bytes 27656 | tf_op jit(solution)/shard_map/ppermute | solution.py:38
  24.2 41.8 %collective-permute-start.4 = (bf16[44,128,128]{2,1,0:T(8,128)(2,1)}, bf16[44,128,128]{2,1,0:T(8,128)(2,1)S(1)}, u32[]{:S(2)}, u32[]{:S(2)}) collective-permute-start(bf16[44,128,128]{2,1,0:T(8,128)(2,1)} %get-tuple-element.20), channel_id=1, source_target_pairs={{0,8},{8,16},{16,24},{24,32},{32,40},{40,48},{48,56},{56,64},{64,7... | collective-permute-start | bytes 4325384 | tf_op jit(solution)/shard_map/ppermute | solution.py:38
  24.3 41.8 %collective-permute-start.5 = (bf16[44,128,128]{2,1,0:T(8,128)(2,1)}, bf16[44,128,128]{2,1,0:T(8,128)(2,1)}, u32[]{:S(2)}, u32[]{:S(2)}) collective-permute-start(bf16[44,128,128]{2,1,0:T(8,128)(2,1)} %get-tuple-element.18.after_ref), channel_id=1, source_target_pairs={{0,120},{8,0},{16,8},{24,16},{32,24},{40,32},{48,40},{56,48},{64,5... | collective-permute-start | bytes 4325384 | tf_op jit(solution)/shard_map/ppermute | solution.py:38
  29.7 12.6 %collective-permute-start.11 = (f32[2,2,32,128]{3,2,1,0:T(8,128)S(1)}, f32[2,2,32,128]{3,2,1,0:T(8,128)S(1)}, u32[]{:S(2)}, u32[]{:S(2)}) collective-permute-start(f32[2,2,32,128]{3,2,1,0:T(8,128)S(1)} %slice.89), channel_id=1, source_target_pairs={{0,2},{1,3},{2,0},{3,1},{4,6},{5,7},{6,4},{7,5},{8,10},{9,11},{10,... | collective-permute-start | bytes 196616 | tf_op jit(solution)/shard_map/ppermute | solution.py:444
  39.3 8.6 %collective-permute-start.6 = (bf16[2,3,16,16,128]{4,3,2,1,0:T(8,128)(2,1)}, bf16[2,3,16,16,128]{4,3,2,1,0:T(8,128)(2,1)S(1)}, u32[]{:S(2)}, u32[]{:S(2)}) collective-permute-start(bf16[2,3,16,16,128]{4,3,2,1,0:T(8,128)(2,1)} %get-tuple-element.21), channel_id=1, source_target_pairs={{0,1},{1,2},{2,3},{3,4},{4,5},{5,6},{6,7},{7,0},{8,9},{9,10},{10,1... | collective-permute-start | bytes 1179656 | tf_op jit(solution)/shard_map/ppermute | solution.py:38
  40.2 7.7 %collective-permute-start.7 = (bf16[2,3,16,16,128]{4,3,2,1,0:T(8,128)(2,1)}, bf16[2,3,16,16,128]{4,3,2,1,0:T(8,128)(2,1)S(1)}, u32[]{:S(2)}, u32[]{:S(2)}) collective-permute-start(bf16[2,3,16,16,128]{4,3,2,1,0:T(8,128)(2,1)} %get-tuple-element.22), channel_id=1, source_target_pairs={{0,7},{1,0},{2,1},{3,2},{4,3},{5,4},{6,5},{7,6},{8,15},{9,8},{10,9... | collective-permute-start | bytes 1179656 | tf_op jit(solution)/shard_map/ppermute | solution.py:38
  42.3 1.3 collective-permute-start.12
  48.0 18.1 %copy-start.1 = (bf16[2,3,16,16,128]{4,3,2,1,0:T(8,128)(2,1)}, bf16[2,3,16,16,128]{4,3,2,1,0:T(8,128)(2,1)S(1)}, u32[]{:S(2)}) copy-start(bf16[2,3,16,16,128]{4,3,2,1,0:T(8,128)(2,1)S(1)} %collective-permute-done.7.right) | copy-start | bytes 1179652
  52.3 13.7 %collective-permute-start.8 = (bf16[2,2,3,4,16,128]{5,4,3,2,1,0:T(8,128)(2,1)S(1)}, bf16[2,2,3,4,16,128]{5,4,3,2,1,0:T(8,128)(2,1)S(1)}, u32[]{:S(2)}, u32[]{:S(2)}) collective-permute-start(bf16[2,2,3,4,16,128]{5,4,3,2,1,0:T(8,128)(2,1)S(1)} %get-tuple-element.30), channel_id=1, source_target_pairs={{0,8},{8,16},{16,24},{24,32},{32,40},{40,48},{48,56},{56,64},{64,7... | collective-permute-start | bytes 589832 | tf_op jit(solution)/shard_map/ppermute | solution.py:38
  52.4 13.6 %collective-permute-start.9 = (bf16[2,2,3,4,16,128]{5,4,3,2,1,0:T(8,128)(2,1)S(1)}, bf16[2,2,3,4,16,128]{5,4,3,2,1,0:T(8,128)(2,1)S(1)}, u32[]{:S(2)}, u32[]{:S(2)}) collective-permute-start(bf16[2,2,3,4,16,128]{5,4,3,2,1,0:T(8,128)(2,1)S(1)} %get-tuple-element.29), channel_id=1, source_target_pairs={{0,120},{8,0},{16,8},{24,16},{32,24},{40,32},{48,40},{56,48},{64,5... | collective-permute-start | bytes 589832 | tf_op jit(solution)/shard_map/ppermute | solution.py:38
  106.6 1.5 collective-permute-start.13
  109.0 6.4 %collective-permute-start.15 = (f32[136,128]{1,0:T(8,128)S(1)}, f32[136,128]{1,0:T(8,128)S(1)}, u32[]{:S(2)}, u32[]{:S(2)}) collective-permute-start(f32[136,128]{1,0:T(8,128)S(1)} %add.154), channel_id=1, source_target_pairs={{0,4},{1,5},{2,6},{3,7},{4,0},{5,1},{6,2},{7,3},{8,12},{9,13},{10,... | collective-permute-start | bytes 208904 | tf_op jit(solution)/shard_map/ppermute | solution.py:451
  109.6 6.7 %collective-permute-start.16 = (f32[136,128]{1,0:T(8,128)S(1)}, f32[136,128]{1,0:T(8,128)S(1)}, u32[]{:S(2)}, u32[]{:S(2)}) collective-permute-start(f32[136,128]{1,0:T(8,128)S(1)} %add.154), channel_id=1, source_target_pairs={{0,6},{1,7},{2,4},{3,5},{4,2},{5,3},{6,0},{7,1},{8,14},{9,15},{10,... | collective-permute-start | bytes 208904 | tf_op jit(solution)/shard_map/ppermute | solution.py:451
  112.3 4.3 %collective-permute-start.14 = (f32[136,128]{1,0:T(8,128)S(1)}, f32[136,128]{1,0:T(8,128)S(1)}, u32[]{:S(2)}, u32[]{:S(2)}) collective-permute-start(f32[136,128]{1,0:T(8,128)S(1)} %add.154), channel_id=1, source_target_pairs={{0,2},{1,3},{2,0},{3,1},{4,6},{5,7},{6,4},{7,5},{8,10},{9,11},{10,... | collective-permute-start | bytes 208904 | tf_op jit(solution)/shard_map/ppermute | solution.py:451
  116.6 6.4 %collective-permute-start.18 = (f32[136,128]{1,0:T(8,128)S(1)}, f32[136,128]{1,0:T(8,128)S(1)}, u32[]{:S(2)}, u32[]{:S(2)}) collective-permute-start(f32[136,128]{1,0:T(8,128)S(1)} %add_add_fusion.2), channel_id=1, source_target_pairs={{0,16},{8,24},{16,0},{24,8},{32,48},{40,56},{48,32},{56,40},{64,80... | collective-permute-start | bytes 208904 | tf_op jit(solution)/shard_map/ppermute | solution.py:451
  116.7 6.6 %collective-permute-start.19 = (f32[136,128]{1,0:T(8,128)S(1)}, f32[136,128]{1,0:T(8,128)S(1)}, u32[]{:S(2)}, u32[]{:S(2)}) collective-permute-start(f32[136,128]{1,0:T(8,128)S(1)} %add_add_fusion.2), channel_id=1, source_target_pairs={{0,24},{8,16},{16,8},{24,0},{32,56},{40,48},{48,40},{56,32},{64,88... | collective-permute-start | bytes 208904 | tf_op jit(solution)/shard_map/ppermute | solution.py:451
  116.8 6.5 %collective-permute-start.17 = (f32[136,128]{1,0:T(8,128)S(1)}, f32[136,128]{1,0:T(8,128)S(1)}, u32[]{:S(2)}, u32[]{:S(2)}) collective-permute-start(f32[136,128]{1,0:T(8,128)S(1)} %add_add_fusion.2), channel_id=1, source_target_pairs={{0,8},{8,0},{16,24},{24,16},{32,40},{40,32},{48,56},{56,48},{64,72... | collective-permute-start | bytes 208904 | tf_op jit(solution)/shard_map/ppermute | solution.py:451
  123.3 6.6 %collective-permute-start.21 = (f32[136,128]{1,0:T(8,128)S(1)}, f32[136,128]{1,0:T(8,128)S(1)}, u32[]{:S(2)}, u32[]{:S(2)}) collective-permute-start(f32[136,128]{1,0:T(8,128)S(1)} %add_add_fusion.1), channel_id=1, source_target_pairs={{0,64},{8,72},{16,80},{24,88},{32,96},{40,104},{48,112},{56,120},{... | collective-permute-start | bytes 208904 | tf_op jit(solution)/shard_map/ppermute | solution.py:451
  125.2 5.5 %collective-permute-start.22 = (f32[136,128]{1,0:T(8,128)S(1)}, f32[136,128]{1,0:T(8,128)S(1)}, u32[]{:S(2)}, u32[]{:S(2)}) collective-permute-start(f32[136,128]{1,0:T(8,128)S(1)} %add_add_fusion.1), channel_id=1, source_target_pairs={{0,96},{8,104},{16,112},{24,120},{32,64},{40,72},{48,80},{56,88},{... | collective-permute-start | bytes 208904 | tf_op jit(solution)/shard_map/ppermute | solution.py:451
  127.3 4.3 %collective-permute-start.20 = (f32[136,128]{1,0:T(8,128)S(1)}, f32[136,128]{1,0:T(8,128)S(1)}, u32[]{:S(2)}, u32[]{:S(2)}) collective-permute-start(f32[136,128]{1,0:T(8,128)S(1)} %add_add_fusion.1), channel_id=1, source_target_pairs={{0,32},{8,40},{16,48},{24,56},{32,0},{40,8},{48,16},{56,24},{64,96... | collective-permute-start | bytes 208904 | tf_op jit(solution)/shard_map/ppermute | solution.py:451
  (5 other events, 24.6 us)

commit v4 on v3

--- a/solution.py
+++ b/solution.py
@@ -58,45 +58,10 @@
 FAR = 3 * HALO - 2
 
 
-def edge_rows(ensemble):
-    def kernel(e_ref, north, south, planes):
+def all_rows(ensemble):
+    def kernel(e_ref, own, left, right, north, south, planes):
         part = pl.program_id(1)
         base = pl.program_id(0) * FAR + part * (HALO - 1) + (part > 0)
-
-        def put(x, value):
-            if x < HALO - 1:
-                north[base + x] = value
-            elif x > ROWS - HALO:
-                south[base + (x - (ROWS - HALO)) - (part > 0)] = value
-            else:
-
-                @pl.when(part == 0)
-                def _():
-                    if x < HALO:
-                        north[base + x] = value
-                    else:
-                        south[base] = value
-
-        rows = list(range(HALO)) + list(range(ROWS - HALO, ROWS))
-        turn_rows(e_ref, planes, rows, put)
-
-    whole = pl.BlockSpec((LAYERS * FAR, COLS, MEMBERS), lambda i, j: (0, 0, 0))
-    shape = jax.ShapeDtypeStruct((LAYERS * FAR, COLS, MEMBERS), BF16)
-    return pl.pallas_call(
-        kernel,
-        grid=(LAYERS, 3),
-        in_specs=[E_BLOCK],
-        out_specs=[whole, whole],
-        out_shape=[shape, shape],
-        scratch_shapes=[pltpu.VMEM((MEMBERS * (ROWS + 1), COLS), F32)],
-        compiler_params=params(),
-        cost_estimate=COST,
-        name="edge_rows",
-    )(ensemble)
-
-
-def all_rows(ensemble, after):
-    def kernel(e_ref, after_ref, own, left, right, planes):
         held = {}
 
         def put(x, value):
@@ -109,6 +74,21 @@
                 )
             else:
                 held[x] = value
+            if x < HALO - 1:
+                north[base + x] = value
+            elif x > ROWS - HALO:
+                south[base + (x - (ROWS - HALO)) - (part > 0)] = value
+            elif x == HALO - 1:
+
+                @pl.when(part == 0)
+                def _():
+                    north[base + x] = value
+
+            elif x == ROWS - HALO:
+
+                @pl.when(part == 0)
+                def _():
+                    south[base] = value
 
         turn_rows(e_ref, planes, list(range(ROWS)), put)
 
@@ -120,22 +100,25 @@
 
     tile = (1, 1, ROWS, COLS, MEMBERS)
     side = (1, 1, ROWS // 2, 16, MEMBERS)
+    edge = (LAYERS * FAR, COLS, MEMBERS)
+    edge_spec = pl.BlockSpec(edge, lambda i, j: (0, 0, 0))
+    edge_shape = jax.ShapeDtypeStruct(edge, BF16)
     return pl.pallas_call(
         kernel,
         grid=(LAYERS, 3),
-        in_specs=[E_BLOCK, pl.BlockSpec(memory_space=pl.ANY)],
-        out_specs=[spec(tile), spec(side), spec(side)],
-        out_shape=[whole(tile), whole(side), whole(side)],
+        in_specs=[E_BLOCK],
+        out_specs=[spec(tile), spec(side), spec(side), edge_spec, edge_spec],
+        out_shape=[whole(tile), whole(side), whole(side), edge_shape, edge_shape],
         scratch_shapes=[pltpu.VMEM((MEMBERS * (ROWS + 1), COLS), F32)],
         compiler_params=params(),
         cost_estimate=COST,
         name="all_rows",
-    )(ensemble, after)
+    )(ensemble)
 
 
 def forecast_kernel(
-    own, top, bottom, left, right, corner_t, corner_b, depth_in, row_in, masks,
-    out, raw, raw_side, depth, st, fx, fy, pr, line, sems,
+    own, top, bottom, left, right, corner_t, corner_b, depth_in, row_in, masks, weight, pull,
+    out, total, raw, raw_side, depth, st, fx, fy, pr, line, y_parts, z_parts, acc, sems,
 ):
     depth_copy = pltpu.make_async_copy(depth_in, depth, sems.at[54])
     depth_copy.start()
@@ -261,8 +244,8 @@
         )
 
     done = []
-    for l in range(LAYERS):
-        for c in range(3):
+    for c in (2, 0, 1):
+        for l in range(LAYERS):
 
             def pack(r, carry):
                 base = lax.rem(r, 4) * (4 * LINE)
@@ -283,8 +266,48 @@
                 )
             )
             done[-1].start()
+    add_up(raw, weight, pull, total, y_parts, z_parts, acc)
     for d in done:
         d.wait()
+
+
+def add_up(state, weight, pull, total, left, right, acc):
+    n = MEMBERS
+    over_last = (((1,), (1,)), ((), ()))
+    eye = lax.broadcasted_iota(jnp.int32, (n, n), 0) == lax.broadcasted_iota(jnp.int32, (n, n), 1)
+    away = (eye.astype(F32) - 1.0 / n).astype(BF16)
+    away = jnp.concatenate([away, away], axis=1)
+    share = jnp.full((8, 2 * n), 1.0 / n, BF16)
+    acc[...] = jnp.zeros_like(acc)
+
+    def body(x, carry):
+        both = jnp.concatenate([state[0, 2, x], state[1, 2, x]], axis=1)
+        z = lax.dot_general(both, away, over_last, preferred_element_type=F32)
+        zt = lax.dot_general(away, both, over_last, preferred_element_type=F32)
+        mean = lax.dot_general(share, both, over_last, preferred_element_type=F32)[0:1]
+        w = weight[pl.ds(x, 1), :]
+        y = zt * w
+        y_high = y.astype(BF16)
+        z_high = z.astype(BF16)
+        left[0, x] = y_high
+        left[1, x] = (y - y_high.astype(F32)).astype(BF16)
+        right[x, :, 0:n] = z_high
+        right[x, :, n:2 * n] = (z - z_high.astype(F32)).astype(BF16)
+        acc[...] += zt * (pull[pl.ds(x, 1), :] - mean * w)
+        return carry
+
+    lax.fori_loop(0, ROWS, body, 0, unroll=4)
+
+    def multiply(x, part):
+        a = jnp.concatenate([left[0, 2 * x], left[0, 2 * x + 1]], axis=1)
+        b = jnp.concatenate([left[1, 2 * x], left[1, 2 * x + 1]], axis=1)
+        z = right[pl.ds(2 * x, 2)].reshape(2 * COLS, 2 * n)
+        main = jnp.dot(a, z, preferred_element_type=F32)
+        low = jnp.dot(b, z[:, 0:n], preferred_element_type=F32)
+        return part + (main[:, 0:n] + (main[:, n:2 * n] + low))
+
+    total[0:n, :] = lax.fori_loop(0, ROWS // 2, multiply, jnp.zeros((n, n), F32), unroll=2)
+    total[n:n + 8, :] = jnp.broadcast_to(jnp.sum(acc[...].T, axis=0, keepdims=True), (8, n))
 
 
 def forecast(*operands):
@@ -294,9 +317,12 @@
     vmem = pl.BlockSpec(memory_space=pltpu.VMEM)
     return pl.pallas_call(
         forecast_kernel,
-        in_specs=[anywhere] * 8 + [pl.BlockSpec(memory_space=pltpu.SMEM), vmem],
-        out_specs=anywhere,
-        out_shape=jax.ShapeDtypeStruct((LAYERS, 3, ROWS, COLS, MEMBERS), BF16),
+        in_specs=[anywhere] * 8 + [pl.BlockSpec(memory_space=pltpu.SMEM), vmem, vmem, vmem],
+        out_specs=[anywhere, vmem],
+        out_shape=[
+            jax.ShapeDtypeStruct((LAYERS, 3, ROWS, COLS, MEMBERS), BF16),
+            jax.ShapeDtypeStruct((MEMBERS + 8, MEMBERS), F32),
+        ],
         scratch_shapes=[
             pltpu.VMEM((LAYERS, 3, WIDE_ROWS, COLS, MEMBERS), BF16),
             pltpu.VMEM((2, LAYERS, 3, WIDE_ROWS // 2, 16, MEMBERS), BF16),
@@ -306,75 +332,15 @@
             pltpu.VMEM(padded, BF16),
             pltpu.VMEM(padded, BF16),
             pltpu.VMEM((16 * LINE, MEMBERS), F32),
+            pltpu.VMEM((2, ROWS, MEMBERS, COLS), BF16),
+            pltpu.VMEM((ROWS, COLS, 2 * MEMBERS), BF16),
+            pltpu.VMEM((MEMBERS, COLS), F32),
             pltpu.SemaphoreType.DMA((61,)),
         ],
         compiler_params=params(),
         cost_estimate=COST,
         name="forecast",
     )(*operands)
-
-
-def gram_kernel(heights, weight, pull, out, left, right, acc):
-    n = MEMBERS
-    over_last = (((1,), (1,)), ((), ()))
-    eye = lax.broadcasted_iota(jnp.int32, (n, n), 0) == lax.broadcasted_iota(jnp.int32, (n, n), 1)
-    away = (eye.astype(F32) - 1.0 / n).astype(BF16)
-    away = jnp.concatenate([away, away], axis=1)
-    share = jnp.full((8, 2 * n), 1.0 / n, BF16)
-    acc[...] = jnp.zeros_like(acc)
-
-    def body(x, carry):
-        both = jnp.concatenate([heights[0, 0, x], heights[1, 0, x]], axis=1)
-        z = lax.dot_general(both, away, over_last, preferred_element_type=F32)
-        zt = lax.dot_general(away, both, over_last, preferred_element_type=F32)
-        mean = lax.dot_general(share, both, over_last, preferred_element_type=F32)[0:1]
-        w = weight[pl.ds(x, 1), :]
-        y = zt * w
-        at = pl.ds(pl.multiple_of(x * COLS, COLS), COLS)
-        y_high = y.astype(BF16)
-        z_high = z.astype(BF16)
-        left[0, x] = y_high
-        left[1, x] = (y - y_high.astype(F32)).astype(BF16)
-        right[x, :, 0:n] = z_high
-        right[x, :, n:2 * n] = (z - z_high.astype(F32)).astype(BF16)
-        acc[...] += zt * (pull[pl.ds(x, 1), :] - mean * w)
-        return carry
-
-    lax.fori_loop(0, ROWS, body, 0, unroll=2)
-
-    def multiply(x, total):
-        a = jnp.concatenate([left[0, 2 * x], left[0, 2 * x + 1]], axis=1)
-        b = jnp.concatenate([left[1, 2 * x], left[1, 2 * x + 1]], axis=1)
-        z = right[pl.ds(2 * x, 2)].reshape(2 * COLS, 2 * n)
-        main = jnp.dot(a, z, preferred_element_type=F32)
-        low = jnp.dot(b, z[:, 0:n], preferred_element_type=F32)
-        return total + (main[:, 0:n] + (main[:, n:2 * n] + low))
-
-    out[0:n, :] = lax.fori_loop(0, ROWS // 2, multiply, jnp.zeros((n, n), F32), unroll=2)
-    out[n:n + 8, :] = jnp.broadcast_to(jnp.sum(acc[...].T, axis=0, keepdims=True), (8, n))
-
-
-def gram_of(state, weight, pull):
-    cells = pl.BlockSpec((ROWS, COLS), lambda i: (0, 0))
-    return pl.pallas_call(
-        gram_kernel,
-        grid=(1,),
-        in_specs=[
-            pl.BlockSpec((LAYERS, 1, ROWS, COLS, MEMBERS), lambda i: (0, 2, 0, 0, 0)),
-            cells,
-            cells,
-        ],
-        out_specs=pl.BlockSpec((MEMBERS + 8, MEMBERS), lambda i: (0, 0)),
-        out_shape=jax.ShapeDtypeStruct((MEMBERS + 8, MEMBERS), F32),
-        scratch_shapes=[
-            pltpu.VMEM((2, ROWS, MEMBERS, COLS), BF16),
-            pltpu.VMEM((ROWS, COLS, 2 * MEMBERS), BF16),
-            pltpu.VMEM((MEMBERS, COLS), F32),
-        ],
-        compiler_params=params(),
-        cost_estimate=COST,
-        name="gram",
-    )(state, weight, pull)
 
 
 def analysis_kernel(state, mix, out, planes):
@@ -425,7 +391,7 @@
     return [p.astype(BF16) for p in (a, b, c)]
 
 
-def observed_cells(dest, cell, value, sigma):
+def observed_cells(dest, cell, value, sigma, with_last):
     tiles = lax.axis_size("gy")
     inverse = 1.0 / sigma
     weight = inverse * inverse
@@ -440,10 +406,12 @@
     field = field.reshape(2, tiles, ROWS, COLS).transpose(1, 0, 2, 3)
     bit = tiles // 2
     while bit:
+        if bit == 1:
+            field, with_last = lax.optimization_barrier((field, with_last))
         swap = [(i, i ^ bit) for i in range(tiles)]
         field = field[:bit] + lax.ppermute(field[bit:], "gy", swap)
         bit //= 2
-    return field[0, 0], field[0, 1]
+    return field[0, 0], field[0, 1], with_last
 
 
 def sum_everywhere(x):
@@ -525,17 +493,19 @@
     col_in = (col0 >= 0) & (col0 < lax.axis_size("gy") * COLS)
     d = layer_depth
     d = jnp.concatenate(
+        [shift(d[:, ROWS - HALO:], "gx", 1), d, shift(d[:, :HALO], "gx", -1)], axis=1
+    )
+    own, left_out, right_out, north, south = all_rows(ensemble)
+    observed = (obs_dest[0, 0], obs_cell[0, 0], obs_value[0, 0], obs_sigma[0, 0])
+    d, north, south = lax.optimization_barrier((d, north, south))
+    top = shift(south, "gx", 1)
+    bottom = shift(north, "gx", -1)
+    left = shift(right_out, "gy", 1)
+    right = shift(left_out, "gy", -1)
+    d, left, observed = lax.optimization_barrier((d, left, observed))
+    d = jnp.concatenate(
         [shift(d[:, :, COLS - HALO:], "gy", 1), d, shift(d[:, :, :HALO], "gy", -1)], axis=2
     )
-    d = jnp.concatenate(
-        [shift(d[:, ROWS - HALO:], "gx", 1), d, shift(d[:, :HALO], "gx", -1)], axis=1
-    )
-    d, north, south = lax.optimization_barrier((d,) + tuple(edge_rows(ensemble)))
-    top = shift(south, "gx", 1)
-    bottom = shift(north, "gx", -1)
-    own, left_out, right_out = all_rows(ensemble, north)
-    left = shift(right_out, "gy", 1)
-    right = shift(left_out, "gy", -1)
     d = jnp.where(row_in[:, None] & col_in[None, :], (HALF * HALF) * d, 0.0).astype(BF16)
     d = d.reshape(LAYERS, WIDE_ROWS, SEGMENTS, POSITIONS).transpose(0, 1, 3, 2)
     depth = jnp.broadcast_to(d[..., None], d.shape + (MEMBERS,))
@@ -544,15 +514,14 @@
     masks = jnp.broadcast_to(mask[..., None], mask.shape + (MEMBERS,))
     row_in = row_in.astype(jnp.int32)[None, :]
     sides = jnp.stack([left, right], axis=0)
-    sides, depth, masks = lax.optimization_barrier((sides, depth, masks))
     corner_t = shift(sides[:, :, :, 12:], "gx", 1)
     corner_b = shift(sides[:, :, :, :4], "gx", -1)
 
-    weight, pull = observed_cells(obs_dest[0, 0], obs_cell[0, 0], obs_value[0, 0], obs_sigma[0, 0])
-    state = forecast(
-        own, top, bottom, left, right, corner_t, corner_b, depth, row_in, masks
+    weight, pull, (depth, masks) = observed_cells(*observed, (depth, masks))
+    state, total = forecast(
+        own, top, bottom, left, right, corner_t, corner_b, depth, row_in, masks, weight, pull
     )
-    total = sum_everywhere(gram_of(state, weight, pull))
+    total = sum_everywhere(total)
     return analyse(state, make_mix(total))
 
 

time: 158 us -> 150 us (0.949)
  waiting for transfers between devices: 24.8 us -> 35.3 us
  Pallas kernels: 79.4 us -> 69.4 us
  starting transfers between devices: 36.8 us -> 32.2 us
  other arithmetic: 5.9 us -> 3.02 us
    pallas_call x3 -> x1, Pallas kernels: 23.9 us -> 9.33 us  [all_rows(): pl.pallas_call(kernel, grid=(LAYERS, 3), in_specs=[E_BLOCK], out_specs=[s...]
    ppermute x3, waiting for transfers between devices: 0.69 us -> 8.5 us  [observed_cells(): field = field[:bit] + lax.ppermute(field[bit:], 'gy', swap)]
    ppermute x10, starting transfers between devices: 22.7 us -> 17.4 us  [shift(): return lax.ppermute(x, axis, [(i, (i + by) % n) for i in range(n)])]
    pallas_call x1, Pallas kernels: 30.8 us -> 35.3 us  [forecast(): pl.pallas_call(forecast_kernel, in_specs=[anywhere] * 8 + [pl.BlockSpec(m...]
    ppermute x10, starting transfers between devices: 11.9 us -> 14.1 us  [other(): lax.ppermute(x, axis, [(i, i ^ k) for i in range(lax.axis_size(axis))])]
    ppermute x10, waiting for transfers between devices: 12.1 us -> 13.8 us  [other(): lax.ppermute(x, axis, [(i, i ^ k) for i in range(lax.axis_size(axis))])]
  transfers between devices with their start and end apart: 23 -> 23, of which waited for: 12 -> 13; matrix products, arithmetic and copies ran while one was open for 8% -> 6% of each run, Pallas kernels for 10% -> 6%
where the time goes in v4:
time: 150 us
  Pallas kernels  69.4 us (46%)
  waiting for transfers between devices  35.3 us (24%)
  starting transfers between devices  32.2 us (21%)
  local copies, waits for them, and re-layouts  7.84 us (5%)
  other arithmetic  3.02 us (2%)
  matrix products  1.91 us (1%)
    pallas_call x1, Pallas kernels, forecast(): pl.pallas_call(forecast_kernel, in_specs=[anywhere] * 8 + [pl.BlockSpec(m...  35.3 us
    ppermute x10, starting transfers between devices, shift(): return lax.ppermute(x, axis, [(i, (i + by) % n) for i in range(n)])  17.4 us
    pallas_call x1, Pallas kernels, analyse(): pl.pallas_call(analysis_kernel, grid=(LAYERS, 3), in_specs=[pl.BlockSpec(...  14.2 us
    ppermute x10, starting transfers between devices, other(): lax.ppermute(x, axis, [(i, i ^ k) for i in range(lax.axis_size(axis))])  14.1 us
    ppermute x10, waiting for transfers between devices, other(): lax.ppermute(x, axis, [(i, i ^ k) for i in range(lax.axis_size(axis))])  13.8 us
    ppermute x10, waiting for transfers between devices, shift(): return lax.ppermute(x, axis, [(i, (i + by) % n) for i in range(n)])  13 us
    pallas_call x1, Pallas kernels, make_mix(): pl.pallas_call(transform_kernel, in_specs=[vmem], out_specs=vmem, out_sha...  10.5 us
    pallas_call x1, Pallas kernels, all_rows(): pl.pallas_call(kernel, grid=(LAYERS, 3), in_specs=[E_BLOCK], out_specs=[s...  9.33 us
  transfers between devices with their start and end apart: 23, of which 13 were waited for; matrix products, arithmetic and copies ran while one was open for 6% of the time, Pallas kernels for 6%

profile of v4, /device:TPU:0, one launch (start us, length us, event | category | flops | bytes accessed | tf_op | source)
XLA Modules:
  0.0 150.0 jit_solution(17839550506744286714)
XLA Ops:
  0.8 1.7 %collective-permute-start = (f32[2,8,128]{2,1,0:T(8,128)S(1)}, f32[2,8,128]{2,1,0:T(8,128)S(1)}, u32[]{:S(2)}, u32[]{:S(2)}) collective-permute-start(f32[2,8,128]{2,1,0:T(8,128)S(1)} %get-tuple-element.54), channel_id=1, source_target_pairs={{0,8},{8,16},{16,24},{24,32},{32,40},{40,48},{48,56},{56,64},{64,7... | collective-permute-start | bytes 24584 | tf_op jit(solution)/shard_map/ppermute | solution.py:38
  2.5 4.9 %collective-permute-start.1 = (f32[2,8,128]{2,1,0:T(8,128)S(1)}, f32[2,8,128]{2,1,0:T(8,128)S(1)}, u32[]{:S(2)}, u32[]{:S(2)}) collective-permute-start(f32[2,8,128]{2,1,0:T(8,128)S(1)} %get-tuple-element.55), channel_id=1, source_target_pairs={{0,120},{8,0},{16,8},{24,16},{32,24},{40,32},{48,40},{56,48},{64,5... | collective-permute-start | bytes 24584 | tf_op jit(solution)/shard_map/ppermute | solution.py:38
  7.4 9.3 %all_rows.1 = (bf16[2,3,32,128,128]{4,3,2,1,0:T(8,128)(2,1)}, bf16[2,3,16,16,128]{4,3,2,1,0:T(8,128)(2,1)}, bf16[2,3,16,16,128]{4,3,2,1,0:T(8,128)(2,1)}, bf16[4...) custom-call(bf16[2,3,128,32,128]{4,3,2,1,0:T(8,128)(2,1)} %e_ref.1), custom_call_target="tpu_custom_call" | custom-call | flops 1 | bytes 1 | tf_op jit(solution)/shard_map/all_rows/pallas_call | solution.py:106
  17.0 5.3 %collective-permute-start.3 = (bf16[44,128,128]{2,1,0:T(8,128)(2,1)}, bf16[44,128,128]{2,1,0:T(8,128)(2,1)}, u32[]{:S(2)}, u32[]{:S(2)}) collective-permute-start(bf16[44,128,128]{2,1,0:T(8,128)(2,1)} %get-tuple-element.28), channel_id=1, source_target_pairs={{0,120},{8,0},{16,8},{24,16},{32,24},{40,32},{48,40},{56,48},{64,5... | collective-permute-start | bytes 4325384 | tf_op jit(solution)/shard_map/ppermute | solution.py:38
  22.4 3.0 %collective-permute-done.4.left = bf16[2,3,16,16,128]{4,3,2,1,0:T(8,128)(2,1)S(1)} collective-permute-done((bf16[2,3,16,16,128]{4,3,2,1,0:T(8,128)(2,1)}, bf16[2,3,16,16,128]{4,3,2,1,0:T(8,128)(2,1)S(1)}, u32[]{:S(2)}, u32[]{:S(2)}) %collective-permute-start.4) | collective-permute-done | bytes 393248 | tf_op jit(solution)/shard_map/ppermute | solution.py:38
  25.6 3.0 %collective-permute-start.11 = (f32[2,48,8]{2,1,0:T(8,128)S(1)}, f32[2,48,8]{2,1,0:T(8,128)S(1)}, u32[]{:S(2)}, u32[]{:S(2)}) collective-permute-start(f32[2,48,8]{2,1,0:T(8,128)S(1)} %get-tuple-element.48), channel_id=1, source_target_pairs={{0,7},{1,0},{2,1},{3,2},{4,3},{5,4},{6,5},{7,6},{8,15},{9,8},{10,9... | collective-permute-start | bytes 9224 | tf_op jit(solution)/shard_map/ppermute | solution.py:38
  29.0 1.9 %fusion.8 = f32[6,256,128]{1,2,0:T(8,128)S(1)} fusion(s32[4096]{0:T(1024)S(1)} %get-tuple-element.60, pred[4096,128]{0,1:T(8,128)(4,1)S(1)} %iota_compare_fusion.1, bf16[6,4096]{1,0:T(8,128)(2,1)S(1)} %bitcast.34), kind=kOutput, calls=%fused_computation.9 | convolution fusion | flops 1614807040 | bytes 1376256 | tf_op jit(solution)/shard_map/rk,pkc->prc/dot_general | solution.py:404
  33.1 4.7 %collective-permute-done.8 = f32[4,2,32,128]{3,2,1,0:T(8,128)S(1)} collective-permute-done((f32[4,2,32,128]{3,2,1,0:T(8,128)S(1)}, f32[4,2,32,128]{3,2,1,0:T(8,128)S(1)}, u32[]{:S(2)}, u32[]{:S(2)}) %collective-permute-start.8) | collective-permute-done | bytes 131104 | tf_op jit(solution)/shard_map/ppermute | solution.py:412
  38.4 3.8 %collective-permute-done.9 = f32[2,2,32,128]{3,2,1,0:T(8,128)S(1)} collective-permute-done((f32[2,2,32,128]{3,2,1,0:T(8,128)S(1)}, f32[2,2,32,128]{3,2,1,0:T(8,128)S(1)}, u32[]{:S(2)}, u32[]{:S(2)}) %collective-permute-start.9) | collective-permute-done | bytes 65568 | tf_op jit(solution)/shard_map/ppermute | solution.py:412
  43.0 3.5 %broadcast_in_dim.55.depth_in = bf16[2,48,9,16,128]{4,3,2,1,0:T(8,128)(2,1)} broadcast(bf16[2,48,9,16]{3,2,1,0:T(8,128)(2,1)S(1)} %copy.13), dimensions={0,1,2,3} | broadcast | bytes 3566592 | tf_op jit(solution)/shard_map/broadcast_in_dim | solution.py:511
  46.5 2.1 %collective-permute-start.7 = (bf16[2,2,3,4,16,128]{5,4,3,2,1,0:T(8,128)(2,1)S(1)}, bf16[2,2,3,4,16,128]{5,4,3,2,1,0:T(8,128)(2,1)S(1)}, u32[]{:S(2)}, u32[]{:S(2)}) collective-permute-start(bf16[2,2,3,4,16,128]{5,4,3,2,1,0:T(8,128)(2,1)S(1)} %get-tuple-element.45), channel_id=1, source_target_pairs={{0,120},{8,0},{16,8},{24,16},{32,24},{40,32},{48,40},{56,48},{64,5... | collective-permute-start | bytes 589832 | tf_op jit(solution)/shard_map/ppermute | solution.py:38
  49.2 9.2 %collective-permute-done.7.corner_b = bf16[2,2,3,4,16,128]{5,4,3,2,1,0:T(8,128)(2,1)S(1)} collective-permute-done((bf16[2,2,3,4,16,128]{5,4,3,2,1,0:T(8,128)(2,1)S(1)}, bf16[2,2,3,4,16,128]{5,4,3,2,1,0:T(8,128)(2,1)S(1)}, u32[]{:S(2)}, u32[]{:S(2)}) %collective-permute-start.7) | collective-permute-done | bytes 196640 | tf_op jit(solution)/shard_map/ppermute | solution.py:38
  60.5 35.3 %forecast.1 = (bf16[2,3,32,128,128]{4,3,2,1,0:T(8,128)(2,1)}, f32[136,128]{1,0:T(8,128)}) custom-call(bf16[2,3,32,128,128]{4,3,2,1,0:T(8,128)(2,1)} %get-tuple-element.24.own, bf16[44,128,128]{2,1,0:T(8,128)(2,1)} %copy-done.2, bf16[44,128,128]{2,1,0:T(8,128)(2,1)} %collective-permute-done.3.bottom, bf16[2,3,16,16,128]{4,3,2,1,0:T(8,128)(2,1)} %copy-done, ...), custom_call_target="tpu_custom_call" | custom-call | flops 1 | bytes 1 | tf_op jit(solution)/shard_map/forecast/pallas_call | solution.py:318
  95.9 1.5 collective-permute-done.13
  98.3 2.4 %collective-permute-start.16 = (f32[136,128]{1,0:T(8,128)S(1)}, f32[136,128]{1,0:T(8,128)S(1)}, u32[]{:S(2)}, u32[]{:S(2)}) collective-permute-start(f32[136,128]{1,0:T(8,128)S(1)} %add.141), channel_id=1, source_target_pairs={{0,6},{1,7},{2,4},{3,5},{4,2},{5,3},{6,0},{7,1},{8,14},{9,15},{10,... | collective-permute-start | bytes 208904 | tf_op jit(solution)/shard_map/ppermute | solution.py:419
  102.4 1.4 collective-permute-done.16
  103.9 3.0 %collective-permute-done.15 = f32[136,128]{1,0:T(8,128)S(1)} collective-permute-done((f32[136,128]{1,0:T(8,128)S(1)}, f32[136,128]{1,0:T(8,128)S(1)}, u32[]{:S(2)}, u32[]{:S(2)}) %collective-permute-start.15) | collective-permute-done | bytes 69664 | tf_op jit(solution)/shard_map/ppermute | solution.py:419
  108.0 3.1 %collective-permute-start.17 = (f32[136,128]{1,0:T(8,128)S(1)}, f32[136,128]{1,0:T(8,128)S(1)}, u32[]{:S(2)}, u32[]{:S(2)}) collective-permute-start(f32[136,128]{1,0:T(8,128)S(1)} %add_add_fusion.2), channel_id=1, source_target_pairs={{0,8},{8,0},{16,24},{24,16},{32,40},{40,32},{48,56},{56,48},{64,72... | collective-permute-start | bytes 208904 | tf_op jit(solution)/shard_map/ppermute | solution.py:419
  111.1 1.4 collective-permute-done.19
  114.1 4.7 %collective-permute-start.22 = (f32[136,128]{1,0:T(8,128)S(1)}, f32[136,128]{1,0:T(8,128)S(1)}, u32[]{:S(2)}, u32[]{:S(2)}) collective-permute-start(f32[136,128]{1,0:T(8,128)S(1)} %add_add_fusion.1), channel_id=1, source_target_pairs={{0,96},{8,104},{16,112},{24,120},{32,64},{40,72},{48,80},{56,88},{... | collective-permute-start | bytes 208904 | tf_op jit(solution)/shard_map/ppermute | solution.py:419
  119.8 1.7 %collective-permute-done.22 = f32[136,128]{1,0:T(8,128)S(1)} collective-permute-done((f32[136,128]{1,0:T(8,128)S(1)}, f32[136,128]{1,0:T(8,128)S(1)}, u32[]{:S(2)}, u32[]{:S(2)}) %collective-permute-start.22) | collective-permute-done | bytes 69664 | tf_op jit(solution)/shard_map/ppermute | solution.py:419
  121.4 3.2 %collective-permute-done.21 = f32[136,128]{1,0:T(8,128)S(1)} collective-permute-done((f32[136,128]{1,0:T(8,128)S(1)}, f32[136,128]{1,0:T(8,128)S(1)}, u32[]{:S(2)}, u32[]{:S(2)}) %collective-permute-start.21) | collective-permute-done | bytes 69664 | tf_op jit(solution)/shard_map/ppermute | solution.py:419
  125.3 10.5 %transform.1.mix = bf16[128,256]{1,0:T(8,128)(2,1)} custom-call(f32[136,128]{1,0:T(8,128)} %add_add_fusion.total), custom_call_target="tpu_custom_call" | custom-call | flops 1 | bytes 1 | tf_op jit(solution)/shard_map/transform/pallas_call | solution.py:474
  135.8 14.2 %analysis.1 = bf16[2,3,128,32,128]{4,3,2,1,0:T(8,128)(2,1)} custom-call(bf16[2,3,32,128,128]{4,3,2,1,0:T(8,128)(2,1)} %get-tuple-element.41.state, bf16[128,256]{1,0:T(8,128)(2,1)} %transform.1.mix), custom_call_target="tpu_custom_call" | custom-call | flops 1 | bytes 1 | tf_op jit(solution)/shard_map/analysis/pallas_call | solution.py:371
  (91 shorter events, 14.9 us)
Async XLA Ops:
  0.0 28.5 %copy-start.8 = (s32[1,1,32,128]{3,2,1,0:T(8,128)S(1)}, s32[1,1,32,128]{3,2,1,0:T(8,128)}, u32[]{:S(2)}) copy-start(s32[1,1,32,128]{3,2,1,0:T(8,128)} %param.9) | copy-start | bytes 49156
  0.8 16.1 %collective-permute-start = (f32[2,8,128]{2,1,0:T(8,128)S(1)}, f32[2,8,128]{2,1,0:T(8,128)S(1)}, u32[]{:S(2)}, u32[]{:S(2)}) collective-permute-start(f32[2,8,128]{2,1,0:T(8,128)S(1)} %get-tuple-element.54), channel_id=1, source_target_pairs={{0,8},{8,16},{16,24},{24,32},{32,40},{40,48},{48,56},{56,64},{64,7... | collective-permute-start | bytes 24584 | tf_op jit(solution)/shard_map/ppermute | solution.py:38
  2.5 14.5 %collective-permute-start.1 = (f32[2,8,128]{2,1,0:T(8,128)S(1)}, f32[2,8,128]{2,1,0:T(8,128)S(1)}, u32[]{:S(2)}, u32[]{:S(2)}) collective-permute-start(f32[2,8,128]{2,1,0:T(8,128)S(1)} %get-tuple-element.55), channel_id=1, source_target_pairs={{0,120},{8,0},{16,8},{24,16},{32,24},{40,32},{48,40},{56,48},{64,5... | collective-permute-start | bytes 24584 | tf_op jit(solution)/shard_map/ppermute | solution.py:38
  16.7 8.6 %collective-permute-start.4 = (bf16[2,3,16,16,128]{4,3,2,1,0:T(8,128)(2,1)}, bf16[2,3,16,16,128]{4,3,2,1,0:T(8,128)(2,1)S(1)}, u32[]{:S(2)}, u32[]{:S(2)}) collective-permute-start(bf16[2,3,16,16,128]{4,3,2,1,0:T(8,128)(2,1)} %get-tuple-element.30), channel_id=1, source_target_pairs={{0,1},{1,2},{2,3},{3,4},{4,5},{5,6},{6,7},{7,0},{8,9},{9,10},{10,1... | collective-permute-start | bytes 1179656 | tf_op jit(solution)/shard_map/ppermute | solution.py:38
  16.9 42.3 %collective-permute-start.2 = (bf16[44,128,128]{2,1,0:T(8,128)(2,1)}, bf16[44,128,128]{2,1,0:T(8,128)(2,1)S(1)}, u32[]{:S(2)}, u32[]{:S(2)}) collective-permute-start(bf16[44,128,128]{2,1,0:T(8,128)(2,1)} %get-tuple-element.27), channel_id=1, source_target_pairs={{0,8},{8,16},{16,24},{24,32},{32,40},{40,48},{48,56},{56,64},{64,7... | collective-permute-start | bytes 4325384 | tf_op jit(solution)/shard_map/ppermute | solution.py:38
  17.0 42.2 %collective-permute-start.3 = (bf16[44,128,128]{2,1,0:T(8,128)(2,1)}, bf16[44,128,128]{2,1,0:T(8,128)(2,1)}, u32[]{:S(2)}, u32[]{:S(2)}) collective-permute-start(bf16[44,128,128]{2,1,0:T(8,128)(2,1)} %get-tuple-element.28), channel_id=1, source_target_pairs={{0,120},{8,0},{16,8},{24,16},{32,24},{40,32},{48,40},{56,48},{64,5... | collective-permute-start | bytes 4325384 | tf_op jit(solution)/shard_map/ppermute | solution.py:38
  25.6 7.0 %collective-permute-start.10 = (f32[2,48,8]{2,1,0:T(8,128)S(1)}, f32[2,48,8]{2,1,0:T(8,128)S(1)}, u32[]{:S(2)}, u32[]{:S(2)}) collective-permute-start(f32[2,48,8]{2,1,0:T(8,128)S(1)} %get-tuple-element.47), channel_id=1, source_target_pairs={{0,1},{1,2},{2,3},{3,4},{4,5},{5,6},{6,7},{7,0},{8,9},{9,10},{10,1... | collective-permute-start | bytes 9224 | tf_op jit(solution)/shard_map/ppermute | solution.py:38
  25.6 7.3 %collective-permute-start.11 = (f32[2,48,8]{2,1,0:T(8,128)S(1)}, f32[2,48,8]{2,1,0:T(8,128)S(1)}, u32[]{:S(2)}, u32[]{:S(2)}) collective-permute-start(f32[2,48,8]{2,1,0:T(8,128)S(1)} %get-tuple-element.48), channel_id=1, source_target_pairs={{0,7},{1,0},{2,1},{3,2},{4,3},{5,4},{6,5},{7,6},{8,15},{9,8},{10,9... | collective-permute-start | bytes 9224 | tf_op jit(solution)/shard_map/ppermute | solution.py:38
  31.3 6.6 %collective-permute-start.8 = (f32[4,2,32,128]{3,2,1,0:T(8,128)S(1)}, f32[4,2,32,128]{3,2,1,0:T(8,128)S(1)}, u32[]{:S(2)}, u32[]{:S(2)}) collective-permute-start(f32[4,2,32,128]{3,2,1,0:T(8,128)S(1)} %slice.87), channel_id=1, source_target_pairs={{0,4},{1,5},{2,6},{3,7},{4,0},{5,1},{6,2},{7,3},{8,12},{9,13},{10,... | collective-permute-start | bytes 393224 | tf_op jit(solution)/shard_map/ppermute | solution.py:412
  32.5 13.9 %collective-permute-start.5 = (bf16[2,3,16,16,128]{4,3,2,1,0:T(8,128)(2,1)S(1)}, bf16[2,3,16,16,128]{4,3,2,1,0:T(8,128)(2,1)S(1)}, u32[]{:S(2)}, u32[]{:S(2)}) collective-permute-start(bf16[2,3,16,16,128]{4,3,2,1,0:T(8,128)(2,1)S(1)} %copy-done.9), channel_id=1, source_target_pairs={{0,7},{1,0},{2,1},{3,2},{4,3},{5,4},{6,5},{7,6},{8,15},{9,8},{10,9... | collective-permute-start | bytes 1179656 | tf_op jit(solution)/shard_map/ppermute | solution.py:38
  37.9 4.3 %collective-permute-start.9 = (f32[2,2,32,128]{3,2,1,0:T(8,128)S(1)}, f32[2,2,32,128]{3,2,1,0:T(8,128)S(1)}, u32[]{:S(2)}, u32[]{:S(2)}) collective-permute-start(f32[2,2,32,128]{3,2,1,0:T(8,128)S(1)} %slice.89), channel_id=1, source_target_pairs={{0,2},{1,3},{2,0},{3,1},{4,6},{5,7},{6,4},{7,5},{8,10},{9,11},{10,... | collective-permute-start | bytes 196616 | tf_op jit(solution)/shard_map/ppermute | solution.py:412
  46.4 2.2 %collective-permute-start.12 = (f32[1,2,32,128]{3,2,1,0:T(8,128)S(1)}, f32[1,2,32,128]{3,2,1,0:T(8,128)S(1)}, u32[]{:S(2)}, u32[]{:S(2)}) collective-permute-start(f32[1,2,32,128]{3,2,1,0:T(8,128)S(1)} %slice.77), channel_id=1, source_target_pairs={{0,1},{1,0},{2,3},{3,2},{4,5},{5,4},{6,7},{7,6},{8,9},{9,8},{10,11... | collective-permute-start | bytes 98312 | tf_op jit(solution)/shard_map/ppermute | solution.py:412
  46.5 11.9 %collective-permute-start.7 = (bf16[2,2,3,4,16,128]{5,4,3,2,1,0:T(8,128)(2,1)S(1)}, bf16[2,2,3,4,16,128]{5,4,3,2,1,0:T(8,128)(2,1)S(1)}, u32[]{:S(2)}, u32[]{:S(2)}) collective-permute-start(bf16[2,2,3,4,16,128]{5,4,3,2,1,0:T(8,128)(2,1)S(1)} %get-tuple-element.45), channel_id=1, source_target_pairs={{0,120},{8,0},{16,8},{24,16},{32,24},{40,32},{48,40},{56,48},{64,5... | collective-permute-start | bytes 589832 | tf_op jit(solution)/shard_map/ppermute | solution.py:38
  48.6 10.6 %collective-permute-start.6 = (bf16[2,2,3,4,16,128]{5,4,3,2,1,0:T(8,128)(2,1)S(1)}, bf16[2,2,3,4,16,128]{5,4,3,2,1,0:T(8,128)(2,1)S(1)}, u32[]{:S(2)}, u32[]{:S(2)}) collective-permute-start(bf16[2,2,3,4,16,128]{5,4,3,2,1,0:T(8,128)(2,1)S(1)} %get-tuple-element.46), channel_id=1, source_target_pairs={{0,8},{8,16},{16,24},{24,32},{32,40},{40,48},{48,56},{56,64},{64,7... | collective-permute-start | bytes 589832 | tf_op jit(solution)/shard_map/ppermute | solution.py:38
  95.8 1.6 %collective-permute-start.13 = (f32[136,128]{1,0:T(8,128)}, f32[136,128]{1,0:T(8,128)S(1)}, u32[]{:S(2)}, u32[]{:S(2)}) collective-permute-start(f32[136,128]{1,0:T(8,128)} %get-tuple-element.42), channel_id=1, source_target_pairs={{0,1},{1,0},{2,3},{3,2},{4,5},{5,4},{6,7},{7,6},{8,9},{9,8},{10,11... | collective-permute-start | bytes 208904 | tf_op jit(solution)/shard_map/ppermute | solution.py:419
  98.3 5.6 %collective-permute-start.16 = (f32[136,128]{1,0:T(8,128)S(1)}, f32[136,128]{1,0:T(8,128)S(1)}, u32[]{:S(2)}, u32[]{:S(2)}) collective-permute-start(f32[136,128]{1,0:T(8,128)S(1)} %add.141), channel_id=1, source_target_pairs={{0,6},{1,7},{2,4},{3,5},{4,2},{5,3},{6,0},{7,1},{8,14},{9,15},{10,... | collective-permute-start | bytes 208904 | tf_op jit(solution)/shard_map/ppermute | solution.py:419
  100.7 6.2 %collective-permute-start.15 = (f32[136,128]{1,0:T(8,128)S(1)}, f32[136,128]{1,0:T(8,128)S(1)}, u32[]{:S(2)}, u32[]{:S(2)}) collective-permute-start(f32[136,128]{1,0:T(8,128)S(1)} %add.141), channel_id=1, source_target_pairs={{0,4},{1,5},{2,6},{3,7},{4,0},{5,1},{6,2},{7,3},{8,12},{9,13},{10,... | collective-permute-start | bytes 208904 | tf_op jit(solution)/shard_map/ppermute | solution.py:419
  101.3 5.5 %collective-permute-start.14 = (f32[136,128]{1,0:T(8,128)S(1)}, f32[136,128]{1,0:T(8,128)S(1)}, u32[]{:S(2)}, u32[]{:S(2)}) collective-permute-start(f32[136,128]{1,0:T(8,128)S(1)} %add.141), channel_id=1, source_target_pairs={{0,2},{1,3},{2,0},{3,1},{4,6},{5,7},{6,4},{7,5},{8,10},{9,11},{10,... | collective-permute-start | bytes 208904 | tf_op jit(solution)/shard_map/ppermute | solution.py:419
  106.9 5.6 %collective-permute-start.19 = (f32[136,128]{1,0:T(8,128)S(1)}, f32[136,128]{1,0:T(8,128)S(1)}, u32[]{:S(2)}, u32[]{:S(2)}) collective-permute-start(f32[136,128]{1,0:T(8,128)S(1)} %add_add_fusion.2), channel_id=1, source_target_pairs={{0,24},{8,16},{16,8},{24,0},{32,56},{40,48},{48,40},{56,32},{64,88... | collective-permute-start | bytes 208904 | tf_op jit(solution)/shard_map/ppermute | solution.py:419
  108.0 5.8 %collective-permute-start.18 = (f32[136,128]{1,0:T(8,128)S(1)}, f32[136,128]{1,0:T(8,128)S(1)}, u32[]{:S(2)}, u32[]{:S(2)}) collective-permute-start(f32[136,128]{1,0:T(8,128)S(1)} %add_add_fusion.2), channel_id=1, source_target_pairs={{0,16},{8,24},{16,0},{24,8},{32,48},{40,56},{48,32},{56,40},{64,80... | collective-permute-start | bytes 208904 | tf_op jit(solution)/shard_map/ppermute | solution.py:419
  108.0 6.1 %collective-permute-start.17 = (f32[136,128]{1,0:T(8,128)S(1)}, f32[136,128]{1,0:T(8,128)S(1)}, u32[]{:S(2)}, u32[]{:S(2)}) collective-permute-start(f32[136,128]{1,0:T(8,128)S(1)} %add_add_fusion.2), channel_id=1, source_target_pairs={{0,8},{8,0},{16,24},{24,16},{32,40},{40,32},{48,56},{56,48},{64,72... | collective-permute-start | bytes 208904 | tf_op jit(solution)/shard_map/ppermute | solution.py:419
  114.1 7.3 %collective-permute-start.22 = (f32[136,128]{1,0:T(8,128)S(1)}, f32[136,128]{1,0:T(8,128)S(1)}, u32[]{:S(2)}, u32[]{:S(2)}) collective-permute-start(f32[136,128]{1,0:T(8,128)S(1)} %add_add_fusion.1), channel_id=1, source_target_pairs={{0,96},{8,104},{16,112},{24,120},{32,64},{40,72},{48,80},{56,88},{... | collective-permute-start | bytes 208904 | tf_op jit(solution)/shard_map/ppermute | solution.py:419
  118.8 5.8 %collective-permute-start.21 = (f32[136,128]{1,0:T(8,128)S(1)}, f32[136,128]{1,0:T(8,128)S(1)}, u32[]{:S(2)}, u32[]{:S(2)}) collective-permute-start(f32[136,128]{1,0:T(8,128)S(1)} %add_add_fusion.1), channel_id=1, source_target_pairs={{0,64},{8,72},{16,80},{24,88},{32,96},{40,104},{48,112},{56,120},{... | collective-permute-start | bytes 208904 | tf_op jit(solution)/shard_map/ppermute | solution.py:419
  118.8 5.8 %collective-permute-start.20 = (f32[136,128]{1,0:T(8,128)S(1)}, f32[136,128]{1,0:T(8,128)S(1)}, u32[]{:S(2)}, u32[]{:S(2)}) collective-permute-start(f32[136,128]{1,0:T(8,128)S(1)} %add_add_fusion.1), channel_id=1, source_target_pairs={{0,32},{8,40},{16,48},{24,56},{32,0},{40,8},{48,16},{56,24},{64,96... | collective-permute-start | bytes 208904 | tf_op jit(solution)/shard_map/ppermute | solution.py:419
  (10 other events, 133.1 us)

commit v5 on v4

--- a/solution.py
+++ b/solution.py
@@ -15,12 +15,11 @@
 SEGMENTS = 16
 POSITIONS = WIDE_COLS // SEGMENTS
 LINE = 40
-PANEL = 8
+PANEL = 32
 LAYERS = 2
 HALF = 0.15
 TURN = 0.12
 COUPLING = 0.5
-VMEM = 60 * 1024 * 1024
 
 F32 = jnp.float32
 BF16 = jnp.bfloat16
@@ -29,8 +28,8 @@
 COST = pl.CostEstimate(flops=1, bytes_accessed=1, transcendentals=0)
 
 
-def params():
-    return pltpu.CompilerParams(vmem_limit_bytes=VMEM)
+def params(mib):
+    return pltpu.CompilerParams(vmem_limit_bytes=mib * 1024 * 1024)
 
 
 def shift(x, axis, by):
@@ -49,7 +48,7 @@
                 planes[pl.ds((4 * m + k) * pitch + lo, 8), :] = plane[lo:lo + 8]
         return carry
 
-    lax.fori_loop(0, MEMBERS // 4, spread, 0, unroll=2)
+    lax.fori_loop(0, MEMBERS // 4, spread, 0, unroll=8)
     for x in rows:
         put(x, planes[pl.ds(x, MEMBERS, stride=pitch), :].astype(BF16).T)
 
@@ -110,7 +109,7 @@
         out_specs=[spec(tile), spec(side), spec(side), edge_spec, edge_spec],
         out_shape=[whole(tile), whole(side), whole(side), edge_shape, edge_shape],
         scratch_shapes=[pltpu.VMEM((MEMBERS * (ROWS + 1), COLS), F32)],
-        compiler_params=params(),
+        compiler_params=params(18),
         cost_estimate=COST,
         name="all_rows",
     )(ensemble)
@@ -186,7 +185,7 @@
                     put_flux(l, r, depth[l, r] * value)
             return carry
 
-        lax.fori_loop(0, WIDE_ROWS // 2, unpack, 0)
+        lax.fori_loop(0, WIDE_ROWS // 2, unpack, 0, unroll=2)
 
     mid = slice(1, POSITIONS + 1)
 
@@ -259,7 +258,7 @@
                 raw[l, c, r] = value.astype(BF16)
                 return carry
 
-            lax.fori_loop(0, ROWS, pack, 0, unroll=2)
+            lax.fori_loop(0, ROWS, pack, 0, unroll=4)
             done.append(
                 pltpu.make_async_copy(
                     raw.at[l, c, pl.ds(0, ROWS)], out.at[l, c], sems.at[55 + 3 * l + c]
@@ -296,7 +295,7 @@
         acc[...] += zt * (pull[pl.ds(x, 1), :] - mean * w)
         return carry
 
-    lax.fori_loop(0, ROWS, body, 0, unroll=4)
+    lax.fori_loop(0, ROWS, body, 0, unroll=8)
 
     def multiply(x, part):
         a = jnp.concatenate([left[0, 2 * x], left[0, 2 * x + 1]], axis=1)
@@ -306,7 +305,7 @@
         low = jnp.dot(b, z[:, 0:n], preferred_element_type=F32)
         return part + (main[:, 0:n] + (main[:, n:2 * n] + low))
 
-    total[0:n, :] = lax.fori_loop(0, ROWS // 2, multiply, jnp.zeros((n, n), F32), unroll=2)
+    total[0:n, :] = lax.fori_loop(0, ROWS // 2, multiply, jnp.zeros((n, n), F32), unroll=8)
     total[n:n + 8, :] = jnp.broadcast_to(jnp.sum(acc[...].T, axis=0, keepdims=True), (8, n))
 
 
@@ -337,7 +336,7 @@
             pltpu.VMEM((MEMBERS, COLS), F32),
             pltpu.SemaphoreType.DMA((61,)),
         ],
-        compiler_params=params(),
+        compiler_params=params(47),
         cost_estimate=COST,
         name="forecast",
     )(*operands)
@@ -357,14 +356,14 @@
         planes[pl.ds(2 * x + 1, MEMBERS, stride=pitch), :] = mixed[:, COLS:]
         return carry
 
-    lax.fori_loop(0, ROWS // 2, body, 0, unroll=2)
+    lax.fori_loop(0, ROWS // 2, body, 0, unroll=16)
 
     def gather(m, carry):
         for k in range(4):
             out[0, 0, 4 * m + k] = planes[pl.ds((4 * m + k) * pitch, ROWS), :].astype(BF16)
         return carry
 
-    lax.fori_loop(0, MEMBERS // 4, gather, 0, unroll=2)
+    lax.fori_loop(0, MEMBERS // 4, gather, 0, unroll=16)
 
 
 def analyse(state, mix):
@@ -378,7 +377,7 @@
         out_specs=pl.BlockSpec((1, 1, MEMBERS, ROWS, COLS), lambda i, j: (i, j, 0, 0, 0)),
         out_shape=jax.ShapeDtypeStruct((LAYERS, 3, MEMBERS, ROWS, COLS), BF16),
         scratch_shapes=[pltpu.VMEM((MEMBERS * (ROWS + 1), COLS), F32)],
-        compiler_params=params(),
+        compiler_params=params(14),
         cost_estimate=COST,
         name="analysis",
     )(state, mix)
@@ -480,7 +479,7 @@
             pltpu.VMEM((MEMBERS, 2 * MEMBERS), F32),
             pltpu.VMEM((MEMBERS, MEMBERS), F32),
         ],
-        compiler_params=params(),
+        compiler_params=params(8),
         cost_estimate=COST,
         name="transform",
     )(total)

time: 150 us -> 135 us (0.900)
  Pallas kernels: 69.4 us -> 49.2 us
  local copies, waits for them, and re-layouts: 7.84 us -> 14.3 us
    pallas_call x1, Pallas kernels: 14.2 us -> 6.6 us  [analyse(): pl.pallas_call(analysis_kernel, grid=(LAYERS, 3), in_specs=[pl.BlockSpec(...]
    unnamed x22 -> x16, local copies, waits for them, and re-layouts: 1.26 us -> 8.28 us
    pallas_call x1, Pallas kernels: 10.5 us -> 4.88 us  [make_mix(): pl.pallas_call(transform_kernel, in_specs=[vmem], out_specs=vmem, out_sha...]
    pallas_call x1, Pallas kernels: 9.33 us -> 5.18 us  [all_rows(): pl.pallas_call(kernel, grid=(LAYERS, 3), in_specs=[E_BLOCK], out_specs=[s...]
    pallas_call x1, Pallas kernels: 35.3 us -> 32.5 us  [forecast(): pl.pallas_call(forecast_kernel, in_specs=[anywhere] * 8 + [pl.BlockSpec(m...]
  transfers between devices with their start and end apart: 23 -> 23, of which waited for: 13 -> 13; matrix products, arithmetic and copies ran while one was open for 6% -> 7% of each run, Pallas kernels for 6% -> 4%
where the time goes in v5:
time: 135 us
  Pallas kernels  49.2 us (36%)
  waiting for transfers between devices  35.5 us (26%)
  starting transfers between devices  32.2 us (24%)
  local copies, waits for them, and re-layouts  14.3 us (11%)
  matrix products  1.92 us (1%)
  other arithmetic  1.74 us (1%)
    pallas_call x1, Pallas kernels, forecast(): pl.pallas_call(forecast_kernel, in_specs=[anywhere] * 8 + [pl.BlockSpec(m...  32.5 us
    ppermute x10, starting transfers between devices, shift(): return lax.ppermute(x, axis, [(i, (i + by) % n) for i in range(n)])  17.4 us
    ppermute x10, starting transfers between devices, other(): lax.ppermute(x, axis, [(i, i ^ k) for i in range(lax.axis_size(axis))])  14.1 us
    ppermute x10, waiting for transfers between devices, other(): lax.ppermute(x, axis, [(i, i ^ k) for i in range(lax.axis_size(axis))])  13.6 us
    ppermute x10, waiting for transfers between devices, shift(): return lax.ppermute(x, axis, [(i, (i + by) % n) for i in range(n)])  13.6 us
    unnamed x16, local copies, waits for them, and re-layouts  8.28 us
    ppermute x3, waiting for transfers between devices, observed_cells(): field = field[:bit] + lax.ppermute(field[bit:], 'gy', swap)  8.25 us
    pallas_call x1, Pallas kernels, analyse(): pl.pallas_call(analysis_kernel, grid=(LAYERS, 3), in_specs=[pl.BlockSpec(...  6.6 us
  transfers between devices with their start and end apart: 23, of which 13 were waited for; matrix products, arithmetic and copies ran while one was open for 7% of the time, Pallas kernels for 4%

profile of v5, /device:TPU:0, one launch (start us, length us, event | category | flops | bytes accessed | tf_op | source)
XLA Modules:
  0.0 135.1 jit_solution(6853042701260560243)
XLA Ops:
  0.8 1.7 %collective-permute-start = (f32[2,8,128]{2,1,0:T(8,128)S(1)}, f32[2,8,128]{2,1,0:T(8,128)S(1)}, u32[]{:S(2)}, u32[]{:S(2)}) collective-permute-start(f32[2,8,128]{2,1,0:T(8,128)S(1)} %get-tuple-element.54), channel_id=1, source_target_pairs={{0,8},{8,16},{16,24},{24,32},{32,40},{40,48},{48,56},{56,64},{64,7... | collective-permute-start | bytes 24584 | tf_op jit(solution)/shard_map/ppermute | solution.py:37
  2.4 4.9 %collective-permute-start.1 = (f32[2,8,128]{2,1,0:T(8,128)S(1)}, f32[2,8,128]{2,1,0:T(8,128)S(1)}, u32[]{:S(2)}, u32[]{:S(2)}) collective-permute-start(f32[2,8,128]{2,1,0:T(8,128)S(1)} %get-tuple-element.55), channel_id=1, source_target_pairs={{0,120},{8,0},{16,8},{24,16},{32,24},{40,32},{48,40},{56,48},{64,5... | collective-permute-start | bytes 24584 | tf_op jit(solution)/shard_map/ppermute | solution.py:37
  7.4 2.8 %copy-done = bf16[2,3,128,32,128]{4,3,2,1,0:T(8,128)(2,1)S(1)} copy-done((bf16[2,3,128,32,128]{4,3,2,1,0:T(8,128)(2,1)S(1)}, bf16[2,3,128,32,128]{4,3,2,1,0:T(8,128)(2,1)}, u32[]{:S(2)}) %copy-start) | copy-done | bytes 6291480
  10.1 5.2 %all_rows.1 = (bf16[2,3,32,128,128]{4,3,2,1,0:T(8,128)(2,1)S(1)}, bf16[2,3,16,16,128]{4,3,2,1,0:T(8,128)(2,1)S(1)}, bf16[2,3,16,16,128]{4,3,2,1,0:T(8,128)(2,1)S...) custom-call(bf16[2,3,128,32,128]{4,3,2,1,0:T(8,128)(2,1)S(1)} %copy-done), custom_call_target="tpu_custom_call" | custom-call | flops 1 | bytes 1 | tf_op jit(solution)/shard_map/all_rows/pallas_call | solution.py:105
  15.3 2.7 %copy-done.1 = bf16[2,3,32,128,128]{4,3,2,1,0:T(8,128)(2,1)} copy-done((bf16[2,3,32,128,128]{4,3,2,1,0:T(8,128)(2,1)}, bf16[2,3,32,128,128]{4,3,2,1,0:T(8,128)(2,1)S(1)}, u32[]{:S(2)}) %copy-start.1) | copy-done | bytes 6291480
  18.3 5.3 %collective-permute-start.3 = (bf16[44,128,128]{2,1,0:T(8,128)(2,1)}, bf16[44,128,128]{2,1,0:T(8,128)(2,1)}, u32[]{:S(2)}, u32[]{:S(2)}) collective-permute-start(bf16[44,128,128]{2,1,0:T(8,128)(2,1)} %get-tuple-element.28), channel_id=1, source_target_pairs={{0,120},{8,0},{16,8},{24,16},{32,24},{40,32},{48,40},{56,48},{64,5... | collective-permute-start | bytes 4325384 | tf_op jit(solution)/shard_map/ppermute | solution.py:37
  23.6 2.8 %collective-permute-done.4.left = bf16[2,3,16,16,128]{4,3,2,1,0:T(8,128)(2,1)S(1)} collective-permute-done((bf16[2,3,16,16,128]{4,3,2,1,0:T(8,128)(2,1)S(1)}, bf16[2,3,16,16,128]{4,3,2,1,0:T(8,128)(2,1)S(1)}, u32[]{:S(2)}, u32[]{:S(2)}) %collective-permute-start.4) | collective-permute-done | bytes 393248 | tf_op jit(solution)/shard_map/ppermute | solution.py:37
  27.3 3.0 %collective-permute-start.11 = (f32[2,48,8]{2,1,0:T(8,128)}, f32[2,48,8]{2,1,0:T(8,128)}, u32[]{:S(2)}, u32[]{:S(2)}) collective-permute-start(f32[2,48,8]{2,1,0:T(8,128)} %get-tuple-element.48), channel_id=1, source_target_pairs={{0,7},{1,0},{2,1},{3,2},{4,3},{5,4},{6,5},{7,6},{8,15},{9,8},{10,9... | collective-permute-start | bytes 9224 | tf_op jit(solution)/shard_map/ppermute | solution.py:37
  30.7 1.9 %fusion.8 = f32[6,256,128]{1,2,0:T(8,128)S(1)} fusion(s32[4096]{0:T(1024)S(1)} %get-tuple-element.60, pred[4096,128]{0,1:T(8,128)(4,1)S(1)} %iota_compare_fusion.1, bf16[6,4096]{1,0:T(8,128)(2,1)S(1)} %bitcast.34), kind=kOutput, calls=%fused_computation.9 | convolution fusion | flops 1614807040 | bytes 1376256 | tf_op jit(solution)/shard_map/rk,pkc->prc/dot_general | solution.py:403
  35.0 4.5 %collective-permute-done.8 = f32[4,2,32,128]{3,2,1,0:T(8,128)S(1)} collective-permute-done((f32[4,2,32,128]{3,2,1,0:T(8,128)S(1)}, f32[4,2,32,128]{3,2,1,0:T(8,128)S(1)}, u32[]{:S(2)}, u32[]{:S(2)}) %collective-permute-start.8) | collective-permute-done | bytes 131104 | tf_op jit(solution)/shard_map/ppermute | solution.py:411
  40.1 3.8 %collective-permute-done.9 = f32[2,2,32,128]{3,2,1,0:T(8,128)S(1)} collective-permute-done((f32[2,2,32,128]{3,2,1,0:T(8,128)S(1)}, f32[2,2,32,128]{3,2,1,0:T(8,128)S(1)}, u32[]{:S(2)}, u32[]{:S(2)}) %collective-permute-start.9) | collective-permute-done | bytes 65568 | tf_op jit(solution)/shard_map/ppermute | solution.py:411
  44.0 3.5 %broadcast_in_dim.55.depth_in = bf16[2,48,9,16,128]{4,3,2,1,0:T(8,128)(2,1)} broadcast(bf16[2,48,9,16]{3,2,1,0:T(8,128)(2,1)S(1)} %copy.13), dimensions={0,1,2,3} | broadcast | bytes 3566592 | tf_op jit(solution)/shard_map/broadcast_in_dim | solution.py:510
  47.6 2.1 %collective-permute-start.7 = (bf16[2,2,3,4,16,128]{5,4,3,2,1,0:T(8,128)(2,1)S(1)}, bf16[2,2,3,4,16,128]{5,4,3,2,1,0:T(8,128)(2,1)S(1)}, u32[]{:S(2)}, u32[]{:S(2)}) collective-permute-start(bf16[2,2,3,4,16,128]{5,4,3,2,1,0:T(8,128)(2,1)S(1)} %get-tuple-element.45), channel_id=1, source_target_pairs={{0,120},{8,0},{16,8},{24,16},{32,24},{40,32},{48,40},{56,48},{64,5... | collective-permute-start | bytes 589832 | tf_op jit(solution)/shard_map/ppermute | solution.py:37
  49.7 10.1 %collective-permute-done.7.corner_b = bf16[2,2,3,4,16,128]{5,4,3,2,1,0:T(8,128)(2,1)S(1)} collective-permute-done((bf16[2,2,3,4,16,128]{5,4,3,2,1,0:T(8,128)(2,1)S(1)}, bf16[2,2,3,4,16,128]{5,4,3,2,1,0:T(8,128)(2,1)S(1)}, u32[]{:S(2)}, u32[]{:S(2)}) %collective-permute-start.7) | collective-permute-done | bytes 196640 | tf_op jit(solution)/shard_map/ppermute | solution.py:37
  60.5 32.5 %forecast.1 = (bf16[2,3,32,128,128]{4,3,2,1,0:T(8,128)(2,1)}, f32[136,128]{1,0:T(8,128)S(1)}) custom-call(bf16[2,3,32,128,128]{4,3,2,1,0:T(8,128)(2,1)} %copy-done.1, bf16[44,128,128]{2,1,0:T(8,128)(2,1)S(1)} %collective-permute-done.2.top, bf16[44,128,128]{2,1,0:T(8,128)(2,1)} %collective-permute-done.3.bottom, ...), custom_call_target="tpu_custom_call" | custom-call | flops 1 | bytes 1 | tf_op jit(solution)/shard_map/forecast/pallas_call | solution.py:317
  94.4 2.5 %collective-permute-start.16 = (f32[136,128]{1,0:T(8,128)S(1)}, f32[136,128]{1,0:T(8,128)S(1)}, u32[]{:S(2)}, u32[]{:S(2)}) collective-permute-start(f32[136,128]{1,0:T(8,128)S(1)} %add.141), channel_id=1, source_target_pairs={{0,6},{1,7},{2,4},{3,5},{4,2},{5,3},{6,0},{7,1},{8,14},{9,15},{10,... | collective-permute-start | bytes 208904 | tf_op jit(solution)/shard_map/ppermute | solution.py:418
  100.0 3.1 %collective-permute-done.15 = f32[136,128]{1,0:T(8,128)S(1)} collective-permute-done((f32[136,128]{1,0:T(8,128)S(1)}, f32[136,128]{1,0:T(8,128)S(1)}, u32[]{:S(2)}, u32[]{:S(2)}) %collective-permute-start.15) | collective-permute-done | bytes 69664 | tf_op jit(solution)/shard_map/ppermute | solution.py:418
  104.2 3.0 %collective-permute-start.17 = (f32[136,128]{1,0:T(8,128)S(1)}, f32[136,128]{1,0:T(8,128)S(1)}, u32[]{:S(2)}, u32[]{:S(2)}) collective-permute-start(f32[136,128]{1,0:T(8,128)S(1)} %add_add_fusion.2), channel_id=1, source_target_pairs={{0,8},{8,0},{16,24},{24,16},{32,40},{40,32},{48,56},{56,48},{64,72... | collective-permute-start | bytes 208904 | tf_op jit(solution)/shard_map/ppermute | solution.py:418
  110.3 4.7 %collective-permute-start.22 = (f32[136,128]{1,0:T(8,128)S(1)}, f32[136,128]{1,0:T(8,128)S(1)}, u32[]{:S(2)}, u32[]{:S(2)}) collective-permute-start(f32[136,128]{1,0:T(8,128)S(1)} %add_add_fusion.1), channel_id=1, source_target_pairs={{0,96},{8,104},{16,112},{24,120},{32,64},{40,72},{48,80},{56,88},{... | collective-permute-start | bytes 208904 | tf_op jit(solution)/shard_map/ppermute | solution.py:418
  116.0 1.7 %collective-permute-done.22 = f32[136,128]{1,0:T(8,128)S(1)} collective-permute-done((f32[136,128]{1,0:T(8,128)S(1)}, f32[136,128]{1,0:T(8,128)S(1)}, u32[]{:S(2)}, u32[]{:S(2)}) %collective-permute-start.22) | collective-permute-done | bytes 69664 | tf_op jit(solution)/shard_map/ppermute | solution.py:418
  117.6 3.2 %collective-permute-done.21 = f32[136,128]{1,0:T(8,128)S(1)} collective-permute-done((f32[136,128]{1,0:T(8,128)S(1)}, f32[136,128]{1,0:T(8,128)S(1)}, u32[]{:S(2)}, u32[]{:S(2)}) %collective-permute-start.21) | collective-permute-done | bytes 69664 | tf_op jit(solution)/shard_map/ppermute | solution.py:418
  120.9 4.9 %transform.1.mix = bf16[128,256]{1,0:T(8,128)(2,1)S(1)} custom-call(f32[136,128]{1,0:T(8,128)S(1)} %add_add_fusion.total), custom_call_target="tpu_custom_call" | custom-call | flops 1 | bytes 1 | tf_op jit(solution)/shard_map/transform/pallas_call | solution.py:473
  125.8 2.8 %copy-done.2 = bf16[2,3,32,128,128]{4,3,2,1,0:T(8,128)(2,1)S(1)} copy-done((bf16[2,3,32,128,128]{4,3,2,1,0:T(8,128)(2,1)S(1)}, bf16[2,3,32,128,128]{4,3,2,1,0:T(8,128)(2,1)}, u32[]{:S(2)}) %copy-start.2) | copy-done | bytes 6291480
  128.5 6.6 %analysis.1 = bf16[2,3,128,32,128]{4,3,2,1,0:T(8,128)(2,1)} custom-call(bf16[2,3,32,128,128]{4,3,2,1,0:T(8,128)(2,1)S(1)} %copy-done.2, bf16[128,256]{1,0:T(8,128)(2,1)S(1)} %transform.1.mix), custom_call_target="tpu_custom_call" | custom-call | flops 1 | bytes 1 | tf_op jit(solution)/shard_map/analysis/pallas_call | solution.py:370
  (85 shorter events, 15.7 us)
Async XLA Ops:
  0.0 26.4 %copy-start.7 = (s32[1,1,32]{2,1,0:T(1,128)S(1)}, s32[1,1,32]{2,1,0:T(1,128)}, u32[]{:S(2)}) copy-start(s32[1,1,32]{2,1,0:T(1,128)} %param.8) | copy-start | bytes 388
  0.8 17.4 %collective-permute-start = (f32[2,8,128]{2,1,0:T(8,128)S(1)}, f32[2,8,128]{2,1,0:T(8,128)S(1)}, u32[]{:S(2)}, u32[]{:S(2)}) collective-permute-start(f32[2,8,128]{2,1,0:T(8,128)S(1)} %get-tuple-element.54), channel_id=1, source_target_pairs={{0,8},{8,16},{16,24},{24,32},{32,40},{40,48},{48,56},{56,64},{64,7... | collective-permute-start | bytes 24584 | tf_op jit(solution)/shard_map/ppermute | solution.py:37
  2.4 15.8 %collective-permute-start.1 = (f32[2,8,128]{2,1,0:T(8,128)S(1)}, f32[2,8,128]{2,1,0:T(8,128)S(1)}, u32[]{:S(2)}, u32[]{:S(2)}) collective-permute-start(f32[2,8,128]{2,1,0:T(8,128)S(1)} %get-tuple-element.55), channel_id=1, source_target_pairs={{0,120},{8,0},{16,8},{24,16},{32,24},{40,32},{48,40},{56,48},{64,5... | collective-permute-start | bytes 24584 | tf_op jit(solution)/shard_map/ppermute | solution.py:37
  18.0 8.4 %collective-permute-start.4 = (bf16[2,3,16,16,128]{4,3,2,1,0:T(8,128)(2,1)S(1)}, bf16[2,3,16,16,128]{4,3,2,1,0:T(8,128)(2,1)S(1)}, u32[]{:S(2)}, u32[]{:S(2)}) collective-permute-start(bf16[2,3,16,16,128]{4,3,2,1,0:T(8,128)(2,1)S(1)} %get-tuple-element.30), channel_id=1, source_target_pairs={{0,1},{1,2},{2,3},{3,4},{4,5},{5,6},{6,7},{7,0},{8,9},{9,10},{10,1... | collective-permute-start | bytes 1179656 | tf_op jit(solution)/shard_map/ppermute | solution.py:37
  18.2 42.3 %collective-permute-start.2 = (bf16[44,128,128]{2,1,0:T(8,128)(2,1)}, bf16[44,128,128]{2,1,0:T(8,128)(2,1)S(1)}, u32[]{:S(2)}, u32[]{:S(2)}) collective-permute-start(bf16[44,128,128]{2,1,0:T(8,128)(2,1)} %get-tuple-element.27), channel_id=1, source_target_pairs={{0,8},{8,16},{16,24},{24,32},{32,40},{40,48},{48,56},{56,64},{64,7... | collective-permute-start | bytes 4325384 | tf_op jit(solution)/shard_map/ppermute | solution.py:37
  18.3 42.2 %collective-permute-start.3 = (bf16[44,128,128]{2,1,0:T(8,128)(2,1)}, bf16[44,128,128]{2,1,0:T(8,128)(2,1)}, u32[]{:S(2)}, u32[]{:S(2)}) collective-permute-start(bf16[44,128,128]{2,1,0:T(8,128)(2,1)} %get-tuple-element.28), channel_id=1, source_target_pairs={{0,120},{8,0},{16,8},{24,16},{32,24},{40,32},{48,40},{56,48},{64,5... | collective-permute-start | bytes 4325384 | tf_op jit(solution)/shard_map/ppermute | solution.py:37
  27.3 6.4 %collective-permute-start.10 = (f32[2,48,8]{2,1,0:T(8,128)}, f32[2,48,8]{2,1,0:T(8,128)S(1)}, u32[]{:S(2)}, u32[]{:S(2)}) collective-permute-start(f32[2,48,8]{2,1,0:T(8,128)} %get-tuple-element.47), channel_id=1, source_target_pairs={{0,1},{1,2},{2,3},{3,4},{4,5},{5,6},{6,7},{7,0},{8,9},{9,10},{10,1... | collective-permute-start | bytes 9224 | tf_op jit(solution)/shard_map/ppermute | solution.py:37
  27.3 6.7 %collective-permute-start.11 = (f32[2,48,8]{2,1,0:T(8,128)}, f32[2,48,8]{2,1,0:T(8,128)}, u32[]{:S(2)}, u32[]{:S(2)}) collective-permute-start(f32[2,48,8]{2,1,0:T(8,128)} %get-tuple-element.48), channel_id=1, source_target_pairs={{0,7},{1,0},{2,1},{3,2},{4,3},{5,4},{6,5},{7,6},{8,15},{9,8},{10,9... | collective-permute-start | bytes 9224 | tf_op jit(solution)/shard_map/ppermute | solution.py:37
  33.0 6.6 %collective-permute-start.8 = (f32[4,2,32,128]{3,2,1,0:T(8,128)S(1)}, f32[4,2,32,128]{3,2,1,0:T(8,128)S(1)}, u32[]{:S(2)}, u32[]{:S(2)}) collective-permute-start(f32[4,2,32,128]{3,2,1,0:T(8,128)S(1)} %slice.87), channel_id=1, source_target_pairs={{0,4},{1,5},{2,6},{3,7},{4,0},{5,1},{6,2},{7,3},{8,12},{9,13},{10,... | collective-permute-start | bytes 393224 | tf_op jit(solution)/shard_map/ppermute | solution.py:411
  33.7 13.9 %collective-permute-start.5 = (bf16[2,3,16,16,128]{4,3,2,1,0:T(8,128)(2,1)S(1)}, bf16[2,3,16,16,128]{4,3,2,1,0:T(8,128)(2,1)S(1)}, u32[]{:S(2)}, u32[]{:S(2)}) collective-permute-start(bf16[2,3,16,16,128]{4,3,2,1,0:T(8,128)(2,1)S(1)} %get-tuple-element.32), channel_id=1, source_target_pairs={{0,7},{1,0},{2,1},{3,2},{4,3},{5,4},{6,5},{7,6},{8,15},{9,8},{10,9... | collective-permute-start | bytes 1179656 | tf_op jit(solution)/shard_map/ppermute | solution.py:37
  39.5 4.3 %collective-permute-start.9 = (f32[2,2,32,128]{3,2,1,0:T(8,128)S(1)}, f32[2,2,32,128]{3,2,1,0:T(8,128)S(1)}, u32[]{:S(2)}, u32[]{:S(2)}) collective-permute-start(f32[2,2,32,128]{3,2,1,0:T(8,128)S(1)} %slice.89), channel_id=1, source_target_pairs={{0,2},{1,3},{2,0},{3,1},{4,6},{5,7},{6,4},{7,5},{8,10},{9,11},{10,... | collective-permute-start | bytes 196616 | tf_op jit(solution)/shard_map/ppermute | solution.py:411
  47.5 2.2 %collective-permute-start.12 = (f32[1,2,32,128]{3,2,1,0:T(8,128)S(1)}, f32[1,2,32,128]{3,2,1,0:T(8,128)S(1)}, u32[]{:S(2)}, u32[]{:S(2)}) collective-permute-start(f32[1,2,32,128]{3,2,1,0:T(8,128)S(1)} %slice.77), channel_id=1, source_target_pairs={{0,1},{1,0},{2,3},{3,2},{4,5},{5,4},{6,7},{7,6},{8,9},{9,8},{10,11... | collective-permute-start | bytes 98312 | tf_op jit(solution)/shard_map/ppermute | solution.py:411
  47.6 12.2 %collective-permute-start.7 = (bf16[2,2,3,4,16,128]{5,4,3,2,1,0:T(8,128)(2,1)S(1)}, bf16[2,2,3,4,16,128]{5,4,3,2,1,0:T(8,128)(2,1)S(1)}, u32[]{:S(2)}, u32[]{:S(2)}) collective-permute-start(bf16[2,2,3,4,16,128]{5,4,3,2,1,0:T(8,128)(2,1)S(1)} %get-tuple-element.45), channel_id=1, source_target_pairs={{0,120},{8,0},{16,8},{24,16},{32,24},{40,32},{48,40},{56,48},{64,5... | collective-permute-start | bytes 589832 | tf_op jit(solution)/shard_map/ppermute | solution.py:37
  49.7 10.8 %collective-permute-start.6 = (bf16[2,2,3,4,16,128]{5,4,3,2,1,0:T(8,128)(2,1)S(1)}, bf16[2,2,3,4,16,128]{5,4,3,2,1,0:T(8,128)(2,1)S(1)}, u32[]{:S(2)}, u32[]{:S(2)}) collective-permute-start(bf16[2,2,3,4,16,128]{5,4,3,2,1,0:T(8,128)(2,1)S(1)} %get-tuple-element.46), channel_id=1, source_target_pairs={{0,8},{8,16},{16,24},{24,32},{32,40},{40,48},{48,56},{56,64},{64,7... | collective-permute-start | bytes 589832 | tf_op jit(solution)/shard_map/ppermute | solution.py:37
  93.1 1.3 collective-permute-start.13
  94.4 5.6 %collective-permute-start.16 = (f32[136,128]{1,0:T(8,128)S(1)}, f32[136,128]{1,0:T(8,128)S(1)}, u32[]{:S(2)}, u32[]{:S(2)}) collective-permute-start(f32[136,128]{1,0:T(8,128)S(1)} %add.141), channel_id=1, source_target_pairs={{0,6},{1,7},{2,4},{3,5},{4,2},{5,3},{6,0},{7,1},{8,14},{9,15},{10,... | collective-permute-start | bytes 208904 | tf_op jit(solution)/shard_map/ppermute | solution.py:418
  96.9 6.2 %collective-permute-start.15 = (f32[136,128]{1,0:T(8,128)S(1)}, f32[136,128]{1,0:T(8,128)S(1)}, u32[]{:S(2)}, u32[]{:S(2)}) collective-permute-start(f32[136,128]{1,0:T(8,128)S(1)} %add.141), channel_id=1, source_target_pairs={{0,4},{1,5},{2,6},{3,7},{4,0},{5,1},{6,2},{7,3},{8,12},{9,13},{10,... | collective-permute-start | bytes 208904 | tf_op jit(solution)/shard_map/ppermute | solution.py:418
  97.5 5.6 %collective-permute-start.14 = (f32[136,128]{1,0:T(8,128)S(1)}, f32[136,128]{1,0:T(8,128)S(1)}, u32[]{:S(2)}, u32[]{:S(2)}) collective-permute-start(f32[136,128]{1,0:T(8,128)S(1)} %add.141), channel_id=1, source_target_pairs={{0,2},{1,3},{2,0},{3,1},{4,6},{5,7},{6,4},{7,5},{8,10},{9,11},{10,... | collective-permute-start | bytes 208904 | tf_op jit(solution)/shard_map/ppermute | solution.py:418
  103.1 5.6 %collective-permute-start.19 = (f32[136,128]{1,0:T(8,128)S(1)}, f32[136,128]{1,0:T(8,128)S(1)}, u32[]{:S(2)}, u32[]{:S(2)}) collective-permute-start(f32[136,128]{1,0:T(8,128)S(1)} %add_add_fusion.2), channel_id=1, source_target_pairs={{0,24},{8,16},{16,8},{24,0},{32,56},{40,48},{48,40},{56,32},{64,88... | collective-permute-start | bytes 208904 | tf_op jit(solution)/shard_map/ppermute | solution.py:418
  104.2 5.8 %collective-permute-start.18 = (f32[136,128]{1,0:T(8,128)S(1)}, f32[136,128]{1,0:T(8,128)S(1)}, u32[]{:S(2)}, u32[]{:S(2)}) collective-permute-start(f32[136,128]{1,0:T(8,128)S(1)} %add_add_fusion.2), channel_id=1, source_target_pairs={{0,16},{8,24},{16,0},{24,8},{32,48},{40,56},{48,32},{56,40},{64,80... | collective-permute-start | bytes 208904 | tf_op jit(solution)/shard_map/ppermute | solution.py:418
  104.2 6.1 %collective-permute-start.17 = (f32[136,128]{1,0:T(8,128)S(1)}, f32[136,128]{1,0:T(8,128)S(1)}, u32[]{:S(2)}, u32[]{:S(2)}) collective-permute-start(f32[136,128]{1,0:T(8,128)S(1)} %add_add_fusion.2), channel_id=1, source_target_pairs={{0,8},{8,0},{16,24},{24,16},{32,40},{40,32},{48,56},{56,48},{64,72... | collective-permute-start | bytes 208904 | tf_op jit(solution)/shard_map/ppermute | solution.py:418
  110.3 7.3 %collective-permute-start.22 = (f32[136,128]{1,0:T(8,128)S(1)}, f32[136,128]{1,0:T(8,128)S(1)}, u32[]{:S(2)}, u32[]{:S(2)}) collective-permute-start(f32[136,128]{1,0:T(8,128)S(1)} %add_add_fusion.1), channel_id=1, source_target_pairs={{0,96},{8,104},{16,112},{24,120},{32,64},{40,72},{48,80},{56,88},{... | collective-permute-start | bytes 208904 | tf_op jit(solution)/shard_map/ppermute | solution.py:418
  115.0 5.8 %collective-permute-start.21 = (f32[136,128]{1,0:T(8,128)S(1)}, f32[136,128]{1,0:T(8,128)S(1)}, u32[]{:S(2)}, u32[]{:S(2)}) collective-permute-start(f32[136,128]{1,0:T(8,128)S(1)} %add_add_fusion.1), channel_id=1, source_target_pairs={{0,64},{8,72},{16,80},{24,88},{32,96},{40,104},{48,112},{56,120},{... | collective-permute-start | bytes 208904 | tf_op jit(solution)/shard_map/ppermute | solution.py:418
  115.0 5.8 %collective-permute-start.20 = (f32[136,128]{1,0:T(8,128)S(1)}, f32[136,128]{1,0:T(8,128)S(1)}, u32[]{:S(2)}, u32[]{:S(2)}) collective-permute-start(f32[136,128]{1,0:T(8,128)S(1)} %add_add_fusion.1), channel_id=1, source_target_pairs={{0,32},{8,40},{16,48},{24,56},{32,0},{40,8},{48,16},{56,24},{64,96... | collective-permute-start | bytes 208904 | tf_op jit(solution)/shard_map/ppermute | solution.py:418
  (7 other events, 79.2 us)

commit v6 on v5

--- a/solution.py
+++ b/solution.py
@@ -109,18 +109,16 @@
         out_specs=[spec(tile), spec(side), spec(side), edge_spec, edge_spec],
         out_shape=[whole(tile), whole(side), whole(side), edge_shape, edge_shape],
         scratch_shapes=[pltpu.VMEM((MEMBERS * (ROWS + 1), COLS), F32)],
-        compiler_params=params(18),
+        compiler_params=params(60),
         cost_estimate=COST,
         name="all_rows",
     )(ensemble)
 
 
 def forecast_kernel(
-    own, top, bottom, left, right, corner_t, corner_b, depth_in, row_in, masks, weight, pull,
-    out, total, raw, raw_side, depth, st, fx, fy, pr, line, y_parts, z_parts, acc, sems,
+    own, top, bottom, left, right, corner_t, corner_b, depth, row_in, masks, weight, pull,
+    out, total, raw, raw_side, st, fx, fy, pr, line, y_parts, z_parts, acc, sems,
 ):
-    depth_copy = pltpu.make_async_copy(depth_in, depth, sems.at[54])
-    depth_copy.start()
     order = [(l, c) for l in range(LAYERS) for c in range(3)]
     copies = {}
     for l, c in order:
@@ -142,7 +140,6 @@
     for key in order:
         for c in copies[key]:
             c.start()
-    depth_copy.wait()
 
     def rolled(x, by):
         return pltpu.roll(x.astype(F32), by % SEGMENTS, 0).astype(BF16)
@@ -261,7 +258,7 @@
             lax.fori_loop(0, ROWS, pack, 0, unroll=4)
             done.append(
                 pltpu.make_async_copy(
-                    raw.at[l, c, pl.ds(0, ROWS)], out.at[l, c], sems.at[55 + 3 * l + c]
+                    raw.at[l, c, pl.ds(0, ROWS)], out.at[l, c], sems.at[54 + 3 * l + c]
                 )
             )
             done[-1].start()
@@ -316,7 +313,7 @@
     vmem = pl.BlockSpec(memory_space=pltpu.VMEM)
     return pl.pallas_call(
         forecast_kernel,
-        in_specs=[anywhere] * 8 + [pl.BlockSpec(memory_space=pltpu.SMEM), vmem, vmem, vmem],
+        in_specs=[anywhere] * 7 + [vmem, pl.BlockSpec(memory_space=pltpu.SMEM), vmem, vmem, vmem],
         out_specs=[anywhere, vmem],
         out_shape=[
             jax.ShapeDtypeStruct((LAYERS, 3, ROWS, COLS, MEMBERS), BF16),
@@ -325,7 +322,6 @@
         scratch_shapes=[
             pltpu.VMEM((LAYERS, 3, WIDE_ROWS, COLS, MEMBERS), BF16),
             pltpu.VMEM((2, LAYERS, 3, WIDE_ROWS // 2, 16, MEMBERS), BF16),
-            pltpu.VMEM(plane, BF16),
             pltpu.VMEM((LAYERS, 3) + plane[1:], BF16),
             pltpu.VMEM(plane, BF16),
             pltpu.VMEM(padded, BF16),
@@ -334,9 +330,9 @@
             pltpu.VMEM((2, ROWS, MEMBERS, COLS), BF16),
             pltpu.VMEM((ROWS, COLS, 2 * MEMBERS), BF16),
             pltpu.VMEM((MEMBERS, COLS), F32),
-            pltpu.SemaphoreType.DMA((61,)),
+            pltpu.SemaphoreType.DMA((60,)),
         ],
-        compiler_params=params(47),
+        compiler_params=params(44),
         cost_estimate=COST,
         name="forecast",
     )(*operands)

time: 135 us -> 134 us (level)
  local copies, waits for them, and re-layouts: 14.3 us -> 6.8 us
  Pallas kernels: 49.2 us -> 53.4 us
  waiting for transfers between devices: 35.5 us -> 37.8 us
    unnamed x16 -> x14, local copies, waits for them, and re-layouts: 8.28 us -> 2.8 us
    pallas_call x1, Pallas kernels: 5.18 us -> 9.37 us  [all_rows(): pl.pallas_call(kernel, grid=(LAYERS, 3), in_specs=[E_BLOCK], out_specs=[s...]
    broadcast_in_dim x1, local copies, waits for them, and re-layouts: 3.52 us -> 2.14 us  [on_device(): depth = jnp.broadcast_to(d[..., None], d.shape + (MEMBERS,))]
  transfers between devices with their start and end apart: 23 -> 23, of which waited for: 13 -> 13; matrix products, arithmetic and copies ran while one was open for 7% -> 4% of each run, Pallas kernels for 4% -> 7%
where the time goes in v6:
time: 134 us
  Pallas kernels  53.4 us (40%)
  waiting for transfers between devices  37.8 us (28%)
  starting transfers between devices  32.6 us (24%)
  local copies, waits for them, and re-layouts  6.8 us (5%)
  matrix products  1.92 us (1%)
    pallas_call x1, Pallas kernels, forecast(): pl.pallas_call(forecast_kernel, in_specs=[anywhere] * 7 + [vmem, pl.Block...  32.6 us
    ppermute x10, starting transfers between devices, shift(): return lax.ppermute(x, axis, [(i, (i + by) % n) for i in range(n)])  17.4 us
    ppermute x10, waiting for transfers between devices, shift(): return lax.ppermute(x, axis, [(i, (i + by) % n) for i in range(n)])  14.9 us
    ppermute x10, starting transfers between devices, other(): lax.ppermute(x, axis, [(i, i ^ k) for i in range(lax.axis_size(axis))])  14.4 us
    ppermute x10, waiting for transfers between devices, other(): lax.ppermute(x, axis, [(i, i ^ k) for i in range(lax.axis_size(axis))])  13.8 us
    pallas_call x1, Pallas kernels, all_rows(): pl.pallas_call(kernel, grid=(LAYERS, 3), in_specs=[E_BLOCK], out_specs=[s...  9.37 us
    ppermute x3, waiting for transfers between devices, observed_cells(): field = field[:bit] + lax.ppermute(field[bit:], 'gy', swap)  9.04 us
    pallas_call x1, Pallas kernels, analyse(): pl.pallas_call(analysis_kernel, grid=(LAYERS, 3), in_specs=[pl.BlockSpec(...  6.6 us
  transfers between devices with their start and end apart: 23, of which 13 were waited for; matrix products, arithmetic and copies ran while one was open for 4% of the time, Pallas kernels for 7%

profile of v6, /device:TPU:0, one launch (start us, length us, event | category | flops | bytes accessed | tf_op | source)
XLA Modules:
  0.0 133.9 jit_solution(8523301994100684055)
XLA Ops:
  0.8 1.7 %collective-permute-start = (f32[2,8,128]{2,1,0:T(8,128)S(1)}, f32[2,8,128]{2,1,0:T(8,128)S(1)}, u32[]{:S(2)}, u32[]{:S(2)}) collective-permute-start(f32[2,8,128]{2,1,0:T(8,128)S(1)} %get-tuple-element.54), channel_id=1, source_target_pairs={{0,8},{8,16},{16,24},{24,32},{32,40},{40,48},{48,56},{56,64},{64,7... | collective-permute-start | bytes 24584 | tf_op jit(solution)/shard_map/ppermute | solution.py:37
  2.5 4.9 %collective-permute-start.1 = (f32[2,8,128]{2,1,0:T(8,128)S(1)}, f32[2,8,128]{2,1,0:T(8,128)S(1)}, u32[]{:S(2)}, u32[]{:S(2)}) collective-permute-start(f32[2,8,128]{2,1,0:T(8,128)S(1)} %get-tuple-element.55), channel_id=1, source_target_pairs={{0,120},{8,0},{16,8},{24,16},{32,24},{40,32},{48,40},{56,48},{64,5... | collective-permute-start | bytes 24584 | tf_op jit(solution)/shard_map/ppermute | solution.py:37
  7.4 9.4 %all_rows.1 = (bf16[2,3,32,128,128]{4,3,2,1,0:T(8,128)(2,1)}, bf16[2,3,16,16,128]{4,3,2,1,0:T(8,128)(2,1)}, bf16[2,3,16,16,128]{4,3,2,1,0:T(8,128)(2,1)}, bf16[4...) custom-call(bf16[2,3,128,32,128]{4,3,2,1,0:T(8,128)(2,1)} %e_ref.1), custom_call_target="tpu_custom_call" | custom-call | flops 1 | bytes 1 | tf_op jit(solution)/shard_map/all_rows/pallas_call | solution.py:105
  17.1 5.3 %collective-permute-start.3 = (bf16[44,128,128]{2,1,0:T(8,128)(2,1)}, bf16[44,128,128]{2,1,0:T(8,128)(2,1)}, u32[]{:S(2)}, u32[]{:S(2)}) collective-permute-start(bf16[44,128,128]{2,1,0:T(8,128)(2,1)} %get-tuple-element.28), channel_id=1, source_target_pairs={{0,120},{8,0},{16,8},{24,16},{32,24},{40,32},{48,40},{56,48},{64,5... | collective-permute-start | bytes 4325384 | tf_op jit(solution)/shard_map/ppermute | solution.py:37
  22.4 3.0 %collective-permute-done.4.left = bf16[2,3,16,16,128]{4,3,2,1,0:T(8,128)(2,1)S(1)} collective-permute-done((bf16[2,3,16,16,128]{4,3,2,1,0:T(8,128)(2,1)}, bf16[2,3,16,16,128]{4,3,2,1,0:T(8,128)(2,1)S(1)}, u32[]{:S(2)}, u32[]{:S(2)}) %collective-permute-start.4) | collective-permute-done | bytes 393248 | tf_op jit(solution)/shard_map/ppermute | solution.py:37
  25.6 3.0 %collective-permute-start.11 = (f32[2,48,8]{2,1,0:T(8,128)S(1)}, f32[2,48,8]{2,1,0:T(8,128)S(1)}, u32[]{:S(2)}, u32[]{:S(2)}) collective-permute-start(f32[2,48,8]{2,1,0:T(8,128)S(1)} %get-tuple-element.48), channel_id=1, source_target_pairs={{0,7},{1,0},{2,1},{3,2},{4,3},{5,4},{6,5},{7,6},{8,15},{9,8},{10,9... | collective-permute-start | bytes 9224 | tf_op jit(solution)/shard_map/ppermute | solution.py:37
  29.1 1.9 %fusion.8 = f32[6,256,128]{1,2,0:T(8,128)S(1)} fusion(s32[4096]{0:T(1024)S(1)} %get-tuple-element.60, pred[4096,128]{0,1:T(8,128)(4,1)S(1)} %iota_compare_fusion.1, bf16[6,4096]{1,0:T(8,128)(2,1)S(1)} %bitcast.34), kind=kOutput, calls=%fused_computation.9 | convolution fusion | flops 1614807040 | bytes 1376256 | tf_op jit(solution)/shard_map/rk,pkc->prc/dot_general | solution.py:399
  32.6 5.3 %collective-permute-done.8 = f32[4,2,32,128]{3,2,1,0:T(8,128)S(1)} collective-permute-done((f32[4,2,32,128]{3,2,1,0:T(8,128)S(1)}, f32[4,2,32,128]{3,2,1,0:T(8,128)S(1)}, u32[]{:S(2)}, u32[]{:S(2)}) %collective-permute-start.8) | collective-permute-done | bytes 131104 | tf_op jit(solution)/shard_map/ppermute | solution.py:407
  38.5 3.8 %collective-permute-done.9 = f32[2,2,32,128]{3,2,1,0:T(8,128)S(1)} collective-permute-done((f32[2,2,32,128]{3,2,1,0:T(8,128)S(1)}, f32[2,2,32,128]{3,2,1,0:T(8,128)S(1)}, u32[]{:S(2)}, u32[]{:S(2)}) %collective-permute-start.9) | collective-permute-done | bytes 65568 | tf_op jit(solution)/shard_map/ppermute | solution.py:407
  42.4 2.1 %broadcast_in_dim.55.depth = bf16[2,48,9,16,128]{4,3,2,1,0:T(8,128)(2,1)S(1)} broadcast(bf16[2,48,9,16]{3,2,1,0:T(8,128)(2,1)S(1)} %copy.13), dimensions={0,1,2,3} | broadcast | bytes 3566592 | tf_op jit(solution)/shard_map/broadcast_in_dim | solution.py:506
  44.7 2.1 %collective-permute-start.7 = (bf16[2,2,3,4,16,128]{5,4,3,2,1,0:T(8,128)(2,1)S(1)}, bf16[2,2,3,4,16,128]{5,4,3,2,1,0:T(8,128)(2,1)S(1)}, u32[]{:S(2)}, u32[]{:S(2)}) collective-permute-start(bf16[2,2,3,4,16,128]{5,4,3,2,1,0:T(8,128)(2,1)S(1)} %get-tuple-element.45), channel_id=1, source_target_pairs={{0,120},{8,0},{16,8},{24,16},{32,24},{40,32},{48,40},{56,48},{64,5... | collective-permute-start | bytes 589832 | tf_op jit(solution)/shard_map/ppermute | solution.py:37
  46.8 11.7 %collective-permute-done.7.corner_b = bf16[2,2,3,4,16,128]{5,4,3,2,1,0:T(8,128)(2,1)S(1)} collective-permute-done((bf16[2,2,3,4,16,128]{5,4,3,2,1,0:T(8,128)(2,1)S(1)}, bf16[2,2,3,4,16,128]{5,4,3,2,1,0:T(8,128)(2,1)S(1)}, u32[]{:S(2)}, u32[]{:S(2)}) %collective-permute-start.7) | collective-permute-done | bytes 196640 | tf_op jit(solution)/shard_map/ppermute | solution.py:37
  58.7 32.6 %forecast.1 = (bf16[2,3,32,128,128]{4,3,2,1,0:T(8,128)(2,1)}, f32[136,128]{1,0:T(8,128)S(1)}) custom-call(bf16[2,3,32,128,128]{4,3,2,1,0:T(8,128)(2,1)} %get-tuple-element.24.own, bf16[44,128,128]{2,1,0:T(8,128)(2,1)S(1)} %collective-permute-done.2.top, bf16[44,128,128]{2,1,0:T(8,128)(2,1)} %collective-permute-done.3.bottom, ...), custom_call_target="tpu_custom_call" | custom-call | flops 1 | bytes 1 | tf_op jit(solution)/shard_map/forecast/pallas_call | solution.py:314
  92.7 3.0 %collective-permute-start.16 = (f32[136,128]{1,0:T(8,128)S(1)}, f32[136,128]{1,0:T(8,128)S(1)}, u32[]{:S(2)}, u32[]{:S(2)}) collective-permute-start(f32[136,128]{1,0:T(8,128)S(1)} %add.141), channel_id=1, source_target_pairs={{0,6},{1,7},{2,4},{3,5},{4,2},{5,3},{6,0},{7,1},{8,14},{9,15},{10,... | collective-permute-start | bytes 208904 | tf_op jit(solution)/shard_map/ppermute | solution.py:414
  96.9 2.1 %collective-permute-done.16 = f32[136,128]{1,0:T(8,128)S(1)} collective-permute-done((f32[136,128]{1,0:T(8,128)S(1)}, f32[136,128]{1,0:T(8,128)S(1)}, u32[]{:S(2)}, u32[]{:S(2)}) %collective-permute-start.16) | collective-permute-done | bytes 69664 | tf_op jit(solution)/shard_map/ppermute | solution.py:414
  98.9 2.9 %collective-permute-done.15 = f32[136,128]{1,0:T(8,128)S(1)} collective-permute-done((f32[136,128]{1,0:T(8,128)S(1)}, f32[136,128]{1,0:T(8,128)S(1)}, u32[]{:S(2)}, u32[]{:S(2)}) %collective-permute-start.15) | collective-permute-done | bytes 69664 | tf_op jit(solution)/shard_map/ppermute | solution.py:414
  103.0 3.1 %collective-permute-start.17 = (f32[136,128]{1,0:T(8,128)S(1)}, f32[136,128]{1,0:T(8,128)S(1)}, u32[]{:S(2)}, u32[]{:S(2)}) collective-permute-start(f32[136,128]{1,0:T(8,128)S(1)} %add_add_fusion.2), channel_id=1, source_target_pairs={{0,8},{8,0},{16,24},{24,16},{32,40},{40,32},{48,56},{56,48},{64,72... | collective-permute-start | bytes 208904 | tf_op jit(solution)/shard_map/ppermute | solution.py:414
  106.1 1.4 %collective-permute-done.19 = f32[136,128]{1,0:T(8,128)S(1)} collective-permute-done((f32[136,128]{1,0:T(8,128)S(1)}, f32[136,128]{1,0:T(8,128)S(1)}, u32[]{:S(2)}, u32[]{:S(2)}) %collective-permute-start.19) | collective-permute-done | bytes 69664 | tf_op jit(solution)/shard_map/ppermute | solution.py:414
  109.1 4.6 %collective-permute-start.22 = (f32[136,128]{1,0:T(8,128)S(1)}, f32[136,128]{1,0:T(8,128)S(1)}, u32[]{:S(2)}, u32[]{:S(2)}) collective-permute-start(f32[136,128]{1,0:T(8,128)S(1)} %add_add_fusion.1), channel_id=1, source_target_pairs={{0,96},{8,104},{16,112},{24,120},{32,64},{40,72},{48,80},{56,88},{... | collective-permute-start | bytes 208904 | tf_op jit(solution)/shard_map/ppermute | solution.py:414
  114.7 1.7 %collective-permute-done.22 = f32[136,128]{1,0:T(8,128)S(1)} collective-permute-done((f32[136,128]{1,0:T(8,128)S(1)}, f32[136,128]{1,0:T(8,128)S(1)}, u32[]{:S(2)}, u32[]{:S(2)}) %collective-permute-start.22) | collective-permute-done | bytes 69664 | tf_op jit(solution)/shard_map/ppermute | solution.py:414
  116.4 3.2 %collective-permute-done.21 = f32[136,128]{1,0:T(8,128)S(1)} collective-permute-done((f32[136,128]{1,0:T(8,128)S(1)}, f32[136,128]{1,0:T(8,128)S(1)}, u32[]{:S(2)}, u32[]{:S(2)}) %collective-permute-start.21) | collective-permute-done | bytes 69664 | tf_op jit(solution)/shard_map/ppermute | solution.py:414
  119.6 4.9 %transform.1.mix = bf16[128,256]{1,0:T(8,128)(2,1)S(1)} custom-call(f32[136,128]{1,0:T(8,128)S(1)} %add_add_fusion.total), custom_call_target="tpu_custom_call" | custom-call | flops 1 | bytes 1 | tf_op jit(solution)/shard_map/transform/pallas_call | solution.py:469
  124.5 2.8 %copy-done = bf16[2,3,32,128,128]{4,3,2,1,0:T(8,128)(2,1)S(1)} copy-done((bf16[2,3,32,128,128]{4,3,2,1,0:T(8,128)(2,1)S(1)}, bf16[2,3,32,128,128]{4,3,2,1,0:T(8,128)(2,1)}, u32[]{:S(2)}) %copy-start) | copy-done | bytes 6291480
  127.3 6.6 %analysis.1 = bf16[2,3,128,32,128]{4,3,2,1,0:T(8,128)(2,1)} custom-call(bf16[2,3,32,128,128]{4,3,2,1,0:T(8,128)(2,1)S(1)} %copy-done, bf16[128,256]{1,0:T(8,128)(2,1)S(1)} %transform.1.mix), custom_call_target="tpu_custom_call" | custom-call | flops 1 | bytes 1 | tf_op jit(solution)/shard_map/analysis/pallas_call | solution.py:366
  (83 shorter events, 10.6 us)
Async XLA Ops:
  0.0 28.5 %copy-start.4 = (s32[1,1,32,128]{3,2,1,0:T(8,128)S(1)}, s32[1,1,32,128]{3,2,1,0:T(8,128)}, u32[]{:S(2)}) copy-start(s32[1,1,32,128]{3,2,1,0:T(8,128)} %param.9) | copy-start | bytes 49156
  0.8 16.1 %collective-permute-start = (f32[2,8,128]{2,1,0:T(8,128)S(1)}, f32[2,8,128]{2,1,0:T(8,128)S(1)}, u32[]{:S(2)}, u32[]{:S(2)}) collective-permute-start(f32[2,8,128]{2,1,0:T(8,128)S(1)} %get-tuple-element.54), channel_id=1, source_target_pairs={{0,8},{8,16},{16,24},{24,32},{32,40},{40,48},{48,56},{56,64},{64,7... | collective-permute-start | bytes 24584 | tf_op jit(solution)/shard_map/ppermute | solution.py:37
  2.5 14.5 %collective-permute-start.1 = (f32[2,8,128]{2,1,0:T(8,128)S(1)}, f32[2,8,128]{2,1,0:T(8,128)S(1)}, u32[]{:S(2)}, u32[]{:S(2)}) collective-permute-start(f32[2,8,128]{2,1,0:T(8,128)S(1)} %get-tuple-element.55), channel_id=1, source_target_pairs={{0,120},{8,0},{16,8},{24,16},{32,24},{40,32},{48,40},{56,48},{64,5... | collective-permute-start | bytes 24584 | tf_op jit(solution)/shard_map/ppermute | solution.py:37
  16.7 8.6 %collective-permute-start.4 = (bf16[2,3,16,16,128]{4,3,2,1,0:T(8,128)(2,1)}, bf16[2,3,16,16,128]{4,3,2,1,0:T(8,128)(2,1)S(1)}, u32[]{:S(2)}, u32[]{:S(2)}) collective-permute-start(bf16[2,3,16,16,128]{4,3,2,1,0:T(8,128)(2,1)} %get-tuple-element.30), channel_id=1, source_target_pairs={{0,1},{1,2},{2,3},{3,4},{4,5},{5,6},{6,7},{7,0},{8,9},{9,10},{10,1... | collective-permute-start | bytes 1179656 | tf_op jit(solution)/shard_map/ppermute | solution.py:37
  17.0 41.7 %collective-permute-start.2 = (bf16[44,128,128]{2,1,0:T(8,128)(2,1)}, bf16[44,128,128]{2,1,0:T(8,128)(2,1)S(1)}, u32[]{:S(2)}, u32[]{:S(2)}) collective-permute-start(bf16[44,128,128]{2,1,0:T(8,128)(2,1)} %get-tuple-element.27), channel_id=1, source_target_pairs={{0,8},{8,16},{16,24},{24,32},{32,40},{40,48},{48,56},{56,64},{64,7... | collective-permute-start | bytes 4325384 | tf_op jit(solution)/shard_map/ppermute | solution.py:37
  17.1 41.6 %collective-permute-start.3 = (bf16[44,128,128]{2,1,0:T(8,128)(2,1)}, bf16[44,128,128]{2,1,0:T(8,128)(2,1)}, u32[]{:S(2)}, u32[]{:S(2)}) collective-permute-start(bf16[44,128,128]{2,1,0:T(8,128)(2,1)} %get-tuple-element.28), channel_id=1, source_target_pairs={{0,120},{8,0},{16,8},{24,16},{32,24},{40,32},{48,40},{56,48},{64,5... | collective-permute-start | bytes 4325384 | tf_op jit(solution)/shard_map/ppermute | solution.py:37
  25.6 6.4 %collective-permute-start.10 = (f32[2,48,8]{2,1,0:T(8,128)S(1)}, f32[2,48,8]{2,1,0:T(8,128)S(1)}, u32[]{:S(2)}, u32[]{:S(2)}) collective-permute-start(f32[2,48,8]{2,1,0:T(8,128)S(1)} %get-tuple-element.47), channel_id=1, source_target_pairs={{0,1},{1,2},{2,3},{3,4},{4,5},{5,6},{6,7},{7,0},{8,9},{9,10},{10,1... | collective-permute-start | bytes 9224 | tf_op jit(solution)/shard_map/ppermute | solution.py:37
  25.6 6.8 %collective-permute-start.11 = (f32[2,48,8]{2,1,0:T(8,128)S(1)}, f32[2,48,8]{2,1,0:T(8,128)S(1)}, u32[]{:S(2)}, u32[]{:S(2)}) collective-permute-start(f32[2,48,8]{2,1,0:T(8,128)S(1)} %get-tuple-element.48), channel_id=1, source_target_pairs={{0,7},{1,0},{2,1},{3,2},{4,3},{5,4},{6,5},{7,6},{8,15},{9,8},{10,9... | collective-permute-start | bytes 9224 | tf_op jit(solution)/shard_map/ppermute | solution.py:37
  31.3 6.6 %collective-permute-start.8 = (f32[4,2,32,128]{3,2,1,0:T(8,128)S(1)}, f32[4,2,32,128]{3,2,1,0:T(8,128)S(1)}, u32[]{:S(2)}, u32[]{:S(2)}) collective-permute-start(f32[4,2,32,128]{3,2,1,0:T(8,128)S(1)} %slice.87), channel_id=1, source_target_pairs={{0,4},{1,5},{2,6},{3,7},{4,0},{5,1},{6,2},{7,3},{8,12},{9,13},{10,... | collective-permute-start | bytes 393224 | tf_op jit(solution)/shard_map/ppermute | solution.py:407
  32.0 12.6 %collective-permute-start.5 = (bf16[2,3,16,16,128]{4,3,2,1,0:T(8,128)(2,1)S(1)}, bf16[2,3,16,16,128]{4,3,2,1,0:T(8,128)(2,1)S(1)}, u32[]{:S(2)}, u32[]{:S(2)}) collective-permute-start(bf16[2,3,16,16,128]{4,3,2,1,0:T(8,128)(2,1)S(1)} %copy-done.5), channel_id=1, source_target_pairs={{0,7},{1,0},{2,1},{3,2},{4,3},{5,4},{6,5},{7,6},{8,15},{9,8},{10,9... | collective-permute-start | bytes 1179656 | tf_op jit(solution)/shard_map/ppermute | solution.py:37
  37.9 4.3 %collective-permute-start.9 = (f32[2,2,32,128]{3,2,1,0:T(8,128)S(1)}, f32[2,2,32,128]{3,2,1,0:T(8,128)S(1)}, u32[]{:S(2)}, u32[]{:S(2)}) collective-permute-start(f32[2,2,32,128]{3,2,1,0:T(8,128)S(1)} %slice.89), channel_id=1, source_target_pairs={{0,2},{1,3},{2,0},{3,1},{4,6},{5,7},{6,4},{7,5},{8,10},{9,11},{10,... | collective-permute-start | bytes 196616 | tf_op jit(solution)/shard_map/ppermute | solution.py:407
  44.5 2.2 %collective-permute-start.12 = (f32[1,2,32,128]{3,2,1,0:T(8,128)S(1)}, f32[1,2,32,128]{3,2,1,0:T(8,128)S(1)}, u32[]{:S(2)}, u32[]{:S(2)}) collective-permute-start(f32[1,2,32,128]{3,2,1,0:T(8,128)S(1)} %slice.77), channel_id=1, source_target_pairs={{0,1},{1,0},{2,3},{3,2},{4,5},{5,4},{6,7},{7,6},{8,9},{9,8},{10,11... | collective-permute-start | bytes 98312 | tf_op jit(solution)/shard_map/ppermute | solution.py:407
  44.7 13.8 %collective-permute-start.7 = (bf16[2,2,3,4,16,128]{5,4,3,2,1,0:T(8,128)(2,1)S(1)}, bf16[2,2,3,4,16,128]{5,4,3,2,1,0:T(8,128)(2,1)S(1)}, u32[]{:S(2)}, u32[]{:S(2)}) collective-permute-start(bf16[2,2,3,4,16,128]{5,4,3,2,1,0:T(8,128)(2,1)S(1)} %get-tuple-element.45), channel_id=1, source_target_pairs={{0,120},{8,0},{16,8},{24,16},{32,24},{40,32},{48,40},{56,48},{64,5... | collective-permute-start | bytes 589832 | tf_op jit(solution)/shard_map/ppermute | solution.py:37
  46.7 12.0 %collective-permute-start.6 = (bf16[2,2,3,4,16,128]{5,4,3,2,1,0:T(8,128)(2,1)S(1)}, bf16[2,2,3,4,16,128]{5,4,3,2,1,0:T(8,128)(2,1)S(1)}, u32[]{:S(2)}, u32[]{:S(2)}) collective-permute-start(bf16[2,2,3,4,16,128]{5,4,3,2,1,0:T(8,128)(2,1)S(1)} %get-tuple-element.46), channel_id=1, source_target_pairs={{0,8},{8,16},{16,24},{24,32},{32,40},{40,48},{48,56},{56,64},{64,7... | collective-permute-start | bytes 589832 | tf_op jit(solution)/shard_map/ppermute | solution.py:37
  91.3 1.4 %collective-permute-start.13 = (f32[136,128]{1,0:T(8,128)S(1)}, f32[136,128]{1,0:T(8,128)S(1)}, u32[]{:S(2)}, u32[]{:S(2)}) collective-permute-start(f32[136,128]{1,0:T(8,128)S(1)} %get-tuple-element.42), channel_id=1, source_target_pairs={{0,1},{1,0},{2,3},{3,2},{4,5},{5,4},{6,7},{7,6},{8,9},{9,8},{10,11... | collective-permute-start | bytes 208904 | tf_op jit(solution)/shard_map/ppermute | solution.py:414
  92.7 6.2 %collective-permute-start.16 = (f32[136,128]{1,0:T(8,128)S(1)}, f32[136,128]{1,0:T(8,128)S(1)}, u32[]{:S(2)}, u32[]{:S(2)}) collective-permute-start(f32[136,128]{1,0:T(8,128)S(1)} %add.141), channel_id=1, source_target_pairs={{0,6},{1,7},{2,4},{3,5},{4,2},{5,3},{6,0},{7,1},{8,14},{9,15},{10,... | collective-permute-start | bytes 208904 | tf_op jit(solution)/shard_map/ppermute | solution.py:414
  95.7 6.2 %collective-permute-start.15 = (f32[136,128]{1,0:T(8,128)S(1)}, f32[136,128]{1,0:T(8,128)S(1)}, u32[]{:S(2)}, u32[]{:S(2)}) collective-permute-start(f32[136,128]{1,0:T(8,128)S(1)} %add.141), channel_id=1, source_target_pairs={{0,4},{1,5},{2,6},{3,7},{4,0},{5,1},{6,2},{7,3},{8,12},{9,13},{10,... | collective-permute-start | bytes 208904 | tf_op jit(solution)/shard_map/ppermute | solution.py:414
  96.3 5.5 %collective-permute-start.14 = (f32[136,128]{1,0:T(8,128)S(1)}, f32[136,128]{1,0:T(8,128)S(1)}, u32[]{:S(2)}, u32[]{:S(2)}) collective-permute-start(f32[136,128]{1,0:T(8,128)S(1)} %add.141), channel_id=1, source_target_pairs={{0,2},{1,3},{2,0},{3,1},{4,6},{5,7},{6,4},{7,5},{8,10},{9,11},{10,... | collective-permute-start | bytes 208904 | tf_op jit(solution)/shard_map/ppermute | solution.py:414
  101.9 5.6 %collective-permute-start.19 = (f32[136,128]{1,0:T(8,128)S(1)}, f32[136,128]{1,0:T(8,128)S(1)}, u32[]{:S(2)}, u32[]{:S(2)}) collective-permute-start(f32[136,128]{1,0:T(8,128)S(1)} %add_add_fusion.2), channel_id=1, source_target_pairs={{0,24},{8,16},{16,8},{24,0},{32,56},{40,48},{48,40},{56,32},{64,88... | collective-permute-start | bytes 208904 | tf_op jit(solution)/shard_map/ppermute | solution.py:414
  103.0 5.8 %collective-permute-start.18 = (f32[136,128]{1,0:T(8,128)S(1)}, f32[136,128]{1,0:T(8,128)S(1)}, u32[]{:S(2)}, u32[]{:S(2)}) collective-permute-start(f32[136,128]{1,0:T(8,128)S(1)} %add_add_fusion.2), channel_id=1, source_target_pairs={{0,16},{8,24},{16,0},{24,8},{32,48},{40,56},{48,32},{56,40},{64,80... | collective-permute-start | bytes 208904 | tf_op jit(solution)/shard_map/ppermute | solution.py:414
  103.0 6.1 %collective-permute-start.17 = (f32[136,128]{1,0:T(8,128)S(1)}, f32[136,128]{1,0:T(8,128)S(1)}, u32[]{:S(2)}, u32[]{:S(2)}) collective-permute-start(f32[136,128]{1,0:T(8,128)S(1)} %add_add_fusion.2), channel_id=1, source_target_pairs={{0,8},{8,0},{16,24},{24,16},{32,40},{40,32},{48,56},{56,48},{64,72... | collective-permute-start | bytes 208904 | tf_op jit(solution)/shard_map/ppermute | solution.py:414
  109.1 7.2 %collective-permute-start.22 = (f32[136,128]{1,0:T(8,128)S(1)}, f32[136,128]{1,0:T(8,128)S(1)}, u32[]{:S(2)}, u32[]{:S(2)}) collective-permute-start(f32[136,128]{1,0:T(8,128)S(1)} %add_add_fusion.1), channel_id=1, source_target_pairs={{0,96},{8,104},{16,112},{24,120},{32,64},{40,72},{48,80},{56,88},{... | collective-permute-start | bytes 208904 | tf_op jit(solution)/shard_map/ppermute | solution.py:414
  113.8 5.8 %collective-permute-start.21 = (f32[136,128]{1,0:T(8,128)S(1)}, f32[136,128]{1,0:T(8,128)S(1)}, u32[]{:S(2)}, u32[]{:S(2)}) collective-permute-start(f32[136,128]{1,0:T(8,128)S(1)} %add_add_fusion.1), channel_id=1, source_target_pairs={{0,64},{8,72},{16,80},{24,88},{32,96},{40,104},{48,112},{56,120},{... | collective-permute-start | bytes 208904 | tf_op jit(solution)/shard_map/ppermute | solution.py:414
  113.8 5.8 %collective-permute-start.20 = (f32[136,128]{1,0:T(8,128)S(1)}, f32[136,128]{1,0:T(8,128)S(1)}, u32[]{:S(2)}, u32[]{:S(2)}) collective-permute-start(f32[136,128]{1,0:T(8,128)S(1)} %add_add_fusion.1), channel_id=1, source_target_pairs={{0,32},{8,40},{16,48},{24,56},{32,0},{40,8},{48,16},{56,24},{64,96... | collective-permute-start | bytes 208904 | tf_op jit(solution)/shard_map/ppermute | solution.py:414
  (6 other events, 98.8 us)
